TPU v7x, 32 devices: a whole 2x2x4 slice. The times are simulated.
32 devices in a mesh: pre: 2 (over x), grp: 4 (over y, core), dec: 4 (over z).
Axes of the slice: x: 2, y: 2, z: 4, core: 2. Of those that a mesh axis runs over, the one named last changes fastest.
Arguments:
- prompt_queries: bfloat16 [16, 1024, 8192], P(('grp', 'dec'), None, 'pre'), may hold values from -6 to 6
- prompt_keys: bfloat16 [16, 1024, 8192], P(('grp', 'dec'), None, 'pre'), may hold values from -6 to 6
- prompt_values: bfloat16 [16, 1024, 8192], P(('grp', 'dec'), None, 'pre'), may hold values from -6 to 6
- prompt_decay: float32 [16, 64, 1024], P(('grp', 'dec'), 'pre'), may hold values from -1 to 0
- prompt_lengths: int32 [16], P(('grp', 'dec')), may hold values from 256 to 1024
- norm_gain: float32 [8192], P('pre'), may hold values from 0.1 to 1.9
- decode_owner: int32 [16], replicated, may hold values from 0 to 3, as said below
- parent_beam: int32 [16, 16], P('grp'), may hold values from 0 to 15, as said below
- step_queries: bfloat16 [2, 16, 16, 8192], P(None, 'grp', 'dec', 'pre'), may hold values from -6 to 6
- step_keys: bfloat16 [2, 16, 16, 8192], P(None, 'grp', 'dec', 'pre'), may hold values from -12 to 12
- step_values: bfloat16 [2, 16, 16, 8192], P(None, 'grp', 'dec', 'pre'), may hold values from -12 to 12
- step_decay: float32 [2, 16, 16, 64], P(None, 'grp', None, 'pre'), may hold values from -1 to -0.05
Outputs:
- prompt_out: bfloat16 [16, 1024, 8192], P(('grp', 'dec'), None, 'pre')
- step_out: bfloat16 [2, 16, 16, 8192], P(None, 'grp', 'dec', 'pre')
Inputs may be any that keep to these rules, and one draw needn't show every extreme that they name: `decode_owner`: each value of grp owns exactly 4 prompts. Among the prompts of one index of dec (over all indices of grp), at most 2 have the same owner, and in every index of dec some owner has 2 of them. `parent_beam`: A parent is a beam of the same slot. In each slot, each block of 16 // 4 beams held by one index of dec has exactly one row whose parent lies in another block. Over the 4 slots of one index of grp, the rows of one block take parents from one other block at most 2 times, and this is reached.
All inputs are finite; a program needn't handle non-finite values.
Results may differ from a plain program's by a relative error of at most 0.0041.
Values may be sent and summed in bfloat16 or wider, within the bound.
No kernel may reach another device: no remote copies, remote signals or barrier semaphores. Data moves between devices by JAX's collectives and lax.ppermute only.
A program may use at most 256 MiB of HBM per device.

v0:
```python
import jax
import jax.numpy as jnp
from jax import lax
from jax.sharding import PartitionSpec as P

HEAD_COUNT = 64
HD = 128
BLK = 256


highest = lax.Precision.HIGHEST
epsilon = 1e-06


def earlier_count(labels):
    total = labels.shape[-1]
    indices = jnp.arange(total, dtype=jnp.int32)
    before = indices[None, :] < indices[:, None]
    same_label = labels[..., :, None] == labels[..., None, :]
    return jnp.sum(jnp.where(same_label & before, 1, 0), axis=-1).astype(jnp.int32)


def pick_rows(matches, sources):
    chosen = jnp.sum(jnp.where(matches, sources, 0), axis=-1)
    return (chosen, jnp.any(matches, axis=-1))


def outer_terms(key_rows, value_rows):
    return jnp.einsum("nbhd,nbhe->nbhde", key_rows, value_rows, preferred_element_type=jnp.float32)


def prompt_pass(prompt_queries, prompt_keys, prompt_values, prompt_decay, prompt_lengths):
    seq_local, token_count, columns = prompt_queries.shape
    head_local = prompt_decay.shape[1]
    head_size = columns // head_local
    position_ids = jnp.arange(token_count, dtype=jnp.int32)
    live_mask = position_ids[None, :] < prompt_lengths[:, None]
    masked_decay = jnp.where(live_mask[:, None, :], prompt_decay, jnp.float32(0.0))
    cumulative = jnp.cumsum(masked_decay, axis=2)
    full_shape = (seq_local, token_count, head_local, head_size)
    queries = prompt_queries.reshape(full_shape)
    keys_live = jnp.where(live_mask[:, :, None], prompt_keys, jnp.zeros_like(prompt_keys)).reshape(
        full_shape
    )
    values = prompt_values.reshape(full_shape)
    return (live_mask, cumulative, queries, keys_live, values)


def final_states(cumulative, keys_live, values):
    weights_end = jnp.exp(cumulative[:, :, -1:] - cumulative)
    scaled = keys_live.astype(jnp.float32) * jnp.swapaxes(weights_end, 1, 2)[..., None]
    return jnp.einsum("sthd,sthe->shde", scaled, values.astype(jnp.float32), precision=highest)


def prompt_mix(cumulative, queries, keys_live, values):
    seq_local, token_count, head_local, head_size = queries.shape
    carried_state = jnp.zeros((seq_local, head_local, head_size, head_size), jnp.float32)
    inner_index = jnp.arange(BLK)
    causal = inner_index[:, None] >= inner_index[None, :]
    pieces = []
    block_total = token_count // BLK
    for block_index in range(block_total):
        block_start = block_index * BLK
        block_stop = block_start + BLK
        query_block = queries[:, block_start:block_stop]
        key_block = keys_live[:, block_start:block_stop]
        value_block = values[:, block_start:block_stop]
        block_cum = cumulative[:, :, block_start:block_stop]
        if block_index == 0:
            anchor = jnp.zeros((seq_local, head_local), jnp.float32)
        else:
            anchor = cumulative[:, :, block_start - 1]
        scores = jnp.einsum(
            "sthd,suhd->shtu", query_block, key_block, preferred_element_type=jnp.float32
        )
        exponent = jnp.where(causal, block_cum[..., :, None] - block_cum[..., None, :], -jnp.inf)
        weights = (scores * jnp.exp(exponent)).astype(jnp.bfloat16)
        local_part = jnp.einsum(
            "shtu,suhe->sthe", weights, value_block, preferred_element_type=jnp.float32
        )
        lift_factor = jnp.swapaxes(jnp.exp(block_cum - anchor[..., None]), 1, 2)[..., None]
        carried = jnp.einsum(
            "sthd,shde->sthe",
            query_block.astype(jnp.float32) * lift_factor,
            carried_state,
            precision=highest,
        )
        pieces.append(local_part + carried)
        if block_index + 1 < block_total:
            block_end = block_cum[..., -1]
            fade_factor = jnp.swapaxes(jnp.exp(block_end[..., None] - block_cum), 1, 2)[..., None]
            carried_state = jnp.exp(block_end - anchor)[
                ..., None, None
            ] * carried_state + jnp.einsum(
                "sthd,sthe->shde",
                key_block.astype(jnp.float32) * fade_factor,
                value_block.astype(jnp.float32),
                precision=highest,
            )
    return jnp.concatenate(pieces, axis=1)


def ship_states(final_state, decode_owner, slot_count):
    group = lax.axis_index("grp")
    seq_total = decode_owner.shape[0]
    seq_ids = jnp.arange(seq_total, dtype=jnp.int32)
    slot_order = jnp.argsort(decode_owner * seq_total + seq_ids)
    wanted = lax.dynamic_slice_in_dim(slot_order, group * slot_count, slot_count, 0)
    everyone = lax.all_gather(final_state, ("grp", "dec"), axis=0, tiled=True)
    return jnp.take(everyone, wanted, axis=0)


def decode_pass(
    prompt_state, norm_gain, parent_beam, step_queries, step_keys, step_values, step_decay
):
    slot_count, per_block, columns = step_queries.shape[1:]
    head_local = prompt_state.shape[1]
    head_size = prompt_state.shape[2]
    own_block = lax.axis_index("dec")
    block_count = lax.axis_size("dec")
    full_shape = (slot_count, per_block, head_local, head_size)
    own_decay = lax.dynamic_slice_in_dim(step_decay, own_block * per_block, per_block, 2)
    first_state = jnp.exp(own_decay[0])[..., None, None] * prompt_state[:, None] + outer_terms(
        step_keys[0].reshape(full_shape), step_values[0].reshape(full_shape)
    )
    first_mix = jnp.einsum(
        "nbhd,nbhde->nbhe",
        step_queries[0].reshape(full_shape).astype(jnp.float32),
        first_state,
        precision=highest,
    )
    row_count = slot_count * per_block
    parent_rows = (
        parent_beam.reshape(slot_count, block_count, per_block)
        .transpose(1, 0, 2)
        .reshape(block_count, row_count)
    )
    source_block = parent_rows // per_block
    source_row = (jnp.arange(row_count, dtype=jnp.int32) // per_block * per_block)[
        None, :
    ] + parent_rows % per_block
    row_rank = earlier_count(source_block)
    capacity = (slot_count + block_count - 2) // (block_count - 1)
    target_block = jnp.arange(block_count, dtype=jnp.int32)[:, None]
    needed = (source_block == own_block) & (target_block != own_block)
    matches = needed[:, None, :] & (
        row_rank[:, None, :] == jnp.arange(capacity, dtype=jnp.int32)[None, :, None]
    )
    chosen, filled_slot = pick_rows(matches, source_row[:, None, :])
    flat_first = first_state.reshape((row_count,) + first_state.shape[2:])
    outgoing = jnp.where(
        filled_slot[..., None, None, None], jnp.take(flat_first, chosen, axis=0), jnp.float32(0.0)
    )
    arrived = lax.all_to_all(outgoing, "dec", split_axis=0, concat_axis=0, tiled=True)
    own_source = lax.dynamic_index_in_dim(source_block, own_block, 0, keepdims=False)
    own_rank = lax.dynamic_index_in_dim(row_rank, own_block, 0, keepdims=False)
    own_row = lax.dynamic_index_in_dim(source_row, own_block, 0, keepdims=False)
    pool_index = jnp.where(
        own_source == own_block, own_row, row_count + own_source * capacity + own_rank
    )
    pooled = jnp.concatenate(
        [flat_first, arrived.reshape((block_count * capacity,) + first_state.shape[2:])], axis=0
    )
    parent_state = jnp.take(pooled, pool_index, axis=0).reshape(first_state.shape)
    second_state = jnp.exp(own_decay[1])[..., None, None] * parent_state + outer_terms(
        step_keys[1].reshape(full_shape), step_values[1].reshape(full_shape)
    )
    second_mix = jnp.einsum(
        "nbhd,nbhde->nbhe",
        step_queries[1].reshape(full_shape).astype(jnp.float32),
        second_state,
        precision=highest,
    )
    both_mix = jnp.stack([first_mix, second_mix])
    square_sums = jnp.sum(both_mix * both_mix, axis=(3, 4))
    totals = lax.psum(square_sums, "pre")
    scale_rows = lax.rsqrt(totals / (HEAD_COUNT * HD) + epsilon)
    return (
        both_mix.reshape(2, slot_count, per_block, columns) * scale_rows[..., None] * norm_gain
    ).astype(jnp.bfloat16)


def local(
    prompt_queries,
    prompt_keys,
    prompt_values,
    prompt_decay,
    prompt_lengths,
    norm_gain,
    decode_owner,
    parent_beam,
    step_queries,
    step_keys,
    step_values,
    step_decay,
):
    live_mask, cumulative, queries, keys_live, values = prompt_pass(
        prompt_queries, prompt_keys, prompt_values, prompt_decay, prompt_lengths
    )
    final_state = final_states(cumulative, keys_live, values)
    prompt_state = ship_states(final_state, decode_owner, parent_beam.shape[0])
    mixed = prompt_mix(cumulative, queries, keys_live, values)
    mixed = jnp.where(live_mask[:, :, None, None], mixed, jnp.float32(0.0))
    square_sums = jnp.sum(mixed * mixed, axis=(2, 3))
    totals = lax.psum(square_sums, "pre")
    scale_rows = lax.rsqrt(totals / (HEAD_COUNT * HD) + epsilon)
    seq_local, token_count, columns = prompt_queries.shape
    prompt_out = (
        mixed.reshape(seq_local, token_count, columns) * scale_rows[..., None] * norm_gain
    ).astype(jnp.bfloat16)
    step_out = decode_pass(
        prompt_state, norm_gain, parent_beam, step_queries, step_keys, step_values, step_decay
    )
    return (prompt_out, step_out)


def solution(mesh):
    in_specs = (
        P(("grp", "dec"), None, "pre"),
        P(("grp", "dec"), None, "pre"),
        P(("grp", "dec"), None, "pre"),
        P(("grp", "dec"), "pre", None),
        P(("grp", "dec")),
        P("pre"),
        P(),
        P("grp", None),
        P(None, "grp", "dec", "pre"),
        P(None, "grp", "dec", "pre"),
        P(None, "grp", "dec", "pre"),
        P(None, "grp", None, "pre"),
    )
    out_specs = (P(("grp", "dec"), None, "pre"), P(None, "grp", "dec", "pre"))
    return jax.shard_map(local, mesh=mesh, in_specs=in_specs, out_specs=out_specs, check_vma=False)
```

profile of v0, /device:TPU:0, one launch (start us, length us, event | category | flops | bytes accessed | tf_op | source)
XLA Modules:
  0.0 783.4 jit_solution(17926176885944047646)
XLA Ops:
  8.8 9.0 %reduce-window.6 = f32[1,32,8,128]{3,2,1,0:T(8,128)S(1)} reduce-window(f32[1,32,8,128]{3,2,1,0:T(8,128)S(1)} %bitcast.288, f32[]{:T(128)} %constant.105.clone.1), window={size=1x1x1x128 pad=0_0x0_0x0_0x127_0}, to_apply=%region_0.1 | reduce-window | flops 4161536 | bytes 262148 | tf_op jit(solution)/shard_map/reduce-window
  18.6 11.9 %copy.178 = bf16[1,1024,4096]{1,2,0:T(8,128)(2,1)} copy(bf16[1,1024,4096]{2,1,0:T(8,128)(2,1)} %param.13) | data formatting | bytes 16777216 | tf_op args[1]
  30.6 7.3 broadcast_select_fusion
  37.9 9.4 %copy.253 = bf16[128,8,32,128]{3,2,1,0:T(8,128)(2,1)} copy(bf16[128,8,32,128]{3,1,2,0:T(8,128)(2,1)} %bitcast.261) | data formatting | bytes 16777216
  47.3 19.3 %fusion.10 = f32[32,128,128]{2,1,0:T(8,128)} fusion(bf16[1024,32,128]{0,2,1:T(8,128)(2,1)} %bitcast.276, bf16[1024,32,128]{2,1,0:T(8,128)(2,1)} %bitcast.282, f32[1024,32]{0,1:T(8,128)S(1)} %copy.219), kind=kOutput, calls=%fused_computation.18 | convolution fusion | flops 6450839552 | bytes 19005440 | tf_op jit(solution)/shard_map/sthd,sthe->shde/dot_general | solution.py:52
  71.1 176.3 %all-gather.3.cloned.1.call-done = f32[512,128,128]{2,1,0:T(8,128)} async-done(((f32[32,128,128]{2,1,0:T(8,128)}), f32[512,128,128]{2,1,0:T(8,128)}) %all-gather.3.cloned.1.call-update) | async-done | bytes 33554448 | tf_op jit(solution)/shard_map/all_gather | solution.py:109
  247.5 7.8 gather_fusion
  259.6 13.7 %multiply_add_fusion = f32[4,4,32,128,128]{4,3,2,1,0:T(8,128)} fusion(f32[4,4,32,128]{3,2,1,0:T(8,128)S(1)} %reshape.923, f32[4,4,32,128]{3,2,1,0:T(8,128)S(1)} %reshape.922, f32[4,32,128,128]{3,2,1,0:T(8,128)S(1)} %broadcast_select_fusion.1, f32[4,4,32]{2,1,0:T(4,128)S(1)} %get-tuple-element.52), kind=kLoop, calls=%fused_computation.9 | loop fusion | flops 25165824 | bytes 42469376 | tf_op jit(solution)/shard_map/add | solution.py:123
  273.2 12.1 %gather_fusion.1 = f32[8,32,128,128]{3,2,1,0:T(8,128)} fusion(f32[16,32,128,128]{3,2,1,0:T(8,128)} %bitcast.249, s32[1024]{0:T(1024)S(1)} %pad_clamp_fusion.1), kind=kCustom, calls=%fused_computation.1 | custom fusion | bytes 33554464 | tf_op jit(solution)/shard_map/jit(_take)/gather | solution.py:152
  285.4 12.3 %select_select_fusion = f32[4,2,32,128,128]{4,3,2,1,0:T(8,128)} fusion(f32[4,2,32,128,128]{4,3,2,1,0:T(8,128)} %bitcast.251, pred[4,2]{1,0:T(4,128)(4,1)S(1)} %copy.223, pred[4,2]{1,0:T(4,128)(4,1)S(1)} %copy.222), kind=kLoop, calls=%fused_computation.22 | loop fusion | flops 8388608 | bytes 33554448 | tf_op jit(solution)/shard_map/jit(_where)/select_n | solution.py:151
  297.7 7.0 all-to-all-start
  304.7 12.0 %copy.186 = bf16[1,1024,4096]{1,2,0:T(8,128)(2,1)} copy(bf16[1,1024,4096]{2,1,0:T(8,128)(2,1)} %param.14) | data formatting | bytes 16777216 | tf_op args[2]
  326.7 12.0 %copy.180 = bf16[1,1024,4096]{1,2,0:T(8,128)(2,1)} copy(bf16[1,1024,4096]{2,1,0:T(8,128)(2,1)} %param.12) | data formatting | bytes 16777216 | tf_op args[0]
  355.2 5.9 fusion.153
  379.3 6.9 fusion.40
  386.2 8.3 %fusion.32 = f32[32,128,128]{2,1,0:T(8,128)} fusion(bf16[1,256,32,128]{3,1,2,0:T(8,128)(2,1)} %copy.248, f32[256,32]{0,1:T(8,128)} %copy.214, bf16[1,1024,32,128]{1,3,2,0:T(8,128)(2,1)} %bitcast.270), kind=kOutput, calls=%fused_computation.42 | convolution fusion | flops 1612709888 | bytes 6324224 | tf_op jit(solution)/shard_map/sthd,sthe->shde/dot_general | solution.py:94
  394.6 7.2 multiply_add_fusion.2
  401.8 6.3 fusion.22
  408.1 7.8 bitcast_add_fusion.3
  416.0 6.5 fusion.26
  422.5 10.3 %bitcast_add_fusion.1 = f32[32,128,256]{2,1,0:T(8,128)} fusion(f32[32,256,128]{1,2,0:T(8,128)} %fusion.26, f32[32,128,128]{2,1,0:T(8,128)} %multiply_add_fusion.2, bf16[1,256,32,128]{3,1,2,0:T(8,128)(2,1)} %copy.249, f32[256,32]{0,1:T(8,128)S(1)} %copy.207), kind=kOutput, calls=%fused_computation.49 | convolution fusion | flops 1613758464 | bytes 12615680 | tf_op jit(solution)/shard_map/sthd,shde->sthe/dot_general | solution.py:82
  432.8 6.4 fusion.24
  439.2 8.6 %bitcast_add_fusion.2 = f32[32,128,256]{2,1,0:T(8,128)} fusion(f32[32,256,128]{1,2,0:T(8,128)} %fusion.24, bf16[1,256,32,128]{3,1,2,0:T(8,128)(2,1)} %copy.247, f32[256,32]{0,1:T(8,128)S(1)} %copy.197, f32[32,128,128]{2,1,0:T(8,128)S(1)} %fusion.40, f32[32]{0:T(128)S(1)} %get-tuple-element.43), kind=kOutput, calls=%fused_computation.54 | convolution fusion | flops 1614282752 | bytes 12615808 | tf_op jit(solution)/shard_map/sthd,shde->sthe/dot_general | solution.py:82
  447.8 6.7 fusion.28
  454.5 8.9 %bitcast_add_fusion = f32[32,128,256]{2,1,0:T(8,128)S(1)} fusion(f32[32,256,128]{1,2,0:T(8,128)} %fusion.28, bf16[1,256,32,128]{3,1,2,0:T(8,128)(2,1)} %copy.251, f32[256,32]{0,1:T(8,128)S(1)} %copy.217, f32[32,128,128]{2,1,0:T(8,128)} %fusion.32, f32[32,128,128]{2,1,0:T(8,128)S(1)} %copy-done.5, f32[32]{0:T(128)S(1)} %copy-done.21), kind=kOutput, calls=%fused_computation.44 | convolution fusion | flops 1614807040 | bytes 14712960 | tf_op jit(solution)/shard_map/sthd,shde->sthe/dot_general | solution.py:82
  467.2 21.5 %fusion.82 = f32[4,4,32,1,128]{4,3,2,1,0:T(1,128)S(1)} fusion(bf16[4,4,32,128,1]{3,4,2,1,0:T(2,128)(2,1)S(1)} %copy-done.9, f32[4,4,32,128]{3,2,1,0:T(8,128)S(1)} %reshape.923, f32[4,4,32,128]{3,2,1,0:T(8,128)S(1)} %reshape.922, f32[4,32,128,128]{3,2,1,0:T(8,128)S(1)} %bitcast.263, f32[4,4,32]{2,1,0:T(4,128)S(1)} %get-tuple-element.52), kind=kOutput, calls=%fused_computation.93 | convolution fusion | flops 125829120 | bytes 9308160 | tf_op jit(solution)/shard_map/nbhd,nbhde->nbhe/dot_general | solution.py:126
  488.8 179.3 %all-to-all-done = f32[4,2,32,128,128]{4,3,2,1,0:T(8,128)} async-done(((f32[4,2,32,128,128]{4,3,2,1,0:T(8,128)}), f32[4,2,32,128,128]{4,3,2,1,0:T(8,128)}, u32[]{:S(2)}, u32[]{:S(2)}) %all-to-all-start) | async-done | bytes 16777248 | tf_op jit(solution)/shard_map/all_to_all | solution.py:154
  668.1 33.5 %pad_maximum_fusion = f32[24,32,128,128]{3,2,1,0:T(8,128)} fusion(f32[8,32,128,128]{3,2,1,0:T(8,128)} %bitcast.87, f32[16,32,128,128]{3,2,1,0:T(8,128)} %bitcast.250), kind=kLoop, calls=%fused_computation.3 | loop fusion | flops 12582912 | bytes 100663296 | tf_op jit(solution)/shard_map/concatenate | solution.py:161
  701.6 23.5 %gather_fusion.2 = f32[16,32,128,128]{3,2,1,0:T(8,128)} fusion(f32[24,32,128,128]{3,2,1,0:T(8,128)} %pad_maximum_fusion, s32[1024]{0:T(1024)} %pad_clamp_fusion), kind=kCustom, calls=%fused_computation.2 | custom fusion | bytes 67108928 | tf_op jit(solution)/shard_map/jit(_take)/gather | solution.py:164
  725.1 23.4 %fusion = f32[4,4,32,1,128]{4,3,2,1,0:T(1,128)S(1)} fusion(bf16[4,4,32,128,1]{3,4,2,1,0:T(2,128)(2,1)S(1)} %reshape.960, f32[4,4,32,128,128]{4,3,2,1,0:T(8,128)} %bitcast.260, f32[4,4,32,128]{3,2,1,0:T(8,128)S(1)} %copy-done.12, f32[4,4,32,128]{3,2,1,0:T(8,128)S(1)} %copy-done.11, f32[4,4,32]{2,1,0:T(4,128)S(1)} %copy-done.20, pred[4,4]{1,0:T(4,128)(4,1)S(1)} %copy-done.23), kind=kOutput, calls=%fused_computation.4 | convolution fusion | flops 134217728 | bytes 34474000 | tf_op jit(solution)/shard_map/nbhd,nbhde->nbhe/dot_general | solution.py:168
  753.9 9.5 %fusion.7 = bf16[1,1024,4096]{1,2,0:T(8,128)(2,1)} fusion(f32[1,256,4096]{1,2,0:T(8,128)} %bitcast.255, f32[1,256,4096]{1,2,0:T(8,128)} %bitcast.252, f32[1,256,4096]{1,2,0:T(8,128)} %bitcast.258, f32[1,256,4096]{1,2,0:T(8,128)} %bitcast.256, f32[4096]{0:T(1024)S(1)} %copy-done.14, f32[1024]{0:T(1024)S(1)} %bitcast.291, ...), kind=kLoop, calls=%fused_computation.13 | loop fusion | flops 29360128 | bytes 25187328 | tf_op jit(solution)/shard_map/convert_element_type | solution.py:210
  763.3 11.9 %copy.225 = bf16[1,1024,4096]{2,1,0:T(8,128)(2,1)} copy(bf16[1,1024,4096]{1,2,0:T(8,128)(2,1)} %fusion.7) | data formatting | bytes 16777216
  (139 shorter events, 65.1 us)
Async XLA Ops:
  7.2 240.3 %all-gather.3.cloned.1.call-start = ((), (), s32[]{:S(2)}) async-start(), calls=%async_computation.1 | async-start | bytes 35651584 | tf_op jit(solution)/shard_map/all_gather | solution.py:109
  47.3 19.3 %copy-start.22 = (s32[4,16]{1,0:T(4,128)S(1)}, s32[4,16]{1,0:T(4,128)}, u32[]{:S(2)}) copy-start(s32[4,16]{1,0:T(4,128)} %param.19) | copy-start | bytes 772
  47.3 20.6 %copy-start.7 = (bf16[2,4,4,4096]{3,2,1,0:T(4,128)(2,1)S(1)}, bf16[2,4,4,4096]{3,2,1,0:T(4,128)(2,1)}, u32[]{:S(2)}) copy-start(bf16[2,4,4,4096]{3,2,1,0:T(4,128)(2,1)} %param.21) | copy-start | bytes 786436
  47.3 20.8 %copy-start.8 = (bf16[2,4,4,4096]{3,2,1,0:T(4,128)(2,1)S(1)}, bf16[2,4,4,4096]{3,2,1,0:T(4,128)(2,1)}, u32[]{:S(2)}) copy-start(bf16[2,4,4,4096]{3,2,1,0:T(4,128)(2,1)} %param.22) | copy-start | bytes 786436
  47.3 21.1 %copy-start.24 = (s32[16]{0:T(128)S(1)}, s32[16]{0:T(128)}, u32[]{:S(2)}) copy-start(s32[16]{0:T(128)} %param.18) | copy-start | bytes 196
  259.5 13.7 %copy-start.4 = (f32[4,32,128,128]{3,2,1,0:T(8,128)}, f32[4,32,128,128]{3,2,1,0:T(8,128)S(1)}, u32[]{:S(2)}) copy-start(f32[4,32,128,128]{3,2,1,0:T(8,128)S(1)} %broadcast_select_fusion.1) | copy-start | bytes 25165828
  297.7 370.4 %all-to-all-start = ((f32[4,2,32,128,128]{4,3,2,1,0:T(8,128)}), f32[4,2,32,128,128]{4,3,2,1,0:T(8,128)}, u32[]{:S(2)}, u32[]{:S(2)}) async-start(f32[4,2,32,128,128]{4,3,2,1,0:T(8,128)} %select_select_fusion), calls=%async_computation | async-start | bytes 33554432 | tf_op jit(solution)/shard_map/all_to_all | solution.py:154
  304.7 13.8 %copy-start.10 = (bf16[2,4,4,4096]{3,2,1,0:T(4,128)(2,1)S(1)}, bf16[2,4,4,4096]{3,2,1,0:T(4,128)(2,1)}, u32[]{:S(2)}) copy-start(bf16[2,4,4,4096]{3,2,1,0:T(4,128)(2,1)} %param.20) | copy-start | bytes 786436
  376.2 18.4 %copy-start.6 = (bf16[1,256,32,128]{3,1,2,0:T(8,128)(2,1)S(1)}, bf16[1,256,32,128]{3,1,2,0:T(8,128)(2,1)}, u32[]{:S(2)}) copy-start(bf16[1,256,32,128]{3,1,2,0:T(8,128)(2,1)} %copy.246) | copy-start | bytes 6291460
  376.2 18.4 %copy-start.13 = (f32[256,32]{0,1:T(8,128)S(1)}, f32[256,32]{0,1:T(8,128)}, u32[]{:S(2)}) copy-start(f32[256,32]{0,1:T(8,128)} %copy.204) | copy-start | bytes 98308
  386.2 15.6 %copy-start.15 = (pred[256,256]{0,1:T(8,128)(4,1)S(1)}, pred[256,256]{0,1:T(8,128)(4,1)}, u32[]{:S(2)}) copy-start(pred[256,256]{0,1:T(8,128)(4,1)} %iota_compare_fusion) | copy-start | bytes 196612
  386.2 15.6 %copy-start.18 = (f32[32,256]{1,0:T(8,128)S(1)}, f32[32,256]{1,0:T(8,128)}, u32[]{:S(2)}) copy-start(f32[32,256]{1,0:T(8,128)} %copy.184) | copy-start | bytes 98308
  408.1 7.8 copy-start.19
  422.5 10.3 %copy-start.17 = (f32[32,256]{1,0:T(8,128)S(1)}, f32[32,256]{1,0:T(8,128)}, u32[]{:S(2)}) copy-start(f32[32,256]{1,0:T(8,128)} %copy.191) | copy-start | bytes 98308
  439.2 8.7 %copy-start.16 = (f32[32,256]{1,0:T(8,128)S(1)}, f32[32,256]{1,0:T(8,128)}, u32[]{:S(2)}) copy-start(f32[32,256]{1,0:T(8,128)} %copy.211) | copy-start | bytes 98308
  447.8 6.7 copy-start.5
  447.8 6.7 copy-start.21
  454.5 9.0 %copy-start = (f32[32,128,256]{2,1,0:T(8,128)S(1)}, f32[32,128,256]{2,1,0:T(8,128)}, u32[]{:S(2)}) copy-start(f32[32,128,256]{2,1,0:T(8,128)} %bitcast_add_fusion.1) | copy-start | bytes 12582916
  454.5 9.0 %copy-start.2 = (f32[32,128,256]{2,1,0:T(8,128)S(1)}, f32[32,128,256]{2,1,0:T(8,128)}, u32[]{:S(2)}) copy-start(f32[32,128,256]{2,1,0:T(8,128)} %bitcast_add_fusion.3) | copy-start | bytes 12582916
  454.5 9.0 %copy-start.3 = (f32[32,128,256]{2,1,0:T(8,128)S(1)}, f32[32,128,256]{2,1,0:T(8,128)}, u32[]{:S(2)}) copy-start(f32[32,128,256]{2,1,0:T(8,128)} %bitcast_add_fusion.2) | copy-start | bytes 12582916
  454.5 11.1 %slice-start = ((s8[8388608]{0:T(1024)(128)(4,1)}), s8[4194304]{0:T(1024)(128)(4,1)S(1)}, s32[]{:S(2)}) async-start(s8[8388608]{0:T(1024)(128)(4,1)} %bitcast.262), calls=%async_computation.2 | async-start | bytes 8388608
  463.5 2.1 copy-start.1
  463.5 3.7 slice-start.1
  463.5 3.7 copy-start.9
  701.6 23.5 %copy-start.11 = (f32[4,4,32,128]{3,2,1,0:T(8,128)S(1)}, f32[4,4,32,128]{3,2,1,0:T(8,128)}, u32[]{:S(2)}) copy-start(f32[4,4,32,128]{3,2,1,0:T(8,128)} %reshape.924) | copy-start | bytes 786436
  701.6 23.5 %copy-start.12 = (f32[4,4,32,128]{3,2,1,0:T(8,128)S(1)}, f32[4,4,32,128]{3,2,1,0:T(8,128)}, u32[]{:S(2)}) copy-start(f32[4,4,32,128]{3,2,1,0:T(8,128)} %reshape.925) | copy-start | bytes 786436
  701.6 23.5 %copy-start.20 = (f32[4,4,32]{2,1,0:T(4,128)S(1)}, f32[4,4,32]{2,1,0:T(4,128)}, u32[]{:S(2)}) copy-start(f32[4,4,32]{2,1,0:T(4,128)} %get-tuple-element.51) | copy-start | bytes 6148
  701.6 23.5 %copy-start.23 = (pred[4,4]{1,0:T(4,128)(4,1)S(1)}, pred[4,4]{1,0:T(4,128)(4,1)}, u32[]{:S(2)}) copy-start(pred[4,4]{1,0:T(4,128)(4,1)} %compare_and_fusion.2) | copy-start | bytes 52
  725.1 28.7 %copy-start.14 = (f32[4096]{0:T(1024)S(1)}, f32[4096]{0:T(1024)}, u32[]{:S(2)}) copy-start(f32[4096]{0:T(1024)} %param.17) | copy-start | bytes 49156
Sparse Core Ops, SparseCore 0:
  66.8 180.6 all-gather.2
where the time goes:
time: 793 us; the launch traced here: 783 us
  waiting for transfers between devices  356 us (45%)
  local copies, waits for them, and re-layouts  152 us (19%)
  matrix products  148 us (19%)
  other arithmetic  100 us (13%)
  between operations  15.6 us (2%)
    all_to_all x1, waiting for transfers between devices, decode_pass(): lax.all_to_all(outgoing, 'dec', split_axis=0, concat_axis=0, tiled=True)  179 us
    all_gather x1, waiting for transfers between devices, ship_states(): everyone = lax.all_gather(final_state, ('grp', 'dec'), axis=0, tiled=True)  176 us
    unnamed x67, local copies, waits for them, and re-layouts  85.1 us
    dot_general x4, matrix products, prompt_mix(): jnp.einsum('sthd,shde->sthe', query_block.astype(jnp.float32) * lift_fact...  35.7 us
    concatenate x1, other arithmetic, decode_pass(): jnp.concatenate([flat_first, arrived.reshape((block_count * capacity,) +...  33.5 us
    dot_general x4, matrix products, prompt_mix(): jnp.einsum('shtu,suhe->sthe', weights, value_block, preferred_element_typ...  25.9 us
    gather x1, local copies, waits for them, and re-layouts, decode_pass(): jnp.take(pooled, pool_index, axis=0).reshape(first_state.shape)  23.5 us
    dot_general x1, matrix products, decode_pass(): jnp.einsum('nbhd,nbhde->nbhe', step_queries[1].reshape(full_shape).astype...  23.4 us
  transfers between devices with their start and end apart: 2, of which 2 were waited for; matrix products, arithmetic and copies ran while one was open for 24% of the time, Pallas kernels for 0%

commit v1 on v0

v1 whole, which is shorter than its diff:
```python
import functools
import math

import jax
import jax.numpy as jnp
from jax import lax
from jax.experimental import pallas as pl
from jax.experimental.pallas import tpu as pltpu
from jax.sharding import PartitionSpec as P

HEAD_COUNT = 64
HD = 128
BLK = 256
SUB = 128
LANES = 128
LOG2E = math.log2(math.e)
VMEM_BYTES = 56 * 1024 * 1024

highest = lax.Precision.HIGHEST
epsilon = 1e-06
f32 = jnp.float32
bf16 = jnp.bfloat16


def dot_nt(left, right, **more):
    return lax.dot_general(
        left, right, (((1,), (1,)), ((), ())), preferred_element_type=f32, **more
    )


def dot_tn(left, right):
    return lax.dot_general(left, right, (((0,), (0,)), ((), ())), preferred_element_type=f32)


def iota(shape, dim):
    return lax.broadcasted_iota(jnp.int32, shape, dim)


def states_kernel(heads, length_ref, decay_ref, keys_ref, values_ref, state_ref, final_ref, col_ref, row_ref):
    block = pl.program_id(0)
    live_row = block * BLK + iota((heads, BLK), 1) < length_ref[0]
    decay = jnp.where(live_row, decay_ref[...] * LOG2E, 0.0)
    later = iota((BLK, BLK), 0) <= iota((BLK, BLK), 1)
    row_ref[...] = jnp.dot(
        decay, later.astype(f32), precision=highest, preferred_element_type=f32
    )
    padded = jnp.concatenate([decay, jnp.zeros((LANES - heads, BLK), f32)], axis=0)
    earlier = iota((BLK, BLK), 1) <= iota((BLK, BLK), 0)
    col = dot_nt(earlier.astype(f32), padded, precision=highest)
    col_ref[...] = col
    end = col[BLK - 1 : BLK, :]
    live_col = block * BLK + iota((BLK, LANES), 0) < length_ref[0]
    fade = jnp.where(live_col, jnp.exp2(end - col), 0.0)
    keep = jnp.where(block == 0, 0.0, jnp.exp2(end))

    @pl.when(block == 0)
    def _():
        final_ref[...] = jnp.zeros_like(final_ref)

    for head in range(heads):
        span = slice(head * HD, (head + 1) * HD)
        faded = (keys_ref[:, span].astype(f32) * fade[:, head : head + 1]).astype(bf16)
        state = final_ref[head] * keep[:, head : head + 1] + dot_tn(values_ref[:, span], faded)
        final_ref[head] = state
        state_ref[0, head] = state.astype(bf16)


def prompt_states(lengths, decay, keys, values):
    heads, tokens = decay.shape
    columns = heads * HD
    blocks = tokens // BLK
    return pl.pallas_call(
        functools.partial(states_kernel, heads),
        grid=(blocks,),
        in_specs=[
            pl.BlockSpec(memory_space=pltpu.SMEM),
            pl.BlockSpec((heads, BLK), lambda b: (0, b)),
            pl.BlockSpec((BLK, columns), lambda b: (b, 0)),
            pl.BlockSpec((BLK, columns), lambda b: (b, 0)),
        ],
        out_specs=[
            pl.BlockSpec((1, heads, HD, HD), lambda b: (b, 0, 0, 0)),
            pl.BlockSpec((heads, HD, HD), lambda b: (0, 0, 0)),
            pl.BlockSpec((BLK, LANES), lambda b: (b, 0)),
            pl.BlockSpec((heads, BLK), lambda b: (0, b)),
        ],
        out_shape=[
            jax.ShapeDtypeStruct((blocks, heads, HD, HD), bf16),
            jax.ShapeDtypeStruct((heads, HD, HD), f32),
            jax.ShapeDtypeStruct((tokens, LANES), f32),
            jax.ShapeDtypeStruct((heads, tokens), f32),
        ],
        compiler_params=pltpu.CompilerParams(vmem_limit_bytes=VMEM_BYTES),
        cost_estimate=pl.CostEstimate(
            flops=2 * tokens * columns * HD,
            bytes_accessed=4 * tokens * columns + 2 * blocks * heads * HD * HD,
            transcendentals=0,
        ),
        name="prompt_states",
    )(lengths, decay, keys, values)


def mix_kernel(group, queries_ref, keys_ref, values_ref, state_ref, col_ref, row_ref, mixed_ref, sums_ref, total):
    block, part = pl.program_id(0), pl.program_id(1)
    shift = lax.rem(LANES - part * group, LANES)
    col_all = pltpu.roll(col_ref[...], shift, 1)
    lift_all = jnp.where(block == 0, 0.0, jnp.exp2(col_all))
    closed = jnp.where(iota((SUB, SUB), 1) <= iota((SUB, SUB), 0), 0.0, -jnp.inf)
    totals = [jnp.zeros((SUB, HD), f32), jnp.zeros((SUB, HD), f32)]
    for head in range(group):
        span = slice(head * HD, (head + 1) * HD)
        queries = queries_ref[:, span]
        keys = keys_ref[:, span]
        values = values_ref[:, span]
        state = state_ref[0, head]
        row = row_ref[head : head + 1, :]
        col = col_all[:, head : head + 1]
        lift = lift_all[:, head : head + 1]
        first = dot_nt(queries[:SUB], jnp.concatenate([keys[:SUB], state], axis=0))
        weights = first[:, :SUB] * jnp.exp2((col[:SUB] - row[:, :SUB]) + closed)
        mixed = jnp.dot(
            weights.astype(bf16), values[:SUB], preferred_element_type=f32
        ) + first[:, SUB:] * lift[:SUB]
        mixed_ref[:SUB, span] = mixed.astype(bf16)
        totals[0] = totals[0] + mixed * mixed
        second = dot_nt(queries[SUB:], keys)
        carried = dot_nt(queries[SUB:], state)
        gap = col[SUB:] - row
        gap = jnp.concatenate([gap[:, :SUB], gap[:, SUB:] + closed], axis=1)
        weights = second * jnp.exp2(gap)
        mixed = jnp.dot(
            weights.astype(bf16), values, preferred_element_type=f32
        ) + carried * lift[SUB:]
        mixed_ref[SUB:, span] = mixed.astype(bf16)
        totals[1] = totals[1] + mixed * mixed
    both = jnp.concatenate(totals, axis=0)

    @pl.when(part == 0)
    def _():
        total[...] = both

    @pl.when(part > 0)
    def _():
        total[...] += both

    @pl.when(part == pl.num_programs(1) - 1)
    def _():
        sums_ref[...] = dot_nt(jnp.ones((8, HD), f32), total[...], precision=highest)


def prompt_mix(queries, keys, values, state, col, row):
    tokens, columns = queries.shape
    heads = columns // HD
    group = min(8, heads)
    blocks = tokens // BLK
    wide = pl.BlockSpec((BLK, group * HD), lambda b, g: (b, g))
    return pl.pallas_call(
        functools.partial(mix_kernel, group),
        grid=(blocks, heads // group),
        in_specs=[
            wide,
            wide,
            wide,
            pl.BlockSpec((1, group, HD, HD), lambda b, g: (jnp.maximum(b - 1, 0), g, 0, 0)),
            pl.BlockSpec((BLK, LANES), lambda b, g: (b, 0)),
            pl.BlockSpec((group, BLK), lambda b, g: (g, b)),
        ],
        out_specs=[wide, pl.BlockSpec((8, BLK), lambda b, g: (0, b))],
        out_shape=[
            jax.ShapeDtypeStruct((tokens, columns), bf16),
            jax.ShapeDtypeStruct((8, tokens), f32),
        ],
        scratch_shapes=[pltpu.VMEM((BLK, HD), f32)],
        compiler_params=pltpu.CompilerParams(vmem_limit_bytes=VMEM_BYTES),
        cost_estimate=pl.CostEstimate(
            flops=2 * tokens * columns * 4 * HD,
            bytes_accessed=8 * tokens * columns,
            transcendentals=tokens * heads * BLK,
        ),
        name="prompt_mix",
    )(queries, keys, values, state, col, row)


def norm_kernel(width, count, length_ref, gain_ref, mixed_ref, *refs):
    block = pl.program_id(0)
    out_ref = refs[count]
    total = refs[0][...]
    for ref in refs[1:count]:
        total = total + ref[...]
    scale = lax.rsqrt(total * (1.0 / width) + epsilon)
    rows = scale.shape[1]
    scale = jnp.where(block * rows + iota(scale.shape, 1) < length_ref[0], scale, 0.0)
    scale = jnp.transpose(scale)[:, :1]
    out_ref[...] = (mixed_ref[...].astype(f32) * scale * gain_ref[...]).astype(bf16)


def prompt_norm(lengths, gain, mixed, sums):
    tokens, columns = mixed.shape
    wide = pl.BlockSpec((BLK, columns), lambda b: (b, 0))
    return pl.pallas_call(
        functools.partial(norm_kernel, HEAD_COUNT * HD, len(sums)),
        grid=(tokens // BLK,),
        in_specs=[
            pl.BlockSpec(memory_space=pltpu.SMEM),
            pl.BlockSpec((1, columns), lambda b: (0, 0)),
            wide,
        ]
        + [pl.BlockSpec((8, BLK), lambda b: (0, b))] * len(sums),
        out_specs=wide,
        out_shape=jax.ShapeDtypeStruct((tokens, columns), bf16),
        compiler_params=pltpu.CompilerParams(vmem_limit_bytes=VMEM_BYTES),
        cost_estimate=pl.CostEstimate(
            flops=3 * tokens * columns, bytes_accessed=4 * tokens * columns, transcendentals=0
        ),
        name="prompt_norm",
    )(lengths, gain, mixed, *sums)


def read_kernel(heads, count, *refs):
    state_ref = refs[count]
    outs = refs[count + 1 :]
    rows = refs[0].shape[0]
    for head in range(heads):
        span = slice(head * HD, (head + 1) * HD)
        state = state_ref[head]
        high = state.astype(bf16)
        low = (state - high.astype(f32)).astype(bf16)
        queries = jnp.concatenate([ref[:, span].astype(f32) for ref in refs[:count]], axis=0)
        queries = queries.astype(bf16)
        read = dot_nt(queries, high) + dot_nt(queries, low)
        for index, out in enumerate(outs):
            out[:, span] = read[index * rows : (index + 1) * rows].astype(bf16)


def read_states(queries, final_state):
    heads = final_state.shape[0]
    count = len(queries)
    return pl.pallas_call(
        functools.partial(read_kernel, heads, count),
        out_shape=[jax.ShapeDtypeStruct(queries[0].shape, bf16)] * count,
        compiler_params=pltpu.CompilerParams(vmem_limit_bytes=VMEM_BYTES),
        cost_estimate=pl.CostEstimate(
            flops=4 * count * queries[0].size * HD,
            bytes_accessed=4 * final_state.size + 4 * count * queries[0].size,
            transcendentals=0,
        ),
        name="read_states",
    )(*queries, final_state)


def steps_kernel(heads, queries_ref, keys_ref, values_ref, reads_ref, parent_keys_ref, parent_values_ref, first_ref, second_ref, mixed_ref, sums_ref):
    rows = queries_ref.shape[0]
    total = jnp.zeros((rows, HD), f32)
    for head in range(heads):
        span = slice(head * HD, (head + 1) * HD)
        queries = queries_ref[:, span].astype(f32)
        own = jnp.sum(queries * keys_ref[:, span].astype(f32), axis=1, keepdims=True)
        parent = jnp.sum(queries * parent_keys_ref[:, span].astype(f32), axis=1, keepdims=True)
        mixed = (
            first_ref[:, head : head + 1] * reads_ref[:, span].astype(f32)
            + own * values_ref[:, span].astype(f32)
            + second_ref[:, head : head + 1] * parent * parent_values_ref[:, span].astype(f32)
        )
        mixed_ref[:, span] = mixed
        total = total + mixed * mixed
    sums_ref[...] = jnp.broadcast_to(jnp.sum(total, axis=1, keepdims=True), sums_ref.shape)


def steps_mix(queries, keys, values, reads, parent_keys, parent_values, first, second):
    rows, columns = queries.shape
    return pl.pallas_call(
        functools.partial(steps_kernel, columns // HD),
        out_shape=[
            jax.ShapeDtypeStruct((rows, columns), f32),
            jax.ShapeDtypeStruct((rows, LANES), f32),
        ],
        compiler_params=pltpu.CompilerParams(vmem_limit_bytes=VMEM_BYTES),
        name="steps_mix",
    )(queries, keys, values, reads, parent_keys, parent_values, first, second)


def swap(array, axis, bit):
    size = lax.axis_size(axis)
    return lax.ppermute(array, axis, [(index, index ^ bit) for index in range(size)])


def over_pre(array):
    size = lax.axis_size("pre")
    return [array] + [swap(array, "pre", bit) for bit in range(1, size)]


def earlier_count(labels):
    total = labels.shape[-1]
    indices = jnp.arange(total, dtype=jnp.int32)
    before = indices[None, :] < indices[:, None]
    same_label = labels[..., :, None] == labels[..., None, :]
    return jnp.sum(jnp.where(same_label & before, 1, 0), axis=-1).astype(jnp.int32)


def pick_rows(matches, sources):
    return jnp.sum(jnp.where(matches, sources, 0), axis=-1)


def local(
    prompt_queries,
    prompt_keys,
    prompt_values,
    prompt_decay,
    prompt_lengths,
    norm_gain,
    decode_owner,
    parent_beam,
    step_queries,
    step_keys,
    step_values,
    step_decay,
):
    tokens, columns = prompt_queries.shape[1:]
    heads = prompt_decay.shape[1]
    steps, slots, per_block = step_queries.shape[:3]
    rows = steps * per_block
    group, block = lax.axis_index("grp"), lax.axis_index("dec")
    group_count, block_count = lax.axis_size("grp"), lax.axis_size("dec")
    seq_total = decode_owner.shape[0]
    near = group_count // 2

    def slot_major(array):
        return jnp.swapaxes(array, 0, 1).reshape(slots, rows, columns)

    queries = slot_major(step_queries)
    keys = slot_major(step_keys)
    values = slot_major(step_values)

    rank = earlier_count(decode_owner)
    slot_ids = jnp.arange(seq_total, dtype=jnp.int32)
    slot_of = decode_owner * slots + rank
    slot_order = pick_rows(slot_of[None, :] == slot_ids[:, None], slot_ids[None, :])
    around = block ^ jnp.arange(block_count, dtype=jnp.int32)

    def widen(array):
        pool = array
        bit = 1
        while bit < near:
            pool = jnp.concatenate([pool, swap(pool, "grp", bit)], axis=0)
            bit *= 2
        return pool

    def place(owner, index, count):
        offset = owner ^ group
        return jnp.where(offset < near, offset * count + index, 0), offset < near

    pool = widen(queries)
    theirs = (group ^ near) * block_count + around
    mine = group * block_count + around
    sent = jnp.take(pool, place(decode_owner[theirs], rank[theirs], slots)[0], axis=0)
    came = swap(sent, "grp", near)
    spot, here = place(decode_owner[mine], rank[mine], slots)
    for_prompts = jnp.where(here[:, None, None], jnp.take(pool, spot, axis=0), came)

    parent_rows = (
        parent_beam.reshape(slots, block_count, per_block)
        .transpose(1, 0, 2)
        .reshape(block_count, slots * per_block)
    )
    source_block = parent_rows // per_block
    slot_row = jnp.arange(slots * per_block, dtype=jnp.int32) // per_block * rows
    source_row = slot_row[None, :] + parent_rows % per_block
    row_rank = earlier_count(source_block)
    capacity = (slots + block_count - 2) // (block_count - 1)
    needed = source_block == block
    matches = needed[:, None, :] & (
        row_rank[:, None, :] == jnp.arange(capacity, dtype=jnp.int32)[None, :, None]
    )
    chosen = pick_rows(matches, source_row[:, None, :])[around]
    flat_keys = keys.reshape(slots * rows, columns)
    flat_values = values.reshape(slots * rows, columns)
    parcel_keys = jnp.take(flat_keys, chosen, axis=0)
    parcel_values = jnp.take(flat_values, chosen, axis=0)
    parcels = jnp.concatenate([parcel_keys, parcel_values], axis=1)

    query_parts, key_parts, value_parts = [for_prompts[0]], [], []
    split = columns * 2 * capacity // rows
    for bit in range(1, block_count):
        message = jnp.concatenate(
            [for_prompts[bit], parcels[bit].reshape(rows, split)], axis=1
        )
        message = swap(message, "dec", bit)
        query_parts.append(message[:, :columns])
        parcel = message[:, columns:].reshape(2 * capacity, columns)
        key_parts.append(parcel[:capacity])
        value_parts.append(parcel[capacity:])

    own_source = lax.dynamic_index_in_dim(source_block, block, 0, keepdims=False)
    own_rank = lax.dynamic_index_in_dim(row_rank, block, 0, keepdims=False)
    own_row = lax.dynamic_index_in_dim(source_row, block, 0, keepdims=False)
    away = (own_source ^ block) - 1
    parent_index = jnp.where(
        own_source == block, own_row, slots * rows + away * capacity + own_rank
    )
    parent_keys = jnp.take(jnp.concatenate([flat_keys] + key_parts), parent_index, axis=0)
    parent_values = jnp.take(jnp.concatenate([flat_values] + value_parts), parent_index, axis=0)

    def second_rows(array):
        array = array.reshape(slots, per_block, array.shape[-1])
        return jnp.pad(array, ((0, 0), (per_block, 0), (0, 0))).reshape(slots * rows, -1)

    parent_keys = second_rows(parent_keys)
    parent_values = second_rows(parent_values)

    own_decay = lax.dynamic_slice_in_dim(step_decay, block * per_block, per_block, 2)
    own_parents = lax.dynamic_slice_in_dim(parent_beam, block * per_block, per_block, 1)
    parent_decay = jnp.take_along_axis(step_decay[0], own_parents[:, :, None], axis=1)
    first = jnp.exp(jnp.stack([own_decay[0], own_decay[1] + parent_decay], axis=1))
    first = first.reshape(slots * rows, heads)
    second = second_rows(jnp.exp(own_decay[1]).reshape(slots * per_block, heads))

    state, final_state, col, row = prompt_states(
        prompt_lengths, prompt_decay[0], prompt_keys[0], prompt_values[0]
    )
    reads = read_states(query_parts, final_state)
    reads = [reads[0]] + [swap(reads[bit], "dec", bit) for bit in range(1, block_count)]
    pool = widen(jnp.stack(reads))

    def located(owner):
        prompts = lax.dynamic_slice_in_dim(slot_order, owner * slots, slots, 0)
        return place(prompts // block_count, (prompts % block_count) ^ block, block_count)

    sent = jnp.take(pool, located(group ^ near)[0], axis=0)
    came = swap(sent, "grp", near)
    spot, here = located(group)
    slot_reads = jnp.where(here[:, None, None], jnp.take(pool, spot, axis=0), came)

    mixed, sums = prompt_mix(
        prompt_queries[0], prompt_keys[0], prompt_values[0], state, col, row
    )
    prompt_out = prompt_norm(prompt_lengths, norm_gain[None], mixed, over_pre(sums))

    step_mixed, step_sums = steps_mix(
        queries.reshape(slots * rows, columns),
        flat_keys,
        flat_values,
        slot_reads.reshape(slots * rows, columns),
        parent_keys,
        parent_values,
        first,
        second,
    )
    step_total = functools.reduce(jnp.add, over_pre(step_sums[:, :1]))
    scale = lax.rsqrt(step_total / (HEAD_COUNT * HD) + epsilon)
    step_out = (step_mixed * scale * norm_gain).astype(bf16)
    step_out = jnp.swapaxes(step_out.reshape(slots, steps, per_block, columns), 0, 1)
    return (prompt_out[None], step_out)


def solution(mesh):
    in_specs = (
        P(("grp", "dec"), None, "pre"),
        P(("grp", "dec"), None, "pre"),
        P(("grp", "dec"), None, "pre"),
        P(("grp", "dec"), "pre", None),
        P(("grp", "dec")),
        P("pre"),
        P(),
        P("grp", None),
        P(None, "grp", "dec", "pre"),
        P(None, "grp", "dec", "pre"),
        P(None, "grp", "dec", "pre"),
        P(None, "grp", None, "pre"),
    )
    out_specs = (P(("grp", "dec"), None, "pre"), P(None, "grp", "dec", "pre"))
    return jax.shard_map(local, mesh=mesh, in_specs=in_specs, out_specs=out_specs, check_vma=False)
```

time: 793 us -> 122 us (0.15); the launches traced: 783 us -> 121 us
  waiting for transfers between devices: 356 us -> 21.4 us
  matrix products: 148 us -> 0 us
  local copies, waits for them, and re-layouts: 152 us -> 19.6 us
  other arithmetic: 100 us -> 4.01 us
  Pallas kernels: 0 us -> 58.9 us
  between operations: 15.6 us -> 1.83 us
  starting transfers between devices: 7.07 us -> 15.7 us
    all_to_all x1 -> x0, waiting for transfers between devices: 179 us -> none  [decode_pass(): lax.all_to_all(outgoing, 'dec', split_axis=0, concat_axis=0, tiled=True)]
    all_gather x1 -> x0, waiting for transfers between devices: 176 us -> none  [ship_states(): everyone = lax.all_gather(final_state, ('grp', 'dec'), axis=0, tiled=True)]
    dot_general x14 -> x0, matrix products: 148 us -> none  [the longest x4 35.7 us: prompt_mix(): jnp.einsum('sthd,shde->sthe', query_block.astype(jnp.float32) * lift_fact...]
    unnamed x67 -> x28, local copies, waits for them, and re-layouts: 85.1 us -> 1.54 us
    pallas_call x0 -> x5, Pallas kernels: none -> 58.9 us  [the longest x1 27.1 us: prompt_mix(): pl.pallas_call(functools.partial(mix_kernel, group), grid=(blocks, heads...]
    gather x3 -> x17, local copies, waits for them, and re-layouts: 43.4 us -> 8.62 us  [the longest x2 1.28 us: local(): spot, here = place(decode_owner[mine], rank[mine], slots)]
    concatenate x1 -> x6, other arithmetic: 33.5 us -> 0.26 us  [the longest x1 0.11 us: local(): parcels = jnp.concatenate([parcel_keys, parcel_values], axis=1)]
    select_n x6 -> x8, other arithmetic: 25.9 us -> 0.59 us  [the longest x2 0.18 us: local(): parcel_keys = jnp.take(flat_keys, chosen, axis=0)]
  transfers between devices with their start and end apart: 2 -> 12, of which waited for: 2 -> 7; matrix products, arithmetic and copies ran while one was open for 24% -> 17% of each run, Pallas kernels for 0% -> 48%
where the time goes in v1:
time: 122 us; the launch traced here: 121 us
  Pallas kernels  58.9 us (48%)
  waiting for transfers between devices  21.4 us (18%)
  local copies, waits for them, and re-layouts  19.6 us (16%)
  starting transfers between devices  15.7 us (13%)
  other arithmetic  4.01 us (3%)
  between operations  1.83 us (2%)
    pallas_call x1, Pallas kernels, prompt_mix(): pl.pallas_call(functools.partial(mix_kernel, group), grid=(blocks, heads...  27.1 us
    ppermute x12, waiting for transfers between devices, swap(): lax.ppermute(array, axis, [(index, index ^ bit) for index in range(size)])  21.4 us
    ppermute x12, starting transfers between devices, swap(): lax.ppermute(array, axis, [(index, index ^ bit) for index in range(size)])  15.7 us
    pallas_call x1, Pallas kernels, prompt_states(): pl.pallas_call(functools.partial(states_kernel, heads), grid=(blocks,), i...  14.4 us
    pallas_call x1, Pallas kernels, prompt_norm(): pl.pallas_call(functools.partial(norm_kernel, HEAD_COUNT * HD, len(sums))...  8.17 us
    pallas_call x1, Pallas kernels, steps_mix(): pl.pallas_call(functools.partial(steps_kernel, columns // HD), out_shape=...  5.52 us
    pallas_call x1, Pallas kernels, read_states(): pl.pallas_call(functools.partial(read_kernel, heads, count), out_shape=[j...  3.67 us
  transfers between devices with their start and end apart: 12, of which 7 were waited for; matrix products, arithmetic and copies ran while one was open for 17% of the time, Pallas kernels for 48%

profile of v1, /device:TPU:0, one launch (start us, length us, event | category | flops | bytes accessed | tf_op | source)
XLA Modules:
  0.0 121.5 jit_solution(15728031567679867288)
XLA Ops:
  0.6 1.2 copy.39
  3.1 14.4 %prompt_states.1 = (bf16[4,32,128,128]{3,2,1,0:T(8,128)(2,1)}, f32[32,128,128]{2,1,0:T(8,128)}, f32[1024,128]{1,0:T(8,128)}, f32[32,1024]{1,0:T(8,128)}) custom-call(s32[1]{0:T(128)S(6)} %copy.55.length_ref, f32[32,1024]{1,0:T(8,128)} %bitcast.78, bf16[1024,4096]{1,0:T(8,128)(2,1)} %bitcast.62, bf16[1024,4096]{1,0:T(8,128)(2,1)} %bitcast.64), custom_call_target="tpu_custom_call" | custom-call | flops 1073741824 | bytes 20971520 | tf_op jit(solution)/shard_map/prompt_states/pallas_call | solution.py:72
  17.6 27.1 %prompt_mix.1 = (bf16[1024,4096]{1,0:T(8,128)(2,1)}, f32[8,1024]{1,0:T(8,128)}) custom-call(bf16[1024,4096]{1,0:T(8,128)(2,1)} %bitcast.66, bf16[1024,4096]{1,0:T(8,128)(2,1)} %bitcast.63, bf16[1024,4096]{1,0:T(8,128)(2,1)} %bitcast.65, bf16[4,32,128,128]{3,2,1,0:T(8,128)(2,1)} %get-tuple-element.17.state_ref, f32[1024,128]{1,0:T(8,128)} %get-tuple-element.18.col_ref, ...), custom_call_target="tpu_custom_call" | custom-call | flops 4294967296 | bytes 33554432 | tf_op jit(solution)/shard_map/prompt_mix/pallas_call | solution.py:157
  44.7 2.5 %collective-permute-start = (f32[8,1024]{1,0:T(8,128)}, f32[8,1024]{1,0:T(8,128)S(1)}, u32[]{:S(2)}, u32[]{:S(2)}) collective-permute-start(f32[8,1024]{1,0:T(8,128)} %get-tuple-element.21.refs_0_), channel_id=1, source_target_pairs={{0,16},{16,0},{1,17},{17,1},{2,18},{18,2},{3,19},{19,3},{4,20},{20... | collective-permute-start | bytes 98312 | tf_op jit(solution)/shard_map/ppermute | solution.py:284
  47.6 0.6 gather_fusion.3
  48.2 0.6 gather_fusion.2
  48.9 0.6 gather_fusion.1
  49.5 0.6 gather_fusion
  55.4 1.6 %collective-permute-start.2 = (bf16[4,8,4096]{2,1,0:T(8,128)(2,1)S(1)}, bf16[4,8,4096]{2,1,0:T(8,128)(2,1)S(1)}, u32[]{:S(2)}, u32[]{:S(2)}) collective-permute-start(bf16[4,8,4096]{2,1,0:T(8,128)(2,1)S(1)} %broadcast_select_fusion.1), channel_id=1, source_target_pairs={{0,8},{4,12},{8,0},{12,4},{1,9},{5,13},{9,1},{13,5},{2,10},{6,14},... | collective-permute-start | bytes 786440 | tf_op jit(solution)/shard_map/ppermute | solution.py:284
  57.8 0.8 reshape_reshape.9.queries_ref
  59.8 4.2 %collective-permute-done.2 = bf16[4,8,4096]{2,1,0:T(8,128)(2,1)S(1)} collective-permute-done((bf16[4,8,4096]{2,1,0:T(8,128)(2,1)S(1)}, bf16[4,8,4096]{2,1,0:T(8,128)(2,1)S(1)}, u32[]{:S(2)}, u32[]{:S(2)}) %collective-permute-start.2) | collective-permute-done | bytes 262176 | tf_op jit(solution)/shard_map/ppermute | solution.py:284
  64.7 1.6 %collective-permute-start.3 = (bf16[8,6144]{1,0:T(8,128)(2,1)S(1)}, bf16[8,6144]{1,0:T(8,128)(2,1)S(1)}, u32[]{:S(2)}, u32[]{:S(2)}) collective-permute-start(bf16[8,6144]{1,0:T(8,128)(2,1)S(1)} %pad_maximum_fusion.3), channel_id=1, source_target_pairs={{0,1},{1,0},{2,3},{3,2},{4,5},{5,4},{6,7},{7,6},{8,9},{9,8},{10,11... | collective-permute-start | bytes 294920 | tf_op jit(solution)/shard_map/ppermute | solution.py:284
  66.4 2.7 %collective-permute-start.4 = (bf16[8,6144]{1,0:T(8,128)(2,1)S(1)}, bf16[8,6144]{1,0:T(8,128)(2,1)S(1)}, u32[]{:S(2)}, u32[]{:S(2)}) collective-permute-start(bf16[8,6144]{1,0:T(8,128)(2,1)S(1)} %pad_maximum_fusion.4), channel_id=1, source_target_pairs={{0,2},{1,3},{2,0},{3,1},{4,6},{5,7},{6,4},{7,5},{8,10},{9,11},{10,... | collective-permute-start | bytes 294920 | tf_op jit(solution)/shard_map/ppermute | solution.py:284
  69.3 1.0 collective-permute-done.3
  70.3 6.1 %collective-permute-done.4 = bf16[8,6144]{1,0:T(8,128)(2,1)S(1)} collective-permute-done((bf16[8,6144]{1,0:T(8,128)(2,1)S(1)}, bf16[8,6144]{1,0:T(8,128)(2,1)S(1)}, u32[]{:S(2)}, u32[]{:S(2)}) %collective-permute-start.4) | collective-permute-done | bytes 98336 | tf_op jit(solution)/shard_map/ppermute | solution.py:284
  80.0 3.7 %read_states.1 = (bf16[8,4096]{1,0:T(8,128)(2,1)}, bf16[8,4096]{1,0:T(8,128)(2,1)}, bf16[8,4096]{1,0:T(8,128)(2,1)}, bf16[8,4096]{1,0:T(8,128)(2,1)}) custom-call(bf16[8,4096]{1,0:T(8,128)(2,1)} %get-tuple-element.46.refs_0_, bf16[8,4096]{1,0:T(8,128)(2,1)} %slice.144.refs_1_, bf16[8,4096]{1,0:T(8,128)(2,1)} %slice.146.refs_2_, ...), custom_call_target="tpu_custom_call" | custom-call | flops 67108864 | bytes 2621440 | tf_op jit(solution)/shard_map/read_states/pallas_call | solution.py:238
  83.7 1.5 %collective-permute-start.6 = (bf16[8,4096]{1,0:T(8,128)(2,1)}, bf16[8,4096]{1,0:T(8,128)(2,1)S(1)}, u32[]{:S(2)}, u32[]{:S(2)}) collective-permute-start(bf16[8,4096]{1,0:T(8,128)(2,1)} %get-tuple-element.24), channel_id=1, source_target_pairs={{0,1},{1,0},{2,3},{3,2},{4,5},{5,4},{6,7},{7,6},{8,9},{9,8},{10,11... | collective-permute-start | bytes 196616 | tf_op jit(solution)/shard_map/ppermute | solution.py:284
  85.2 1.6 %collective-permute-start.7 = (bf16[8,4096]{1,0:T(8,128)(2,1)}, bf16[8,4096]{1,0:T(8,128)(2,1)S(1)}, u32[]{:S(2)}, u32[]{:S(2)}) collective-permute-start(bf16[8,4096]{1,0:T(8,128)(2,1)} %get-tuple-element.25), channel_id=1, source_target_pairs={{0,2},{1,3},{2,0},{3,1},{4,6},{5,7},{6,4},{7,5},{8,10},{9,11},{10,... | collective-permute-start | bytes 196616 | tf_op jit(solution)/shard_map/ppermute | solution.py:284
  86.8 1.3 %collective-permute-start.8 = (bf16[8,4096]{1,0:T(8,128)(2,1)}, bf16[8,4096]{1,0:T(8,128)(2,1)S(1)}, u32[]{:S(2)}, u32[]{:S(2)}) collective-permute-start(bf16[8,4096]{1,0:T(8,128)(2,1)} %get-tuple-element.26), channel_id=1, source_target_pairs={{0,3},{1,2},{2,1},{3,0},{4,7},{5,6},{6,5},{7,4},{8,11},{9,10},{10,... | collective-permute-start | bytes 196616 | tf_op jit(solution)/shard_map/ppermute | solution.py:284
  88.1 0.8 constant_dynamic-update-slice_fusion.6
  88.9 0.8 pad_bitcast_fusion.parent_values_ref
  89.8 1.7 %collective-permute-done.7 = bf16[8,4096]{1,0:T(8,128)(2,1)S(1)} collective-permute-done((bf16[8,4096]{1,0:T(8,128)(2,1)}, bf16[8,4096]{1,0:T(8,128)(2,1)S(1)}, u32[]{:S(2)}, u32[]{:S(2)}) %collective-permute-start.7) | collective-permute-done | bytes 65568 | tf_op jit(solution)/shard_map/ppermute | solution.py:284
  91.5 1.5 %collective-permute-done.8 = bf16[8,4096]{1,0:T(8,128)(2,1)S(1)} collective-permute-done((bf16[8,4096]{1,0:T(8,128)(2,1)}, bf16[8,4096]{1,0:T(8,128)(2,1)S(1)}, u32[]{:S(2)}, u32[]{:S(2)}) %collective-permute-start.8) | collective-permute-done | bytes 65568 | tf_op jit(solution)/shard_map/ppermute | solution.py:284
  93.0 0.9 pad_maximum_fusion.2
  94.0 1.5 %collective-permute-done.9 = bf16[4,8,4096]{2,1,0:T(8,128)(2,1)S(1)} collective-permute-done((bf16[4,8,4096]{2,1,0:T(8,128)(2,1)S(1)}, bf16[4,8,4096]{2,1,0:T(8,128)(2,1)S(1)}, u32[]{:S(2)}, u32[]{:S(2)}) %collective-permute-start.9) | collective-permute-done | bytes 262176 | tf_op jit(solution)/shard_map/ppermute | solution.py:284
  96.2 1.6 %collective-permute-start.10 = (bf16[4,8,4096]{2,1,0:T(8,128)(2,1)S(1)}, bf16[4,8,4096]{2,1,0:T(8,128)(2,1)S(1)}, u32[]{:S(2)}, u32[]{:S(2)}) collective-permute-start(bf16[4,8,4096]{2,1,0:T(8,128)(2,1)S(1)} %broadcast_select_fusion), channel_id=1, source_target_pairs={{0,8},{4,12},{8,0},{12,4},{1,9},{5,13},{9,1},{13,5},{2,10},{6,14},... | collective-permute-start | bytes 786440 | tf_op jit(solution)/shard_map/ppermute | solution.py:284
  97.8 0.8 pad_bitcast_fusion.1.parent_keys_ref
  99.1 5.5 %collective-permute-done.10 = bf16[4,8,4096]{2,1,0:T(8,128)(2,1)S(1)} collective-permute-done((bf16[4,8,4096]{2,1,0:T(8,128)(2,1)S(1)}, bf16[4,8,4096]{2,1,0:T(8,128)(2,1)S(1)}, u32[]{:S(2)}, u32[]{:S(2)}) %collective-permute-start.10) | collective-permute-done | bytes 262176 | tf_op jit(solution)/shard_map/ppermute | solution.py:284
  104.6 0.8 fusion.reads_ref
  105.4 5.5 %steps_mix.1 = (f32[32,4096]{1,0:T(8,128)}, f32[32,128]{1,0:T(8,128)}) custom-call(bf16[32,4096]{1,0:T(8,128)(2,1)} %reshape_reshape.9.queries_ref, bf16[32,4096]{1,0:T(8,128)(2,1)} %copy-done.1, bf16[32,4096]{1,0:T(8,128)(2,1)} %copy-done.2, bf16[32,4096]{1,0:T(8,128)(2,1)} %fusion.reads_ref, bf16[32,4096]{1,0:T(8,128)(2,1)} %pad_bitcast_fusion.1.parent_keys_ref, ...), custom_call_target="tpu_custom_call" | custom-call | tf_op jit(solution)/shard_map/steps_mix/pallas_call | solution.py:271
  112.1 8.2 %prompt_norm.1 = bf16[1024,4096]{1,0:T(8,128)(2,1)} custom-call(s32[1]{0:T(128)S(6)} %copy.55.length_ref, f32[1,4096]{1,0:T(1,128)} %bitcast.80, bf16[1024,4096]{1,0:T(8,128)(2,1)} %get-tuple-element.20.mixed_ref, f32[8,1024]{1,0:T(8,128)} %get-tuple-element.21.refs_0_, f32[8,1024]{1,0:T(8,128)} %copy-done.9), custom_call_target="tpu_custom_call" | custom-call | flops 12582912 | bytes 16777216 | tf_op jit(solution)/shard_map/prompt_norm/pallas_call | solution.py:200
  120.7 0.8 copy.49
  (129 shorter events, 15.6 us)
Async XLA Ops:
  2.0 52.8 %collective-permute-start.1 = (bf16[4,8,4096]{2,1,0:T(8,128)(2,1)S(1)}, bf16[4,8,4096]{2,1,0:T(8,128)(2,1)S(1)}, u32[]{:S(2)}, u32[]{:S(2)}) collective-permute-start(bf16[4,8,4096]{2,1,0:T(8,128)(2,1)S(1)} %get-tuple-element.47), channel_id=1, source_target_pairs={{0,4},{4,0},{8,12},{12,8},{1,5},{5,1},{9,13},{13,9},{2,6},{6,2},{1... | collective-permute-start | bytes 786440 | tf_op jit(solution)/shard_map/ppermute | solution.py:284
  17.6 29.6 %copy-start.10 = (s32[4,16]{1,0:T(4,128)S(1)}, s32[4,16]{1,0:T(4,128)}, u32[]{:S(2)}) copy-start(s32[4,16]{1,0:T(4,128)} %param.25) | copy-start | bytes 772
  17.6 29.8 %copy-start = (s32[16]{0:T(128)S(1)}, s32[16]{0:T(128)}, u32[]{:S(2)}) copy-start(s32[16]{0:T(128)} %param.24) | copy-start | bytes 196
  17.6 34.4 %copy-start.8 = (f32[2,4,16,32]{3,2,1,0:T(8,128)S(1)}, f32[2,4,16,32]{3,2,1,0:T(8,128)}, u32[]{:S(2)}) copy-start(f32[2,4,16,32]{3,2,1,0:T(8,128)} %param.29) | copy-start | bytes 49156
  17.6 34.4 %copy-start.5 = (bf16[2,4,4,4096]{3,2,1,0:T(4,128)(2,1)S(1)}, bf16[2,4,4,4096]{3,2,1,0:T(4,128)(2,1)}, u32[]{:S(2)}) copy-start(bf16[2,4,4,4096]{3,2,1,0:T(4,128)(2,1)} %param.27) | copy-start | bytes 786436
  17.6 35.2 %copy-start.6 = (bf16[2,4,4,4096]{3,2,1,0:T(4,128)(2,1)S(1)}, bf16[2,4,4,4096]{3,2,1,0:T(4,128)(2,1)}, u32[]{:S(2)}) copy-start(bf16[2,4,4,4096]{3,2,1,0:T(4,128)(2,1)} %param.28) | copy-start | bytes 786436
  17.6 39.4 %copy-start.3 = (bf16[2,4,4,4096]{3,2,1,0:T(4,128)(2,1)S(1)}, bf16[2,4,4,4096]{3,2,1,0:T(4,128)(2,1)}, u32[]{:S(2)}) copy-start(bf16[2,4,4,4096]{3,2,1,0:T(4,128)(2,1)} %param.26) | copy-start | bytes 786436
  44.7 66.8 %collective-permute-start = (f32[8,1024]{1,0:T(8,128)}, f32[8,1024]{1,0:T(8,128)S(1)}, u32[]{:S(2)}, u32[]{:S(2)}) collective-permute-start(f32[8,1024]{1,0:T(8,128)} %get-tuple-element.21.refs_0_), channel_id=1, source_target_pairs={{0,16},{16,0},{1,17},{17,1},{2,18},{18,2},{3,19},{19,3},{4,20},{20... | collective-permute-start | bytes 98312 | tf_op jit(solution)/shard_map/ppermute | solution.py:284
  52.2 37.6 %copy-start.1 = (bf16[32,4096]{1,0:T(8,128)(2,1)}, bf16[32,4096]{1,0:T(8,128)(2,1)S(1)}, u32[]{:S(2)}) copy-start(bf16[32,4096]{1,0:T(8,128)(2,1)S(1)} %reshape_reshape.10.keys_ref) | copy-start | bytes 786436
  53.0 43.1 %copy-start.2 = (bf16[32,4096]{1,0:T(8,128)(2,1)}, bf16[32,4096]{1,0:T(8,128)(2,1)S(1)}, u32[]{:S(2)}) copy-start(bf16[32,4096]{1,0:T(8,128)(2,1)S(1)} %reshape_reshape.11.values_ref) | copy-start | bytes 786436
  55.4 8.5 %collective-permute-start.2 = (bf16[4,8,4096]{2,1,0:T(8,128)(2,1)S(1)}, bf16[4,8,4096]{2,1,0:T(8,128)(2,1)S(1)}, u32[]{:S(2)}, u32[]{:S(2)}) collective-permute-start(bf16[4,8,4096]{2,1,0:T(8,128)(2,1)S(1)} %broadcast_select_fusion.1), channel_id=1, source_target_pairs={{0,8},{4,12},{8,0},{12,4},{1,9},{5,13},{9,1},{13,5},{2,10},{6,14},... | collective-permute-start | bytes 786440 | tf_op jit(solution)/shard_map/ppermute | solution.py:284
  64.7 5.6 %collective-permute-start.3 = (bf16[8,6144]{1,0:T(8,128)(2,1)S(1)}, bf16[8,6144]{1,0:T(8,128)(2,1)S(1)}, u32[]{:S(2)}, u32[]{:S(2)}) collective-permute-start(bf16[8,6144]{1,0:T(8,128)(2,1)S(1)} %pad_maximum_fusion.3), channel_id=1, source_target_pairs={{0,1},{1,0},{2,3},{3,2},{4,5},{5,4},{6,7},{7,6},{8,9},{9,8},{10,11... | collective-permute-start | bytes 294920 | tf_op jit(solution)/shard_map/ppermute | solution.py:284
  66.4 10.0 %collective-permute-start.4 = (bf16[8,6144]{1,0:T(8,128)(2,1)S(1)}, bf16[8,6144]{1,0:T(8,128)(2,1)S(1)}, u32[]{:S(2)}, u32[]{:S(2)}) collective-permute-start(bf16[8,6144]{1,0:T(8,128)(2,1)S(1)} %pad_maximum_fusion.4), channel_id=1, source_target_pairs={{0,2},{1,3},{2,0},{3,1},{4,6},{5,7},{6,4},{7,5},{8,10},{9,11},{10,... | collective-permute-start | bytes 294920 | tf_op jit(solution)/shard_map/ppermute | solution.py:284
  69.0 7.5 %collective-permute-start.5 = (bf16[8,6144]{1,0:T(8,128)(2,1)S(1)}, bf16[8,6144]{1,0:T(8,128)(2,1)S(1)}, u32[]{:S(2)}, u32[]{:S(2)}) collective-permute-start(bf16[8,6144]{1,0:T(8,128)(2,1)S(1)} %pad_maximum_fusion.5), channel_id=1, source_target_pairs={{0,3},{1,2},{2,1},{3,0},{4,7},{5,6},{6,5},{7,4},{8,11},{9,10},{10,... | collective-permute-start | bytes 294920 | tf_op jit(solution)/shard_map/ppermute | solution.py:284
  83.7 6.1 %collective-permute-start.6 = (bf16[8,4096]{1,0:T(8,128)(2,1)}, bf16[8,4096]{1,0:T(8,128)(2,1)S(1)}, u32[]{:S(2)}, u32[]{:S(2)}) collective-permute-start(bf16[8,4096]{1,0:T(8,128)(2,1)} %get-tuple-element.24), channel_id=1, source_target_pairs={{0,1},{1,0},{2,3},{3,2},{4,5},{5,4},{6,7},{7,6},{8,9},{9,8},{10,11... | collective-permute-start | bytes 196616 | tf_op jit(solution)/shard_map/ppermute | solution.py:284
  85.2 6.3 %collective-permute-start.7 = (bf16[8,4096]{1,0:T(8,128)(2,1)}, bf16[8,4096]{1,0:T(8,128)(2,1)S(1)}, u32[]{:S(2)}, u32[]{:S(2)}) collective-permute-start(bf16[8,4096]{1,0:T(8,128)(2,1)} %get-tuple-element.25), channel_id=1, source_target_pairs={{0,2},{1,3},{2,0},{3,1},{4,6},{5,7},{6,4},{7,5},{8,10},{9,11},{10,... | collective-permute-start | bytes 196616 | tf_op jit(solution)/shard_map/ppermute | solution.py:284
  86.8 6.3 %collective-permute-start.8 = (bf16[8,4096]{1,0:T(8,128)(2,1)}, bf16[8,4096]{1,0:T(8,128)(2,1)S(1)}, u32[]{:S(2)}, u32[]{:S(2)}) collective-permute-start(bf16[8,4096]{1,0:T(8,128)(2,1)} %get-tuple-element.26), channel_id=1, source_target_pairs={{0,3},{1,2},{2,1},{3,0},{4,7},{5,6},{6,5},{7,4},{8,11},{9,10},{10,... | collective-permute-start | bytes 196616 | tf_op jit(solution)/shard_map/ppermute | solution.py:284
  93.9 1.6 %collective-permute-start.9 = (bf16[4,8,4096]{2,1,0:T(8,128)(2,1)S(1)}, bf16[4,8,4096]{2,1,0:T(8,128)(2,1)S(1)}, u32[]{:S(2)}, u32[]{:S(2)}) collective-permute-start(bf16[4,8,4096]{2,1,0:T(8,128)(2,1)S(1)} %pad_maximum_fusion.2), channel_id=1, source_target_pairs={{0,4},{4,0},{8,12},{12,8},{1,5},{5,1},{9,13},{13,9},{2,6},{6,2},{1... | collective-permute-start | bytes 786440 | tf_op jit(solution)/shard_map/ppermute | solution.py:284
  96.2 8.4 %collective-permute-start.10 = (bf16[4,8,4096]{2,1,0:T(8,128)(2,1)S(1)}, bf16[4,8,4096]{2,1,0:T(8,128)(2,1)S(1)}, u32[]{:S(2)}, u32[]{:S(2)}) collective-permute-start(bf16[4,8,4096]{2,1,0:T(8,128)(2,1)S(1)} %broadcast_select_fusion), channel_id=1, source_target_pairs={{0,8},{4,12},{8,0},{12,4},{1,9},{5,13},{9,1},{13,5},{2,10},{6,14},... | collective-permute-start | bytes 786440 | tf_op jit(solution)/shard_map/ppermute | solution.py:284
  111.0 9.3 %collective-permute-start.11 = (f32[32,1]{1,0:T(8,128)}, f32[32,1]{1,0:T(8,128)S(1)}, u32[]{:S(2)}, u32[]{:S(2)}) collective-permute-start(f32[32,1]{1,0:T(8,128)} %bitcast.83), channel_id=1, source_target_pairs={{0,16},{16,0},{1,17},{17,1},{2,18},{18,2},{3,19},{19,3},{4,20},{20... | collective-permute-start | bytes 392 | tf_op jit(solution)/shard_map/ppermute | solution.py:284
  111.5 0.6 copy-start.9
  112.1 8.2 %copy-start.11 = (f32[32,128]{1,0:T(8,128)S(1)}, f32[32,128]{1,0:T(8,128)}, u32[]{:S(2)}) copy-start(f32[32,128]{1,0:T(8,128)} %get-tuple-element.28) | copy-start | bytes 49156
  112.1 8.3 %copy-start.4 = (f32[32,4096]{1,0:T(8,128)S(1)}, f32[32,4096]{1,0:T(8,128)}, u32[]{:S(2)}) copy-start(f32[32,4096]{1,0:T(8,128)} %get-tuple-element.27) | copy-start | bytes 1572868
  112.1 8.3 %copy-start.7 = (f32[4096]{0:T(1024)S(1)}, f32[4096]{0:T(1024)}, u32[]{:S(2)}) copy-start(f32[4096]{0:T(1024)} %param.23) | copy-start | bytes 49156

commit v2 on v1

v2 whole, which is shorter than its diff:
```python
import functools
import math

import jax
import jax.numpy as jnp
from jax import lax
from jax.experimental import pallas as pl
from jax.experimental.pallas import tpu as pltpu
from jax.sharding import PartitionSpec as P

HEAD_COUNT = 64
HD = 128
SUB = 128
LANES = 128
LOG2E = math.log2(math.e)
MIB = 1024 * 1024

highest = lax.Precision.HIGHEST
epsilon = 1e-06
f32 = jnp.float32
bf16 = jnp.bfloat16


def dot_nt(left, right, **more):
    return lax.dot_general(
        left, right, (((1,), (1,)), ((), ())), preferred_element_type=f32, **more
    )


def dot_tn(left, right):
    return lax.dot_general(left, right, (((0,), (0,)), ((), ())), preferred_element_type=f32)


def iota(shape, dim):
    return lax.broadcasted_iota(jnp.int32, shape, dim)


def pieces(array, count):
    parts = []
    for _ in range(count):
        part = array.astype(bf16)
        parts.append(part)
        array = array - part.astype(f32)
    return parts


def dot(left, right):
    return jnp.dot(left, right, preferred_element_type=f32)


def pass_kernel(heads, subs, each, length_ref, decay_ref, queries_ref, keys_ref, values_ref, after_ref, mixed_ref, sums_ref, state_ref, fade, lift, keep, total):
    step = pl.program_id(0)
    lower = iota((SUB, SUB), 1) <= iota((SUB, SUB), 0)

    @pl.when(step == 0)
    def _():
        upper = iota((SUB, SUB), 0) <= iota((SUB, SUB), 1)
        upper = upper.astype(f32).astype(bf16)
        earlier = lower.astype(f32).astype(bf16)
        rates, live = [], []
        for sub in range(subs):
            span = slice(sub * SUB, (sub + 1) * SUB)
            alive = sub * SUB + iota((heads, SUB), 1) < length_ref[0]
            rates.append(jnp.where(alive, decay_ref[:, span] * LOG2E, 0.0))
            live.append(alive)
        rates = jnp.concatenate(pieces(jnp.concatenate(rates, axis=0), 3), axis=1)
        row = dot(rates, jnp.concatenate([upper] * 3, axis=0))
        col = dot_nt(jnp.concatenate([earlier] * 3, axis=1), rates)
        half = 0.5 * row[:, SUB - 1 : SUB]
        fall = jnp.exp2(half - row)
        rise = jnp.exp2(col - 0.5 * col[SUB - 1 : SUB, :])
        scale = jnp.exp2(half)
        for sub in range(subs):
            span = slice(sub * heads, (sub + 1) * heads)
            fade[sub] = jnp.where(live[sub], fall[span], 0.0)
            lift[sub, :, :heads] = rise[:, span]
            after = scale[(sub + 1) * heads : (sub + 2) * heads] if sub + 1 < subs else 1.0
            keep[sub] = jnp.broadcast_to(scale[span] * after, (heads, LANES))
        state_ref[...] = jnp.zeros_like(state_ref)

    for index in range(each):
        sub = step * each + index
        rows = slice(index * SUB, (index + 1) * SUB)
        acc = jnp.zeros((SUB, HD), f32)
        for head in range(heads):
            span = slice(head * HD, (head + 1) * HD)
            queries = queries_ref[rows, span]
            values = values_ref[rows, span]
            keys = jnp.transpose(keys_ref[rows, span])
            weight = fade[sub, head : head + 1, :]
            faded = (keys.astype(f32) * weight).astype(bf16)
            scores = jnp.where(lower, dot(queries, keys) * weight, 0.0).astype(bf16)
            state = state_ref[head]
            mixed = dot(
                jnp.concatenate([scores, queries], axis=1),
                jnp.concatenate([values, state.astype(bf16)], axis=0),
            )
            mixed = mixed * lift[sub, :, head : head + 1]
            state_ref[head] = (state + dot(faded, values)) * keep[sub, head : head + 1, :]
            mixed_ref[rows, span] = mixed.astype(bf16)
            acc = acc + mixed * mixed
        total[pl.ds(pl.multiple_of(sub * SUB, SUB), SUB), :] = acc

    @pl.when(step == subs // each - 1)
    def _():
        sums_ref[...] = dot_nt(
            jnp.ones((8, 2 * HD), bf16), jnp.concatenate(pieces(total[...], 2), axis=1)
        )


def prompt_pass(lengths, decay, queries, keys, values, after):
    heads, tokens = decay.shape
    columns = heads * HD
    subs = tokens // SUB
    each = 2
    wide = pl.BlockSpec((SUB * each, columns), lambda b: (b, 0))
    return pl.pallas_call(
        functools.partial(pass_kernel, heads, subs, each),
        grid=(subs // each,),
        in_specs=[
            pl.BlockSpec(memory_space=pltpu.SMEM),
            pl.BlockSpec((heads, tokens), lambda b: (0, 0)),
            wide,
            wide,
            wide,
            pl.BlockSpec(memory_space=pl.ANY),
        ],
        out_specs=[
            wide,
            pl.BlockSpec((8, tokens), lambda b: (0, 0)),
            pl.BlockSpec((heads, HD, HD), lambda b: (0, 0, 0)),
        ],
        out_shape=[
            jax.ShapeDtypeStruct((tokens, columns), bf16),
            jax.ShapeDtypeStruct((8, tokens), f32),
            jax.ShapeDtypeStruct((heads, HD, HD), f32),
        ],
        scratch_shapes=[
            pltpu.VMEM((subs, heads, LANES), f32),
            pltpu.VMEM((subs, SUB, LANES), f32),
            pltpu.VMEM((subs, heads, LANES), f32),
            pltpu.VMEM((tokens, HD), f32),
        ],
        compiler_params=pltpu.CompilerParams(vmem_limit_bytes=48 * MIB),
        cost_estimate=pl.CostEstimate(
            flops=8 * tokens * columns * HD, bytes_accessed=8 * tokens * columns, transcendentals=0
        ),
        name="prompt_pass",
    )(lengths, decay, queries, keys, values, after)


def norm_kernel(width, count, base, length_ref, gain_ref, mixed_ref, *refs):
    block = pl.program_id(0)
    out_ref = refs[-1]
    total = refs[0][...]
    for ref in refs[1:count]:
        total = total + ref[...]
    scale = lax.rsqrt(total * (1.0 / width) + epsilon)
    rows = scale.shape[1]
    scale = jnp.where(base + block * rows + iota(scale.shape, 1) < length_ref[0], scale, 0.0)
    scale = jnp.transpose(scale)[:, :1]
    for column in range(0, gain_ref.shape[1], 512):
        span = slice(column, column + 512)
        out_ref[:, span] = (
            mixed_ref[:, span].astype(f32) * scale * gain_ref[:, span]
        ).astype(bf16)


def prompt_norm(lengths, gain, mixed, sums, base, rows, out, after):
    tokens, columns = mixed.shape
    skip = base // SUB
    spare = pl.BlockSpec(memory_space=pl.ANY)
    more = [after] if out is None else [after, out]
    return pl.pallas_call(
        functools.partial(norm_kernel, HEAD_COUNT * HD, len(sums), base),
        grid=(rows // SUB,),
        in_specs=[
            pl.BlockSpec(memory_space=pltpu.SMEM),
            pl.BlockSpec((1, columns), lambda b: (0, 0)),
            pl.BlockSpec((SUB, columns), lambda b: (b + skip, 0)),
        ]
        + [pl.BlockSpec((8, SUB), lambda b: (0, b + skip))] * len(sums)
        + [spare] * len(more),
        out_specs=pl.BlockSpec((SUB, columns), lambda b: (b + skip, 0)),
        out_shape=jax.ShapeDtypeStruct((tokens, columns), bf16),
        input_output_aliases={} if out is None else {4 + len(sums): 0},
        compiler_params=pltpu.CompilerParams(vmem_limit_bytes=12 * MIB),
        cost_estimate=pl.CostEstimate(
            flops=3 * rows * columns, bytes_accessed=4 * rows * columns, transcendentals=0
        ),
        name="prompt_norm",
    )(lengths, gain, mixed, *sums, *more)


def read_kernel(heads, count, *refs):
    state_ref = refs[count]
    outs = refs[count + 1 :]
    rows = refs[0].shape[0]
    for head in range(heads):
        span = slice(head * HD, (head + 1) * HD)
        high, low = pieces(state_ref[head], 2)
        queries = jnp.concatenate([ref[:, span].astype(f32) for ref in refs[:count]], axis=0)
        queries = queries.astype(bf16)
        read = dot(
            jnp.concatenate([queries, queries], axis=1), jnp.concatenate([high, low], axis=0)
        )
        for index, out in enumerate(outs):
            out[:, span] = read[index * rows : (index + 1) * rows].astype(bf16)


def read_states(queries, state):
    heads = state.shape[0]
    count = len(queries)
    rows = queries[0].shape[0]
    group = min(8, heads)
    part = pl.BlockSpec((rows, group * HD), lambda g: (0, g))
    return pl.pallas_call(
        functools.partial(read_kernel, group, count),
        grid=(heads // group,),
        in_specs=[part] * count + [pl.BlockSpec((group, HD, HD), lambda g: (g, 0, 0))],
        out_specs=[part] * count,
        out_shape=[jax.ShapeDtypeStruct((rows, heads * HD), bf16)] * count,
        compiler_params=pltpu.CompilerParams(vmem_limit_bytes=12 * MIB),
        cost_estimate=pl.CostEstimate(
            flops=4 * count * rows * heads * HD * HD,
            bytes_accessed=4 * state.size + 4 * count * rows * heads * HD,
            transcendentals=0,
        ),
        name="read_states",
    )(*queries, state)


def rank_of(owner_ref, prompt):
    owner = owner_ref[prompt]
    rank = jnp.int32(0)
    for other in range(owner_ref.shape[0]):
        rank = rank + jnp.where((owner_ref[other] == owner) & (other < prompt), 1, 0)
    return owner, rank


def prompts_of(owner_ref, owner, slots):
    found = [jnp.int32(0)] * slots
    seen = jnp.int32(0)
    for prompt in range(owner_ref.shape[0]):
        mine = owner_ref[prompt] == owner
        found = [
            jnp.where(mine & (seen == slot), prompt, one) for slot, one in enumerate(found)
        ]
        seen = seen + jnp.where(mine, 1, 0)
    return found


def copy_one(choice, pool, write):
    for index, take in enumerate(pool):

        @pl.when(choice == index)
        def _(take=take):
            write(take())


def ask_kernel(near, owner_ref, place_ref, *refs):
    pool, out_ref = refs[:near], refs[near]
    group, block = place_ref[0], place_ref[1]
    count = out_ref.shape[0]
    for bit in range(count):
        owner, rank = rank_of(owner_ref, (group ^ near) * count + (block ^ bit))
        offset = owner ^ group

        def write(value, bit=bit):
            out_ref[bit] = value

        copy_one(offset, [lambda ref=ref, rank=rank: ref[rank] for ref in pool], write)


def ask(owner, place, pool, count):
    whole = pl.BlockSpec(memory_space=pltpu.VMEM)
    scalar = pl.BlockSpec(memory_space=pltpu.SMEM)
    return pl.pallas_call(
        functools.partial(ask_kernel, len(pool)),
        in_specs=[scalar, scalar] + [whole] * len(pool),
        out_specs=whole,
        out_shape=jax.ShapeDtypeStruct((count,) + pool[0].shape[1:], bf16),
        compiler_params=pltpu.CompilerParams(vmem_limit_bytes=8 * MIB),
        name="ask",
    )(owner, place, *pool)


def one_hot(mask):
    return mask.astype(f32).astype(bf16)


def parcel_kernel(near, slots, capacity, owner_ref, place_ref, parent_ref, *refs):
    pool, (came_ref, keys_ref, values_ref) = refs[:near], refs[near : near + 3]
    outs = refs[near + 3 :]
    group, block = place_ref[0], place_ref[1]
    count = len(outs)
    rows, columns = outs[0].shape
    per_block = rows // 2
    halves = rows // (2 * capacity)
    split = columns // halves
    lines = slots * rows
    for bit, out in enumerate(outs):
        owner, rank = rank_of(owner_ref, group * count + (block ^ bit))
        choice = jnp.minimum(owner ^ group, near)

        def write(value, out=out):
            out[:, :columns] = value

        copy_one(
            choice,
            [lambda ref=ref, rank=rank: ref[rank] for ref in pool]
            + [lambda bit=bit: came_ref[bit]],
            write,
        )
        if bit == 0:
            continue
        target = block ^ bit
        seen = jnp.int32(0)
        sources = [jnp.int32(0)] * capacity
        for slot in range(slots):
            for beam in range(per_block):
                parent = parent_ref[slot, target * per_block + beam]
                hit = lax.div(parent, per_block) == block
                row = slot * rows + parent - block * per_block
                sources = [
                    jnp.where(hit & (seen == index), row, one)
                    for index, one in enumerate(sources)
                ]
                seen = seen + jnp.where(hit, 1, 0)
        line, source = iota((rows, lines), 0), iota((rows, lines), 1)
        parcel = jnp.zeros((rows, split), f32)
        for half in range(halves):
            span = slice(half * split, (half + 1) * split)
            first = half * 2 * capacity
            for kind, ref in enumerate((keys_ref, values_ref)):
                mask = (line == first + kind * capacity) & (source == sources[0])
                for index in range(1, capacity):
                    mask = mask | (
                        (line == first + kind * capacity + index) & (source == sources[index])
                    )
                parcel = parcel + dot(one_hot(mask), ref[:, span])
        out[:, columns:] = parcel.astype(bf16)


def parcels(owner, place, parents, pool, came, keys, values, capacity):
    whole = pl.BlockSpec(memory_space=pltpu.VMEM)
    scalar = pl.BlockSpec(memory_space=pltpu.SMEM)
    count, rows, columns = came.shape
    wide = columns + columns * 2 * capacity // rows
    return pl.pallas_call(
        functools.partial(parcel_kernel, len(pool), parents.shape[0], capacity),
        in_specs=[scalar] * 3 + [whole] * (len(pool) + 3),
        out_specs=[whole] * count,
        out_shape=[
            jax.ShapeDtypeStruct((rows, wide if bit else columns), bf16) for bit in range(count)
        ],
        compiler_params=pltpu.CompilerParams(vmem_limit_bytes=12 * MIB),
        name="parcels",
    )(owner, place, parents, *pool, came, keys, values)


def reply_kernel(near, owner_ref, place_ref, *refs):
    pool, out_ref = refs[:-1], refs[-1]
    group, block = place_ref[0], place_ref[1]
    count = len(pool) // near
    for slot, prompt in enumerate(prompts_of(owner_ref, group ^ near, out_ref.shape[0])):
        offset = lax.div(prompt, count) ^ group
        choice = offset * count + (lax.rem(prompt, count) ^ block)

        def write(value, slot=slot):
            out_ref[slot] = value

        copy_one(choice, [lambda ref=ref: ref[...] for ref in pool], write)


def reply(owner, place, pool, near, slots):
    whole = pl.BlockSpec(memory_space=pltpu.VMEM)
    scalar = pl.BlockSpec(memory_space=pltpu.SMEM)
    return pl.pallas_call(
        functools.partial(reply_kernel, near),
        in_specs=[scalar, scalar] + [whole] * len(pool),
        out_specs=whole,
        out_shape=jax.ShapeDtypeStruct((slots,) + pool[0].shape, bf16),
        compiler_params=pltpu.CompilerParams(vmem_limit_bytes=8 * MIB),
        name="reply",
    )(owner, place, *pool)


def terms_kernel(slots, capacity, count, place_ref, parent_ref, decay_ref, queries_ref, keys_ref, values_ref, *refs):
    far = refs[:count]
    terms_ref, first_ref, second, parent_keys, parent_values = refs[count + 1 :]
    block = place_ref[1]
    lines, columns = queries_ref.shape
    heads = columns // HD
    rows = lines // slots
    per_block = rows // 2
    halves = rows // (2 * capacity)
    split = columns // halves
    line = iota((lines, LANES), 0)
    near_col = jnp.full((lines, LANES), -1, jnp.int32)
    far_col = jnp.full((lines, LANES), -1, jnp.int32)
    sources = []
    for slot in range(slots):
        for beam in range(per_block):
            parent = parent_ref[slot, block * per_block + beam]
            source = lax.div(parent, per_block)
            rank = jnp.int32(0)
            for other in sources:
                rank = rank + jnp.where(other == source, 1, 0)
            sources.append(source)
            away = source ^ block
            near_at = slot * rows + parent - source * per_block
            near_at = jnp.where(away == 0, near_at, -1)
            far_at = jnp.where(away == 0, -1, (away - 1) * rows + rank)
            here = line == slot * rows + per_block + beam
            near_col = jnp.where(here, near_at, near_col)
            far_col = jnp.where(here, far_at, far_col)
            own = block * per_block + beam
            now = slot * rows + beam
            then = now + per_block
            step_one = decay_ref[1, slot, pl.ds(own, 1), :]
            first_ref[now : now + 1, :] = decay_ref[0, slot, pl.ds(own, 1), :]
            first_ref[then : then + 1, :] = step_one + decay_ref[0, slot, pl.ds(parent, 1), :]
            second[now : now + 1, :] = jnp.full_like(step_one, -1e30)
            second[then : then + 1, :] = step_one
    first_ref[...] = jnp.exp(first_ref[...])
    second[...] = jnp.exp(second[...])
    own_hot = one_hot(iota((lines, lines), 1) == near_col[:, :lines])
    column = iota((lines, rows), 1)
    for half in range(halves):
        span = slice(half * split, (half + 1) * split)
        for kind, (ref, store) in enumerate(
            ((keys_ref, parent_keys), (values_ref, parent_values))
        ):
            picked = dot(own_hot, ref[:, span])
            for index, message in enumerate(far):
                low, high = half * 2 * capacity, kind * capacity
                hot = (column == far_col[:, :rows] - index * rows + low + high) & (
                    (far_col[:, :rows] >= index * rows)
                    & (far_col[:, :rows] < index * rows + capacity)
                )
                picked = picked + dot(one_hot(hot), message[:, columns:])
            store[:, span] = picked
    for head in range(heads):
        span = slice(head * HD, (head + 1) * HD)
        queries = queries_ref[:, span].astype(f32)
        own = jnp.sum(queries * keys_ref[:, span].astype(f32), axis=1, keepdims=True)
        parent = jnp.sum(queries * parent_keys[:, span], axis=1, keepdims=True)
        terms_ref[:, span] = own * values_ref[:, span].astype(f32) + (
            second[:, head : head + 1] * parent
        ) * parent_values[:, span]


def step_terms(place, parents, decay, queries, keys, values, far, capacity, after):
    lines, columns = queries.shape
    heads = columns // HD
    whole = pl.BlockSpec(memory_space=pltpu.VMEM)
    scalar = pl.BlockSpec(memory_space=pltpu.SMEM)
    return pl.pallas_call(
        functools.partial(terms_kernel, parents.shape[0], capacity, len(far)),
        in_specs=[scalar] * 2
        + [whole] * (4 + len(far))
        + [pl.BlockSpec(memory_space=pl.ANY)],
        out_shape=[
            jax.ShapeDtypeStruct((lines, columns), f32),
            jax.ShapeDtypeStruct((lines, heads), f32),
        ],
        scratch_shapes=[
            pltpu.VMEM((lines, heads), f32),
            pltpu.VMEM((lines, columns), f32),
            pltpu.VMEM((lines, columns), f32),
        ],
        compiler_params=pltpu.CompilerParams(vmem_limit_bytes=12 * MIB),
        name="step_terms",
    )(place, parents, decay, queries, keys, values, *far, after)


def steps_kernel(heads, near, owner_ref, place_ref, *refs):
    pool = refs[:-5]
    came_ref, terms_ref, first_ref, mixed_ref, sums_ref = refs[-5:]
    group, block = place_ref[0], place_ref[1]
    count = len(pool) // near
    slots, rows = came_ref.shape[:2]
    for slot, prompt in enumerate(prompts_of(owner_ref, group, slots)):
        offset = lax.div(prompt, count) ^ group
        choice = offset * count + (lax.rem(prompt, count) ^ block)
        lines = slice(slot * rows, (slot + 1) * rows)
        total = jnp.zeros((rows, HD), f32)
        for head in range(heads):
            span = slice(head * HD, (head + 1) * HD)
            read = came_ref[slot, :, span].astype(f32)
            for index in range(len(pool)):
                read = jnp.where(choice == index, pool[index][:, span].astype(f32), read)
            mixed = first_ref[lines, head : head + 1] * read + terms_ref[lines, span]
            mixed_ref[lines, span] = mixed
            total = total + mixed * mixed
        sums_ref[lines, :] = jnp.broadcast_to(
            jnp.sum(total, axis=1, keepdims=True), (rows, LANES)
        )


def steps_mix(owner, place, pool, near, came, terms, first):
    lines, columns = terms.shape
    whole = pl.BlockSpec(memory_space=pltpu.VMEM)
    scalar = pl.BlockSpec(memory_space=pltpu.SMEM)
    return pl.pallas_call(
        functools.partial(steps_kernel, columns // HD, near),
        in_specs=[scalar, scalar] + [whole] * (len(pool) + 3),
        out_shape=[
            jax.ShapeDtypeStruct((lines, columns), f32),
            jax.ShapeDtypeStruct((lines, LANES), f32),
        ],
        compiler_params=pltpu.CompilerParams(vmem_limit_bytes=12 * MIB),
        name="steps_mix",
    )(owner, place, *pool, came, terms, first)


def swap(array, axis, bit):
    size = lax.axis_size(axis)
    return lax.ppermute(array, axis, [(index, index ^ bit) for index in range(size)])


def over_pre(array):
    size = lax.axis_size("pre")
    return [array] + [swap(array, "pre", bit) for bit in range(1, size)]


def local(
    prompt_queries,
    prompt_keys,
    prompt_values,
    prompt_decay,
    prompt_lengths,
    norm_gain,
    decode_owner,
    parent_beam,
    step_queries,
    step_keys,
    step_values,
    step_decay,
):
    tokens, columns = prompt_queries.shape[1:]
    heads = prompt_decay.shape[1]
    steps, slots, per_block = step_queries.shape[:3]
    rows = steps * per_block
    group, block = lax.axis_index("grp"), lax.axis_index("dec")
    group_count, block_count = lax.axis_size("grp"), lax.axis_size("dec")
    near = group_count // 2

    def slot_major(array):
        return jnp.swapaxes(array, 0, 1).reshape(slots, rows, columns)

    def widen(pool):
        bit = 1
        while bit < near:
            pool = pool + [swap(one, "grp", bit) for one in pool]
            bit *= 2
        return pool

    place = jnp.stack([group, block]).astype(jnp.int32)
    capacity = (slots + block_count - 2) // (block_count - 1)

    queries = slot_major(step_queries)
    asked = widen([queries])
    sent = ask(decode_owner, place, asked, block_count)
    came = swap(sent, "grp", near)
    mixed, sums, state = prompt_pass(
        prompt_lengths, prompt_decay[0], prompt_queries[0], prompt_keys[0], prompt_values[0], sent
    )
    came, step_keys, step_values, sums = lax.optimization_barrier(
        (came, step_keys, step_values, sums)
    )
    queries = queries.reshape(slots * rows, columns)
    keys = slot_major(step_keys).reshape(slots * rows, columns)
    values = slot_major(step_values).reshape(slots * rows, columns)

    messages = parcels(
        decode_owner, place, parent_beam, asked, came, keys, values, capacity
    )
    far = [swap(messages[bit], "dec", bit) for bit in range(1, block_count)]
    squares = over_pre(sums)
    share = tokens // 2
    prompt_out = prompt_norm(
        prompt_lengths, norm_gain[None], mixed, squares, 0, share, None, messages[-1]
    )
    state, prompt_out = lax.optimization_barrier((state, prompt_out))
    reads = read_states([messages[0]] + far, state)
    prompt_out = prompt_norm(
        prompt_lengths, norm_gain[None], mixed, squares, share, share, prompt_out, reads[-1]
    )
    reads = [reads[0]] + [swap(reads[bit], "dec", bit) for bit in range(1, block_count)]
    reads, prompt_out = lax.optimization_barrier((reads, prompt_out))
    pool = widen(reads)
    sent = reply(decode_owner, place, pool, near, slots)
    came = swap(sent, "grp", near)
    terms, first = step_terms(
        place, parent_beam, step_decay, queries, keys, values, far, capacity, sent
    )
    step_mixed, step_sums = steps_mix(decode_owner, place, pool, near, came, terms, first)
    step_total = functools.reduce(jnp.add, over_pre(step_sums[:, :1]))
    scale = lax.rsqrt(step_total / (HEAD_COUNT * HD) + epsilon)
    step_out = (step_mixed * scale * norm_gain).astype(bf16)
    step_out = jnp.swapaxes(step_out.reshape(slots, steps, per_block, columns), 0, 1)
    return (prompt_out[None], step_out)


def solution(mesh):
    in_specs = (
        P(("grp", "dec"), None, "pre"),
        P(("grp", "dec"), None, "pre"),
        P(("grp", "dec"), None, "pre"),
        P(("grp", "dec"), "pre", None),
        P(("grp", "dec")),
        P("pre"),
        P(),
        P("grp", None),
        P(None, "grp", "dec", "pre"),
        P(None, "grp", "dec", "pre"),
        P(None, "grp", "dec", "pre"),
        P(None, "grp", None, "pre"),
    )
    out_specs = (P(("grp", "dec"), None, "pre"), P(None, "grp", "dec", "pre"))
    return jax.shard_map(local, mesh=mesh, in_specs=in_specs, out_specs=out_specs, check_vma=False)
```

time: 122 us -> 75.5 us (0.62)
  Pallas kernels: 58.9 us -> 33.6 us
  local copies, waits for them, and re-layouts: 19.6 us -> 9.97 us
  waiting for transfers between devices: 21.4 us -> 12.9 us
  other arithmetic: 4.01 us -> 0.32 us
  starting transfers between devices: 15.7 us -> 17 us
    pallas_call x5 -> x9, Pallas kernels: 58.9 us -> 33.6 us  [the longest x1 18.6 us: prompt_pass(): pl.pallas_call(functools.partial(pass_kernel, heads, subs, each), grid=(s...]
    gather x17 -> x0, local copies, waits for them, and re-layouts: 8.62 us -> none  [the longest x2 1.28 us: local(): spot, here = place(decode_owner[mine], rank[mine], slots)]
    ppermute x12 -> x15, waiting for transfers between devices: 21.4 us -> 12.9 us  [swap(): lax.ppermute(array, axis, [(index, index ^ bit) for index in range(size)])]
    unnamed x28 -> x22, local copies, waits for them, and re-layouts: 1.54 us -> 4.97 us
    reshape x7 -> x0, local copies, waits for them, and re-layouts: 2.46 us -> none  [the longest x3 2.18 us: second_rows(): jnp.pad(array, ((0, 0), (per_block, 0), (0, 0))).reshape(slots * rows, -1)]
    slice x12 -> x0, local copies, waits for them, and re-layouts: 2.05 us -> none  [the longest x3 1.87 us: local(): query_parts.append(message[:, :columns])]
    transpose x4 -> x3, local copies, waits for them, and re-layouts: 1.44 us -> 2.88 us  [slot_major(): return jnp.swapaxes(array, 0, 1).reshape(slots, rows, columns)]
    ppermute x12 -> x15, starting transfers between devices: 15.7 us -> 17 us  [swap(): lax.ppermute(array, axis, [(index, index ^ bit) for index in range(size)])]
  transfers between devices with their start and end apart: 12 -> 15, of which waited for: 7 -> 10; matrix products, arithmetic and copies ran while one was open for 17% -> 0% of each run, Pallas kernels for 48% -> 38%
where the time goes in v2:
time: 75.5 us; the launch traced here: 75.2 us
  Pallas kernels  33.6 us (45%)
  starting transfers between devices  17 us (23%)
  waiting for transfers between devices  12.9 us (17%)
  local copies, waits for them, and re-layouts  9.97 us (13%)
  between operations  1.44 us (2%)
    pallas_call x1, Pallas kernels, prompt_pass(): pl.pallas_call(functools.partial(pass_kernel, heads, subs, each), grid=(s...  18.6 us
    ppermute x15, starting transfers between devices, swap(): lax.ppermute(array, axis, [(index, index ^ bit) for index in range(size)])  17 us
    ppermute x15, waiting for transfers between devices, swap(): lax.ppermute(array, axis, [(index, index ^ bit) for index in range(size)])  12.9 us
    pallas_call x2, Pallas kernels, prompt_norm(): pl.pallas_call(functools.partial(norm_kernel, HEAD_COUNT * HD, len(sums),...  6.24 us
    unnamed x22, local copies, waits for them, and re-layouts  4.97 us
    pallas_call x1, Pallas kernels, step_terms(): pl.pallas_call(functools.partial(terms_kernel, parents.shape[0], capacity...  3.85 us
    transpose x3, local copies, waits for them, and re-layouts, slot_major(): return jnp.swapaxes(array, 0, 1).reshape(slots, rows, columns)  2.88 us
    pallas_call x1, Pallas kernels, parcels(): pl.pallas_call(functools.partial(parcel_kernel, len(pool), parents.shape[...  1.55 us
  transfers between devices with their start and end apart: 15, of which 10 were waited for; matrix products, arithmetic and copies ran while one was open for 0% of the time, Pallas kernels for 38%

profile of v2, /device:TPU:0, one launch (start us, length us, event | category | flops | bytes accessed | tf_op | source)
XLA Modules:
  0.0 75.2 jit_solution(7457702156468199282)
XLA Ops:
  0.6 1.0 %copy.20 = bf16[4,2,4,4096]{3,2,1,0:T(4,128)(2,1)S(1)} copy(bf16[4,2,4,4096]{3,2,0,1:T(4,128)(2,1)} %bitcast.23) | data formatting | bytes 524288 | tf_op jit(solution)/shard_map/transpose | solution.py:551
  1.8 0.5 collective-permute-start
  3.0 0.4 collective-permute-done.refs_1_
  3.4 0.7 copy-done.6
  4.1 0.7 ask.1.after_ref
  4.8 3.0 %collective-permute-start.1 = (bf16[4,8,4096]{2,1,0:T(8,128)(2,1)S(1)}, bf16[4,8,4096]{2,1,0:T(8,128)(2,1)S(1)}, u32[]{:S(2)}, u32[]{:S(2)}) collective-permute-start(bf16[4,8,4096]{2,1,0:T(8,128)(2,1)S(1)} %ask.1.after_ref), channel_id=1, source_target_pairs={{0,8},{4,12},{8,0},{12,4},{1,9},{5,13},{9,1},{13,5},{2,10},{6,14},... | collective-permute-start | bytes 786440 | tf_op jit(solution)/shard_map/ppermute | solution.py:520
  7.8 0.9 %copy-done.3 = f32[1,32,1024]{2,1,0:T(8,128)S(1)} copy-done((f32[1,32,1024]{2,1,0:T(8,128)S(1)}, f32[1,32,1024]{2,1,0:T(8,128)}, u32[]{:S(2)}) %copy-start.3) | copy-done | bytes 131096
  8.7 18.6 %prompt_pass.1 = (bf16[1024,4096]{1,0:T(8,128)(2,1)}, f32[8,1024]{1,0:T(8,128)S(1)}, f32[32,128,128]{2,1,0:T(8,128)S(1)}) custom-call(s32[1]{0:T(128)S(6)} %copy.28.length_ref, f32[32,1024]{1,0:T(8,128)S(1)} %bitcast.17, bf16[1024,4096]{1,0:T(8,128)(2,1)} %bitcast.20, bf16[1024,4096]{1,0:T(8,128)(2,1)} %bitcast.21, bf16[1024,4096]{1,0:T(8,128)(2,1)} %bitcast.22, ...), custom_call_target="tpu_custom_call" | custom-call | flops 4294967296 | bytes 33554432 | tf_op jit(solution)/shard_map/prompt_pass/pallas_call | solution.py:117
  27.4 1.7 %copy.22 = bf16[4,2,4,4096]{3,2,1,0:T(4,128)(2,1)} copy(bf16[4,2,4,4096]{3,2,0,1:T(4,128)(2,1)} %bitcast.25) | data formatting | bytes 524288 | tf_op jit(solution)/shard_map/transpose | solution.py:551
  29.2 1.0 %reshape_reshape.10.refs_4_.values_ref = bf16[32,4096]{1,0:T(8,128)(2,1)S(1)} reshape(bf16[4,2,4,4096]{3,2,1,0:T(4,128)(2,1)} %copy.22) | data formatting | bytes 524288 | tf_op jit(solution)/shard_map/reshape;reshape | solution.py:575
  30.2 1.6 %parcels.1 = (bf16[8,4096]{1,0:T(8,128)(2,1)S(1)}, bf16[8,6144]{1,0:T(8,128)(2,1)S(1)}, bf16[8,6144]{1,0:T(8,128)(2,1)S(1)}, bf16[8,6144]{1,0:T(8,128)(2,1)S(1)}) custom-call(s32[16]{0:T(128)S(1)} %copy-done.7, s32[2]{0:T(128)S(1)} %pad_add_fusion.place_ref, s32[4,16]{1,0:T(4,128)S(1)} %copy-done.5, bf16[4,8,4096]{2,1,0:T(8,128)(2,1)S(1)} %reshape.11.refs_0_, ...), custom_call_target="tpu_custom_call" | custom-call | tf_op jit(solution)/shard_map/parcels/pallas_call | solution.py:350
  31.8 1.6 %collective-permute-start.2 = (bf16[8,6144]{1,0:T(8,128)(2,1)S(1)}, bf16[8,6144]{1,0:T(8,128)(2,1)S(1)}, u32[]{:S(2)}, u32[]{:S(2)}) collective-permute-start(bf16[8,6144]{1,0:T(8,128)(2,1)S(1)} %get-tuple-element.33), channel_id=1, source_target_pairs={{0,1},{1,0},{2,3},{3,2},{4,5},{5,4},{6,7},{7,6},{8,9},{9,8},{10,11... | collective-permute-start | bytes 294920 | tf_op jit(solution)/shard_map/ppermute | solution.py:520
  33.4 2.6 %collective-permute-start.3 = (bf16[8,6144]{1,0:T(8,128)(2,1)S(1)}, bf16[8,6144]{1,0:T(8,128)(2,1)S(1)}, u32[]{:S(2)}, u32[]{:S(2)}) collective-permute-start(bf16[8,6144]{1,0:T(8,128)(2,1)S(1)} %get-tuple-element.34), channel_id=1, source_target_pairs={{0,2},{1,3},{2,0},{3,1},{4,6},{5,7},{6,4},{7,5},{8,10},{9,11},{10,... | collective-permute-start | bytes 294920 | tf_op jit(solution)/shard_map/ppermute | solution.py:520
  36.2 1.5 %collective-permute-start.5 = (f32[8,1024]{1,0:T(8,128)S(1)}, f32[8,1024]{1,0:T(8,128)S(1)}, u32[]{:S(2)}, u32[]{:S(2)}) collective-permute-start(f32[8,1024]{1,0:T(8,128)S(1)} %get-tuple-element.38.refs_0_), channel_id=1, source_target_pairs={{0,16},{16,0},{1,17},{17,1},{2,18},{18,2},{3,19},{19,3},{4,20},{20... | collective-permute-start | bytes 98312 | tf_op jit(solution)/shard_map/ppermute | solution.py:520
  37.7 2.4 %collective-permute-done.5.refs_1_ = f32[8,1024]{1,0:T(8,128)S(1)} collective-permute-done((f32[8,1024]{1,0:T(8,128)S(1)}, f32[8,1024]{1,0:T(8,128)S(1)}, u32[]{:S(2)}, u32[]{:S(2)}) %collective-permute-start.5) | collective-permute-done | bytes 32800 | tf_op jit(solution)/shard_map/ppermute | solution.py:520
  40.1 3.4 %copy-done = bf16[1024,4096]{1,0:T(8,128)(2,1)S(1)} copy-done((bf16[1024,4096]{1,0:T(8,128)(2,1)S(1)}, bf16[1024,4096]{1,0:T(8,128)(2,1)}, u32[]{:S(2)}) %copy-start) | copy-done | bytes 8388632
  43.5 3.1 %prompt_norm.2.refs_3_ = bf16[1024,4096]{1,0:T(8,128)(2,1)} custom-call(s32[1]{0:T(128)S(6)} %copy.28.length_ref, f32[1,4096]{1,0:T(1,128)S(1)} %bitcast.15, bf16[1024,4096]{1,0:T(8,128)(2,1)S(1)} %copy-done, f32[8,1024]{1,0:T(8,128)S(1)} %get-tuple-element.38.refs_0_, f32[8,1024]{1,0:T(8,128)S(1)} %collective-permute-done.5.refs_1_, ...), custom_call_target="tpu_custom_call" | custom-call | flops 6291456 | bytes 8388608 | tf_op jit(solution)/shard_map/prompt_norm/pallas_call | solution.py:174
  46.7 0.9 %read_states.1 = (bf16[8,4096]{1,0:T(8,128)(2,1)S(1)}, bf16[8,4096]{1,0:T(8,128)(2,1)S(1)}, bf16[8,4096]{1,0:T(8,128)(2,1)S(1)}, bf16[8,4096]{1,0:T(8,128)(2,1)S(1)}) custom-call(bf16[8,4096]{1,0:T(8,128)(2,1)S(1)} %get-tuple-element.32.refs_0_, bf16[8,6144]{1,0:T(8,128)(2,1)S(1)} %collective-permute-done.2.refs_1_.refs_0_, ...), custom_call_target="tpu_custom_call" | custom-call | flops 67108864 | bytes 2621440 | tf_op jit(solution)/shard_map/read_states/pallas_call | solution.py:217
  47.6 0.7 collective-permute-start.6
  48.3 3.5 %collective-permute-start.7 = (bf16[8,4096]{1,0:T(8,128)(2,1)S(1)}, bf16[8,4096]{1,0:T(8,128)(2,1)S(1)}, u32[]{:S(2)}, u32[]{:S(2)}) collective-permute-start(bf16[8,4096]{1,0:T(8,128)(2,1)S(1)} %get-tuple-element.42), channel_id=1, source_target_pairs={{0,2},{1,3},{2,0},{3,1},{4,6},{5,7},{6,4},{7,5},{8,10},{9,11},{10,... | collective-permute-start | bytes 196616 | tf_op jit(solution)/shard_map/ppermute | solution.py:520
  52.0 3.1 %prompt_norm.3 = bf16[1024,4096]{1,0:T(8,128)(2,1)} custom-call(s32[1]{0:T(128)S(6)} %copy.28.length_ref, f32[1,4096]{1,0:T(1,128)S(1)} %bitcast.16, bf16[1024,4096]{1,0:T(8,128)(2,1)S(1)} %copy-done.1, f32[8,1024]{1,0:T(8,128)S(1)} %get-tuple-element.38.refs_0_, f32[8,1024]{1,0:T(8,128)S(1)} %collective-permute-done.5.refs_1_, ...), custom_call_target="tpu_custom_call", output_to_operand_aliasing={{}: (6, {})} | custom-call | flops 6291456 | bytes 8388608 | tf_op jit(solution)/shard_map/prompt_norm/pallas_call | solution.py:174
  55.4 2.4 %collective-permute-done.8.refs_3_ = bf16[8,4096]{1,0:T(8,128)(2,1)S(1)} collective-permute-done((bf16[8,4096]{1,0:T(8,128)(2,1)S(1)}, bf16[8,4096]{1,0:T(8,128)(2,1)S(1)}, u32[]{:S(2)}, u32[]{:S(2)}) %collective-permute-start.8) | collective-permute-done | bytes 65568 | tf_op jit(solution)/shard_map/ppermute | solution.py:520
  57.9 0.5 collective-permute-start.10
  58.4 0.5 collective-permute-start.12
  59.8 0.8 %reply.1.refs_3_ = bf16[4,8,4096]{2,1,0:T(8,128)(2,1)S(1)} custom-call(s32[16]{0:T(128)S(1)} %copy-done.7, s32[2]{0:T(128)S(1)} %pad_add_fusion.place_ref, bf16[8,4096]{1,0:T(8,128)(2,1)S(1)} %get-tuple-element.46.refs_0_, bf16[8,4096]{1,0:T(8,128)(2,1)S(1)} %collective-permute-done.6.refs_1_, bf16[8,4096]{1,0:T(8,128)(2,1)S(1)} %collective-permute-done.7.refs_2_, ...), custom_call_target="tpu_custom_call" | custom-call | tf_op jit(solution)/shard_map/reply/pallas_call | solution.py:379
  60.6 0.6 collective-permute-start.13
  61.2 3.8 %step_terms.1 = (f32[32,4096]{1,0:T(8,128)S(1)}, f32[32,32]{1,0:T(8,128)S(1)}) custom-call(s32[2]{0:T(128)S(1)} %pad_add_fusion.place_ref, s32[4,16]{1,0:T(4,128)S(1)} %copy-done.5, f32[2,4,16,32]{3,2,1,0:T(8,128)S(1)} %copy-done.4, bf16[32,4096]{1,0:T(8,128)(2,1)S(1)} %reshape_reshape.11.queries_ref, bf16[32,4096]{1,0:T(8,128)(2,1)S(1)} %reshape_reshape.9.refs_3_.keys_ref, ...), custom_call_target="tpu_custom_call" | custom-call | tf_op jit(solution)/shard_map/step_terms/pallas_call | solution.py:459
  65.1 4.1 %collective-permute-done.13.refs_8_ = bf16[4,8,4096]{2,1,0:T(8,128)(2,1)S(1)} collective-permute-done((bf16[4,8,4096]{2,1,0:T(8,128)(2,1)S(1)}, bf16[4,8,4096]{2,1,0:T(8,128)(2,1)S(1)}, u32[]{:S(2)}, u32[]{:S(2)}) %collective-permute-start.13) | collective-permute-done | bytes 262176 | tf_op jit(solution)/shard_map/ppermute | solution.py:520
  69.2 1.1 %steps_mix.1 = (f32[32,4096]{1,0:T(8,128)S(1)}, f32[32,128]{1,0:T(8,128)S(1)}) custom-call(s32[16]{0:T(128)S(1)} %copy-done.7, s32[2]{0:T(128)S(1)} %pad_add_fusion.place_ref, bf16[8,4096]{1,0:T(8,128)(2,1)S(1)} %get-tuple-element.46.refs_0_, bf16[8,4096]{1,0:T(8,128)(2,1)S(1)} %collective-permute-done.6.refs_1_, ...), custom_call_target="tpu_custom_call" | custom-call | tf_op jit(solution)/shard_map/steps_mix/pallas_call | solution.py:506
  70.3 1.5 %collective-permute-start.14 = (f32[32,1]{1,0:T(8,128)S(1)}, f32[32,1]{1,0:T(8,128)S(1)}, u32[]{:S(2)}, u32[]{:S(2)}) collective-permute-start(f32[32,1]{1,0:T(8,128)S(1)} %bitcast.18), channel_id=1, source_target_pairs={{0,16},{16,0},{1,17},{17,1},{2,18},{18,2},{3,19},{19,3},{4,20},{20... | collective-permute-start | bytes 392 | tf_op jit(solution)/shard_map/ppermute | solution.py:520
  71.8 2.2 %collective-permute-done.14 = f32[32,1]{1,0:T(8,128)S(1)} collective-permute-done((f32[32,1]{1,0:T(8,128)S(1)}, f32[32,1]{1,0:T(8,128)S(1)}, u32[]{:S(2)}, u32[]{:S(2)}) %collective-permute-start.14) | collective-permute-done | bytes 160 | tf_op jit(solution)/shard_map/ppermute | solution.py:520
  74.4 0.8 %copy.26 = bf16[4,2,4,4096]{3,2,0,1:T(4,128)(2,1)} copy(bf16[4,2,4,4096]{3,2,1,0:T(4,128)(2,1)S(1)} %reshape.12) | data formatting | bytes 524288 | tf_op jit(solution)/shard_map/reshape | solution.py:603
  (41 shorter events, 2.4 us)
Async XLA Ops:
  1.7 25.6 %copy-start.8 = (bf16[4,2,4,4096]{3,2,1,0:T(4,128)(2,1)}, bf16[4,2,4,4096]{3,2,1,0:T(4,128)(2,1)S(1)}, u32[]{:S(2)}) copy-start(bf16[4,2,4,4096]{3,2,1,0:T(4,128)(2,1)S(1)} %copy.20) | copy-start | bytes 786436
  1.8 1.7 %collective-permute-start = (bf16[4,8,4096]{2,1,0:T(8,128)(2,1)S(1)}, bf16[4,8,4096]{2,1,0:T(8,128)(2,1)S(1)}, u32[]{:S(2)}, u32[]{:S(2)}) collective-permute-start(bf16[4,8,4096]{2,1,0:T(8,128)(2,1)S(1)} %reshape.11.refs_0_), channel_id=1, source_target_pairs={{0,4},{4,0},{8,12},{12,8},{1,5},{5,1},{9,13},{13,9},{2,6},{6,2},{1... | collective-permute-start | bytes 786440 | tf_op jit(solution)/shard_map/ppermute | solution.py:520
  3.4 0.7 copy-start.6
  4.8 22.4 %collective-permute-start.1 = (bf16[4,8,4096]{2,1,0:T(8,128)(2,1)S(1)}, bf16[4,8,4096]{2,1,0:T(8,128)(2,1)S(1)}, u32[]{:S(2)}, u32[]{:S(2)}) collective-permute-start(bf16[4,8,4096]{2,1,0:T(8,128)(2,1)S(1)} %ask.1.after_ref), channel_id=1, source_target_pairs={{0,8},{4,12},{8,0},{12,4},{1,9},{5,13},{9,1},{13,5},{2,10},{6,14},... | collective-permute-start | bytes 786440 | tf_op jit(solution)/shard_map/ppermute | solution.py:520
  7.8 0.9 %copy-start.3 = (f32[1,32,1024]{2,1,0:T(8,128)S(1)}, f32[1,32,1024]{2,1,0:T(8,128)}, u32[]{:S(2)}) copy-start(f32[1,32,1024]{2,1,0:T(8,128)} %param.15) | copy-start | bytes 393220
  8.7 18.6 %copy-start.10 = (bf16[2,4,4,4096]{3,2,1,0:T(4,128)(2,1)S(1)}, bf16[2,4,4,4096]{3,2,1,0:T(4,128)(2,1)}, u32[]{:S(2)}) copy-start(bf16[2,4,4,4096]{3,2,1,0:T(4,128)(2,1)} %param.21) | copy-start | bytes 786436
  8.7 21.5 %copy-start.5 = (s32[4,16]{1,0:T(4,128)S(1)}, s32[4,16]{1,0:T(4,128)}, u32[]{:S(2)}) copy-start(s32[4,16]{1,0:T(4,128)} %parent_ref.3) | copy-start | bytes 772
  8.7 21.5 %copy-start.7 = (s32[16]{0:T(128)S(1)}, s32[16]{0:T(128)}, u32[]{:S(2)}) copy-start(s32[16]{0:T(128)} %owner_ref.7) | copy-start | bytes 196
  8.7 31.5 %copy-start.2 = (f32[4096]{0:T(1024)S(1)}, f32[4096]{0:T(1024)}, u32[]{:S(2)}) copy-start(f32[4096]{0:T(1024)} %param.17) | copy-start | bytes 49156
  31.8 14.9 %collective-permute-start.2 = (bf16[8,6144]{1,0:T(8,128)(2,1)S(1)}, bf16[8,6144]{1,0:T(8,128)(2,1)S(1)}, u32[]{:S(2)}, u32[]{:S(2)}) collective-permute-start(bf16[8,6144]{1,0:T(8,128)(2,1)S(1)} %get-tuple-element.33), channel_id=1, source_target_pairs={{0,1},{1,0},{2,3},{3,2},{4,5},{5,4},{6,7},{7,6},{8,9},{9,8},{10,11... | collective-permute-start | bytes 294920 | tf_op jit(solution)/shard_map/ppermute | solution.py:520
  33.4 13.2 %collective-permute-start.3 = (bf16[8,6144]{1,0:T(8,128)(2,1)S(1)}, bf16[8,6144]{1,0:T(8,128)(2,1)S(1)}, u32[]{:S(2)}, u32[]{:S(2)}) collective-permute-start(bf16[8,6144]{1,0:T(8,128)(2,1)S(1)} %get-tuple-element.34), channel_id=1, source_target_pairs={{0,2},{1,3},{2,0},{3,1},{4,6},{5,7},{6,4},{7,5},{8,10},{9,11},{10,... | collective-permute-start | bytes 294920 | tf_op jit(solution)/shard_map/ppermute | solution.py:520
  36.0 10.6 %collective-permute-start.4 = (bf16[8,6144]{1,0:T(8,128)(2,1)S(1)}, bf16[8,6144]{1,0:T(8,128)(2,1)S(1)}, u32[]{:S(2)}, u32[]{:S(2)}) collective-permute-start(bf16[8,6144]{1,0:T(8,128)(2,1)S(1)} %get-tuple-element.35.refs_2_), channel_id=1, source_target_pairs={{0,3},{1,2},{2,1},{3,0},{4,7},{5,6},{6,5},{7,4},{8,11},{9,10},{10,... | collective-permute-start | bytes 294920 | tf_op jit(solution)/shard_map/ppermute | solution.py:520
  36.2 3.9 %collective-permute-start.5 = (f32[8,1024]{1,0:T(8,128)S(1)}, f32[8,1024]{1,0:T(8,128)S(1)}, u32[]{:S(2)}, u32[]{:S(2)}) collective-permute-start(f32[8,1024]{1,0:T(8,128)S(1)} %get-tuple-element.38.refs_0_), channel_id=1, source_target_pairs={{0,16},{16,0},{1,17},{17,1},{2,18},{18,2},{3,19},{19,3},{4,20},{20... | collective-permute-start | bytes 98312 | tf_op jit(solution)/shard_map/ppermute | solution.py:520
  40.1 3.4 %copy-start = (bf16[1024,4096]{1,0:T(8,128)(2,1)S(1)}, bf16[1024,4096]{1,0:T(8,128)(2,1)}, u32[]{:S(2)}) copy-start(bf16[1024,4096]{1,0:T(8,128)(2,1)} %get-tuple-element.37.mixed_ref) | copy-start | bytes 25165828
  43.5 8.5 %copy-start.1 = (bf16[1024,4096]{1,0:T(8,128)(2,1)S(1)}, bf16[1024,4096]{1,0:T(8,128)(2,1)}, u32[]{:S(2)}) copy-start(bf16[1024,4096]{1,0:T(8,128)(2,1)} %get-tuple-element.37.mixed_ref) | copy-start | bytes 25165828
  47.6 7.6 %collective-permute-start.6 = (bf16[8,4096]{1,0:T(8,128)(2,1)S(1)}, bf16[8,4096]{1,0:T(8,128)(2,1)S(1)}, u32[]{:S(2)}, u32[]{:S(2)}) collective-permute-start(bf16[8,4096]{1,0:T(8,128)(2,1)S(1)} %get-tuple-element.41), channel_id=1, source_target_pairs={{0,1},{1,0},{2,3},{3,2},{4,5},{5,4},{6,7},{7,6},{8,9},{9,8},{10,11... | collective-permute-start | bytes 196616 | tf_op jit(solution)/shard_map/ppermute | solution.py:520
  48.3 7.1 %collective-permute-start.7 = (bf16[8,4096]{1,0:T(8,128)(2,1)S(1)}, bf16[8,4096]{1,0:T(8,128)(2,1)S(1)}, u32[]{:S(2)}, u32[]{:S(2)}) collective-permute-start(bf16[8,4096]{1,0:T(8,128)(2,1)S(1)} %get-tuple-element.42), channel_id=1, source_target_pairs={{0,2},{1,3},{2,0},{3,1},{4,6},{5,7},{6,4},{7,5},{8,10},{9,11},{10,... | collective-permute-start | bytes 196616 | tf_op jit(solution)/shard_map/ppermute | solution.py:520
  51.8 9.3 %copy-start.9 = (bf16[4,2,4,4096]{3,2,1,0:T(4,128)(2,1)S(1)}, bf16[4,2,4,4096]{3,2,1,0:T(4,128)(2,1)}, u32[]{:S(2)}) copy-start(bf16[4,2,4,4096]{3,2,1,0:T(4,128)(2,1)} %copy-done.8) | copy-start | bytes 786436
  51.8 9.4 %copy-start.4 = (f32[2,4,16,32]{3,2,1,0:T(8,128)S(1)}, f32[2,4,16,32]{3,2,1,0:T(8,128)}, u32[]{:S(2)}) copy-start(f32[2,4,16,32]{3,2,1,0:T(8,128)} %decay_ref.1) | copy-start | bytes 49156
  51.8 6.1 %collective-permute-start.8 = (bf16[8,4096]{1,0:T(8,128)(2,1)S(1)}, bf16[8,4096]{1,0:T(8,128)(2,1)S(1)}, u32[]{:S(2)}, u32[]{:S(2)}) collective-permute-start(bf16[8,4096]{1,0:T(8,128)(2,1)S(1)} %get-tuple-element.43.refs_2_), channel_id=1, source_target_pairs={{0,3},{1,2},{2,1},{3,0},{4,7},{5,6},{6,5},{7,4},{8,11},{9,10},{10,... | collective-permute-start | bytes 196616 | tf_op jit(solution)/shard_map/ppermute | solution.py:520
  57.9 1.3 %collective-permute-start.9 = (bf16[8,4096]{1,0:T(8,128)(2,1)S(1)}, bf16[8,4096]{1,0:T(8,128)(2,1)S(1)}, u32[]{:S(2)}, u32[]{:S(2)}) collective-permute-start(bf16[8,4096]{1,0:T(8,128)(2,1)S(1)} %get-tuple-element.46.refs_0_), channel_id=1, source_target_pairs={{0,4},{4,0},{8,12},{12,8},{1,5},{5,1},{9,13},{13,9},{2,6},{6,2},{1... | collective-permute-start | bytes 196616 | tf_op jit(solution)/shard_map/ppermute | solution.py:520
  57.9 1.4 %collective-permute-start.10 = (bf16[8,4096]{1,0:T(8,128)(2,1)S(1)}, bf16[8,4096]{1,0:T(8,128)(2,1)S(1)}, u32[]{:S(2)}, u32[]{:S(2)}) collective-permute-start(bf16[8,4096]{1,0:T(8,128)(2,1)S(1)} %collective-permute-done.6.refs_1_), channel_id=1, source_target_pairs={{0,4},{4,0},{8,12},{12,8},{1,5},{5,1},{9,13},{13,9},{2,6},{6,2},{1... | collective-permute-start | bytes 196616 | tf_op jit(solution)/shard_map/ppermute | solution.py:520
  58.4 1.3 %collective-permute-start.11 = (bf16[8,4096]{1,0:T(8,128)(2,1)S(1)}, bf16[8,4096]{1,0:T(8,128)(2,1)S(1)}, u32[]{:S(2)}, u32[]{:S(2)}) collective-permute-start(bf16[8,4096]{1,0:T(8,128)(2,1)S(1)} %collective-permute-done.7.refs_2_), channel_id=1, source_target_pairs={{0,4},{4,0},{8,12},{12,8},{1,5},{5,1},{9,13},{13,9},{2,6},{6,2},{1... | collective-permute-start | bytes 196616 | tf_op jit(solution)/shard_map/ppermute | solution.py:520
  58.4 1.4 %collective-permute-start.12 = (bf16[8,4096]{1,0:T(8,128)(2,1)S(1)}, bf16[8,4096]{1,0:T(8,128)(2,1)S(1)}, u32[]{:S(2)}, u32[]{:S(2)}) collective-permute-start(bf16[8,4096]{1,0:T(8,128)(2,1)S(1)} %collective-permute-done.8.refs_3_), channel_id=1, source_target_pairs={{0,4},{4,0},{8,12},{12,8},{1,5},{5,1},{9,13},{13,9},{2,6},{6,2},{1... | collective-permute-start | bytes 196616 | tf_op jit(solution)/shard_map/ppermute | solution.py:520
  60.6 8.6 %collective-permute-start.13 = (bf16[4,8,4096]{2,1,0:T(8,128)(2,1)S(1)}, bf16[4,8,4096]{2,1,0:T(8,128)(2,1)S(1)}, u32[]{:S(2)}, u32[]{:S(2)}) collective-permute-start(bf16[4,8,4096]{2,1,0:T(8,128)(2,1)S(1)} %reply.1.refs_3_), channel_id=1, source_target_pairs={{0,8},{4,12},{8,0},{12,4},{1,9},{5,13},{9,1},{13,5},{2,10},{6,14},... | collective-permute-start | bytes 786440 | tf_op jit(solution)/shard_map/ppermute | solution.py:520
  70.3 3.7 %collective-permute-start.14 = (f32[32,1]{1,0:T(8,128)S(1)}, f32[32,1]{1,0:T(8,128)S(1)}, u32[]{:S(2)}, u32[]{:S(2)}) collective-permute-start(f32[32,1]{1,0:T(8,128)S(1)} %bitcast.18), channel_id=1, source_target_pairs={{0,16},{16,0},{1,17},{17,1},{2,18},{18,2},{3,19},{19,3},{4,20},{20... | collective-permute-start | bytes 392 | tf_op jit(solution)/shard_map/ppermute | solution.py:520

commit v3 on v2

--- a/solution.py
+++ b/solution.py
@@ -166,7 +166,7 @@
         ).astype(bf16)
 
 
-def prompt_norm(lengths, gain, mixed, sums, base, rows, out, after):
+def prompt_norm(lengths, gain, mixed, sums, base, rows, out, after, room=50):
     tokens, columns = mixed.shape
     skip = base // SUB
     spare = pl.BlockSpec(memory_space=pl.ANY)
@@ -184,7 +184,7 @@
         out_specs=pl.BlockSpec((SUB, columns), lambda b: (b + skip, 0)),
         out_shape=jax.ShapeDtypeStruct((tokens, columns), bf16),
         input_output_aliases={} if out is None else {4 + len(sums): 0},
-        compiler_params=pltpu.CompilerParams(vmem_limit_bytes=12 * MIB),
+        compiler_params=pltpu.CompilerParams(vmem_limit_bytes=room * MIB),
         cost_estimate=pl.CostEstimate(
             flops=3 * rows * columns, bytes_accessed=4 * rows * columns, transcendentals=0
         ),
@@ -230,6 +230,10 @@
     )(*queries, state)
 
 
+def where_am_i():
+    return lax.axis_index("grp"), lax.axis_index("dec")
+
+
 def rank_of(owner_ref, prompt):
     owner = owner_ref[prompt]
     rank = jnp.int32(0)
@@ -258,58 +262,49 @@
             write(take())
 
 
-def ask_kernel(near, owner_ref, place_ref, *refs):
-    pool, out_ref = refs[:near], refs[near]
-    group, block = place_ref[0], place_ref[1]
-    count = out_ref.shape[0]
-    for bit in range(count):
-        owner, rank = rank_of(owner_ref, (group ^ near) * count + (block ^ bit))
-        offset = owner ^ group
-
-        def write(value, bit=bit):
-            out_ref[bit] = value
-
-        copy_one(offset, [lambda ref=ref, rank=rank: ref[rank] for ref in pool], write)
-
-
-def ask(owner, place, pool, count):
-    whole = pl.BlockSpec(memory_space=pltpu.VMEM)
-    scalar = pl.BlockSpec(memory_space=pltpu.SMEM)
-    return pl.pallas_call(
-        functools.partial(ask_kernel, len(pool)),
-        in_specs=[scalar, scalar] + [whole] * len(pool),
-        out_specs=whole,
-        out_shape=jax.ShapeDtypeStruct((count,) + pool[0].shape[1:], bf16),
-        compiler_params=pltpu.CompilerParams(vmem_limit_bytes=8 * MIB),
-        name="ask",
-    )(owner, place, *pool)
+def held_at(offset, near):
+    spot = jnp.int32(0)
+    low, high = 1, near
+    while high > 1:
+        spot = spot + jnp.where((offset & high) != 0, low, 0)
+        low, high = low * 2, high // 2
+    return spot
 
 
 def one_hot(mask):
     return mask.astype(f32).astype(bf16)
 
 
-def parcel_kernel(near, slots, capacity, owner_ref, place_ref, parent_ref, *refs):
-    pool, (came_ref, keys_ref, values_ref) = refs[:near], refs[near : near + 3]
-    outs = refs[near + 3 :]
-    group, block = place_ref[0], place_ref[1]
+def stack_rows(parts):
+    return jnp.concatenate([part.astype(f32) for part in parts], axis=0)
+
+
+def parcel_kernel(near, capacity, owner_ref, parent_ref, *refs):
+    pool, (keys_ref, values_ref) = refs[: 2 * near], refs[2 * near : 2 * near + 2]
+    outs = refs[2 * near + 2 :]
+    group, block = where_am_i()
     count = len(outs)
     rows, columns = outs[0].shape
-    per_block = rows // 2
+    steps, slots, per_block = keys_ref.shape[:3]
     halves = rows // (2 * capacity)
     split = columns // halves
-    lines = slots * rows
+    lines = slots * per_block
+    first_keys = stack_rows([keys_ref[0, slot] for slot in range(slots)]).astype(bf16)
+    first_values = stack_rows([values_ref[0, slot] for slot in range(slots)]).astype(bf16)
     for bit, out in enumerate(outs):
         owner, rank = rank_of(owner_ref, group * count + (block ^ bit))
-        choice = jnp.minimum(owner ^ group, near)
+        offset = owner ^ group
+        choice = held_at(offset, near) + jnp.where((offset & 1) != 0, near, 0)
 
         def write(value, out=out):
-            out[:, :columns] = value
+            out[:, :columns] = stack_rows(value).astype(bf16)
 
         copy_one(
             choice,
-            [lambda ref=ref, rank=rank: ref[rank] for ref in pool]
-            + [lambda bit=bit: came_ref[bit]],
+            [
+                lambda ref=ref, rank=rank: [ref[step, rank] for step in range(steps)]
+                for ref in pool
+            ],
             write,
         )
         if bit == 0:
@@ -321,7 +316,7 @@
             for beam in range(per_block):
                 parent = parent_ref[slot, target * per_block + beam]
                 hit = lax.div(parent, per_block) == block
-                row = slot * rows + parent - block * per_block
+                row = slot * per_block + parent - block * per_block
                 sources = [
                     jnp.where(hit & (seen == index), row, one)
                     for index, one in enumerate(sources)
@@ -332,40 +327,41 @@
         for half in range(halves):
             span = slice(half * split, (half + 1) * split)
             first = half * 2 * capacity
-            for kind, ref in enumerate((keys_ref, values_ref)):
+            for kind, held in enumerate((first_keys, first_values)):
                 mask = (line == first + kind * capacity) & (source == sources[0])
                 for index in range(1, capacity):
                     mask = mask | (
                         (line == first + kind * capacity + index) & (source == sources[index])
                     )
-                parcel = parcel + dot(one_hot(mask), ref[:, span])
+                parcel = parcel + dot(one_hot(mask), held[:, span])
         out[:, columns:] = parcel.astype(bf16)
 
 
-def parcels(owner, place, parents, pool, came, keys, values, capacity):
+def parcels(owner, parents, pool, keys, values, capacity, count):
     whole = pl.BlockSpec(memory_space=pltpu.VMEM)
     scalar = pl.BlockSpec(memory_space=pltpu.SMEM)
-    count, rows, columns = came.shape
+    steps, _, per_block, columns = keys.shape
+    rows = steps * per_block
     wide = columns + columns * 2 * capacity // rows
     return pl.pallas_call(
-        functools.partial(parcel_kernel, len(pool), parents.shape[0], capacity),
-        in_specs=[scalar] * 3 + [whole] * (len(pool) + 3),
+        functools.partial(parcel_kernel, len(pool) // 2, capacity),
+        in_specs=[scalar] * 2 + [whole] * (len(pool) + 2),
         out_specs=[whole] * count,
         out_shape=[
             jax.ShapeDtypeStruct((rows, wide if bit else columns), bf16) for bit in range(count)
         ],
         compiler_params=pltpu.CompilerParams(vmem_limit_bytes=12 * MIB),
         name="parcels",
-    )(owner, place, parents, *pool, came, keys, values)
-
-
-def reply_kernel(near, owner_ref, place_ref, *refs):
+    )(owner, parents, *pool, keys, values)
+
+
+def reply_kernel(near, owner_ref, *refs):
     pool, out_ref = refs[:-1], refs[-1]
-    group, block = place_ref[0], place_ref[1]
+    group, block = where_am_i()
     count = len(pool) // near
-    for slot, prompt in enumerate(prompts_of(owner_ref, group ^ near, out_ref.shape[0])):
+    for slot, prompt in enumerate(prompts_of(owner_ref, group ^ 1, out_ref.shape[0])):
         offset = lax.div(prompt, count) ^ group
-        choice = offset * count + (lax.rem(prompt, count) ^ block)
+        choice = held_at(offset, near) * count + (lax.rem(prompt, count) ^ block)
 
         def write(value, slot=slot):
             out_ref[slot] = value
@@ -373,27 +369,27 @@
         copy_one(choice, [lambda ref=ref: ref[...] for ref in pool], write)
 
 
-def reply(owner, place, pool, near, slots):
+def reply(owner, pool, near, slots):
     whole = pl.BlockSpec(memory_space=pltpu.VMEM)
     scalar = pl.BlockSpec(memory_space=pltpu.SMEM)
     return pl.pallas_call(
         functools.partial(reply_kernel, near),
-        in_specs=[scalar, scalar] + [whole] * len(pool),
+        in_specs=[scalar] + [whole] * len(pool),
         out_specs=whole,
         out_shape=jax.ShapeDtypeStruct((slots,) + pool[0].shape, bf16),
         compiler_params=pltpu.CompilerParams(vmem_limit_bytes=8 * MIB),
         name="reply",
-    )(owner, place, *pool)
-
-
-def terms_kernel(slots, capacity, count, place_ref, parent_ref, decay_ref, queries_ref, keys_ref, values_ref, *refs):
+    )(owner, *pool)
+
+
+def terms_kernel(capacity, count, parent_ref, decay_ref, queries_ref, keys_ref, values_ref, *refs):
     far = refs[:count]
     terms_ref, first_ref, second, parent_keys, parent_values = refs[count + 1 :]
-    block = place_ref[1]
-    lines, columns = queries_ref.shape
+    block = where_am_i()[1]
+    steps, slots, per_block, columns = queries_ref.shape
     heads = columns // HD
-    rows = lines // slots
-    per_block = rows // 2
+    rows = steps * per_block
+    lines = slots * rows
     halves = rows // (2 * capacity)
     split = columns // halves
     line = iota((lines, LANES), 0)
@@ -409,7 +405,7 @@
                 rank = rank + jnp.where(other == source, 1, 0)
             sources.append(source)
             away = source ^ block
-            near_at = slot * rows + parent - source * per_block
+            near_at = slot * per_block + parent - source * per_block
             near_at = jnp.where(away == 0, near_at, -1)
             far_at = jnp.where(away == 0, -1, (away - 1) * rows + rank)
             here = line == slot * rows + per_block + beam
@@ -425,14 +421,16 @@
             second[then : then + 1, :] = step_one
     first_ref[...] = jnp.exp(first_ref[...])
     second[...] = jnp.exp(second[...])
-    own_hot = one_hot(iota((lines, lines), 1) == near_col[:, :lines])
+    held = slots * per_block
+    own_hot = one_hot(iota((lines, held), 1) == near_col[:, :held])
     column = iota((lines, rows), 1)
     for half in range(halves):
         span = slice(half * split, (half + 1) * split)
         for kind, (ref, store) in enumerate(
             ((keys_ref, parent_keys), (values_ref, parent_values))
         ):
-            picked = dot(own_hot, ref[:, span])
+            own = stack_rows([ref[0, slot, :, span] for slot in range(slots)])
+            picked = dot(own_hot, own.astype(bf16))
             for index, message in enumerate(far):
                 low, high = half * 2 * capacity, kind * capacity
                 hot = (column == far_col[:, :rows] - index * rows + low + high) & (
@@ -443,22 +441,26 @@
             store[:, span] = picked
     for head in range(heads):
         span = slice(head * HD, (head + 1) * HD)
-        queries = queries_ref[:, span].astype(f32)
-        own = jnp.sum(queries * keys_ref[:, span].astype(f32), axis=1, keepdims=True)
+        queries, keys, values = [
+            stack_rows([ref[step, slot, :, span] for slot in range(slots) for step in range(steps)])
+            for ref in (queries_ref, keys_ref, values_ref)
+        ]
+        own = jnp.sum(queries * keys, axis=1, keepdims=True)
         parent = jnp.sum(queries * parent_keys[:, span], axis=1, keepdims=True)
-        terms_ref[:, span] = own * values_ref[:, span].astype(f32) + (
+        terms_ref[:, span] = own * values + (
             second[:, head : head + 1] * parent
         ) * parent_values[:, span]
 
 
-def step_terms(place, parents, decay, queries, keys, values, far, capacity, after):
-    lines, columns = queries.shape
+def step_terms(parents, decay, queries, keys, values, far, capacity, after):
+    steps, slots, per_block, columns = queries.shape
+    lines = steps * slots * per_block
     heads = columns // HD
     whole = pl.BlockSpec(memory_space=pltpu.VMEM)
     scalar = pl.BlockSpec(memory_space=pltpu.SMEM)
     return pl.pallas_call(
-        functools.partial(terms_kernel, parents.shape[0], capacity, len(far)),
-        in_specs=[scalar] * 2
+        functools.partial(terms_kernel, capacity, len(far)),
+        in_specs=[scalar]
         + [whole] * (4 + len(far))
         + [pl.BlockSpec(memory_space=pl.ANY)],
         out_shape=[
@@ -472,18 +474,19 @@
         ],
         compiler_params=pltpu.CompilerParams(vmem_limit_bytes=12 * MIB),
         name="step_terms",
-    )(place, parents, decay, queries, keys, values, *far, after)
-
-
-def steps_kernel(heads, near, owner_ref, place_ref, *refs):
+    )(parents, decay, queries, keys, values, *far, after)
+
+
+def steps_kernel(heads, near, owner_ref, *refs):
     pool = refs[:-5]
     came_ref, terms_ref, first_ref, mixed_ref, sums_ref = refs[-5:]
-    group, block = place_ref[0], place_ref[1]
+    group, block = where_am_i()
     count = len(pool) // near
     slots, rows = came_ref.shape[:2]
     for slot, prompt in enumerate(prompts_of(owner_ref, group, slots)):
         offset = lax.div(prompt, count) ^ group
-        choice = offset * count + (lax.rem(prompt, count) ^ block)
+        choice = held_at(offset, near) * count + (lax.rem(prompt, count) ^ block)
+        choice = jnp.where((offset & 1) != 0, len(pool), choice)
         lines = slice(slot * rows, (slot + 1) * rows)
         total = jnp.zeros((rows, HD), f32)
         for head in range(heads):
@@ -499,25 +502,58 @@
         )
 
 
-def steps_mix(owner, place, pool, near, came, terms, first):
+def steps_mix(owner, pool, near, came, terms, first):
     lines, columns = terms.shape
     whole = pl.BlockSpec(memory_space=pltpu.VMEM)
     scalar = pl.BlockSpec(memory_space=pltpu.SMEM)
     return pl.pallas_call(
         functools.partial(steps_kernel, columns // HD, near),
-        in_specs=[scalar, scalar] + [whole] * (len(pool) + 3),
+        in_specs=[scalar] + [whole] * (len(pool) + 3),
         out_shape=[
             jax.ShapeDtypeStruct((lines, columns), f32),
             jax.ShapeDtypeStruct((lines, LANES), f32),
         ],
         compiler_params=pltpu.CompilerParams(vmem_limit_bytes=12 * MIB),
         name="steps_mix",
-    )(owner, place, *pool, came, terms, first)
+    )(owner, *pool, came, terms, first)
+
+
+def finish_kernel(width, count, gain_ref, mixed_ref, *refs):
+    out_ref = refs[count]
+    steps, slots, per_block, columns = out_ref.shape
+    total = refs[0][...]
+    for ref in refs[1:count]:
+        total = total + ref[...]
+    scale = lax.rsqrt(total * (1.0 / width) + epsilon)
+    for column in range(0, columns, LANES):
+        span = slice(column, column + LANES)
+        scaled = (mixed_ref[:, span] * scale * gain_ref[:, span]).astype(bf16)
+        for slot in range(slots):
+            for step in range(steps):
+                line = (slot * steps + step) * per_block
+                out_ref[step, slot, :, span] = scaled[line : line + per_block]
+
+
+def finish(gain, mixed, sums, shape):
+    whole = pl.BlockSpec(memory_space=pltpu.VMEM)
+    return pl.pallas_call(
+        functools.partial(finish_kernel, HEAD_COUNT * HD, len(sums)),
+        in_specs=[whole] * (2 + len(sums)),
+        out_shape=jax.ShapeDtypeStruct(shape, bf16),
+        compiler_params=pltpu.CompilerParams(vmem_limit_bytes=8 * MIB),
+        name="finish",
+    )(gain, mixed, *sums)
 
 
 def swap(array, axis, bit):
     size = lax.axis_size(axis)
     return lax.ppermute(array, axis, [(index, index ^ bit) for index in range(size)])
+
+
+def exchange(parts):
+    order = sorted(range(1, len(parts)), key=lambda bit: (bit & 1, bit))
+    came = {bit: swap(parts[bit], "dec", bit) for bit in order}
+    return [came[bit] for bit in range(1, len(parts))]
 
 
 def over_pre(array):
@@ -540,67 +576,68 @@
     step_decay,
 ):
     tokens, columns = prompt_queries.shape[1:]
-    heads = prompt_decay.shape[1]
-    steps, slots, per_block = step_queries.shape[:3]
-    rows = steps * per_block
-    group, block = lax.axis_index("grp"), lax.axis_index("dec")
+    slots = step_queries.shape[1]
     group_count, block_count = lax.axis_size("grp"), lax.axis_size("dec")
     near = group_count // 2
-
-    def slot_major(array):
-        return jnp.swapaxes(array, 0, 1).reshape(slots, rows, columns)
+    capacity = (slots + block_count - 2) // (block_count - 1)
+    gain = norm_gain[None]
 
     def widen(pool):
-        bit = 1
-        while bit < near:
+        bit = near
+        while bit > 1:
             pool = pool + [swap(one, "grp", bit) for one in pool]
-            bit *= 2
+            bit //= 2
         return pool
 
-    place = jnp.stack([group, block]).astype(jnp.int32)
-    capacity = (slots + block_count - 2) // (block_count - 1)
-
-    queries = slot_major(step_queries)
-    asked = widen([queries])
-    sent = ask(decode_owner, place, asked, block_count)
-    came = swap(sent, "grp", near)
+    asked = widen([step_queries])
+    sibling = swap(step_queries, "grp", 1)
     mixed, sums, state = prompt_pass(
-        prompt_lengths, prompt_decay[0], prompt_queries[0], prompt_keys[0], prompt_values[0], sent
+        prompt_lengths, prompt_decay[0], prompt_queries[0], prompt_keys[0], prompt_values[0], sibling
     )
-    came, step_keys, step_values, sums = lax.optimization_barrier(
-        (came, step_keys, step_values, sums)
+    far_rows, sums = lax.optimization_barrier((asked[1:], sums))
+    asked = [step_queries] + far_rows + [sibling] + [swap(one, "grp", 1) for one in far_rows]
+
+    messages = parcels(
+        decode_owner, parent_beam, asked, step_keys, step_values, capacity, block_count
     )
-    queries = queries.reshape(slots * rows, columns)
-    keys = slot_major(step_keys).reshape(slots * rows, columns)
-    values = slot_major(step_values).reshape(slots * rows, columns)
-
-    messages = parcels(
-        decode_owner, place, parent_beam, asked, came, keys, values, capacity
-    )
-    far = [swap(messages[bit], "dec", bit) for bit in range(1, block_count)]
+    far = exchange(messages)
     squares = over_pre(sums)
-    share = tokens // 2
-    prompt_out = prompt_norm(
-        prompt_lengths, norm_gain[None], mixed, squares, 0, share, None, messages[-1]
-    )
+    share = tokens // 4
+
+    def norm(first, count, out, after, **more):
+        return prompt_norm(
+            prompt_lengths,
+            gain,
+            mixed,
+            squares,
+            first * share,
+            count * share,
+            out,
+            after,
+            **more,
+        )
+
+    prompt_out = norm(0, 1, None, messages[-1])
     state, prompt_out = lax.optimization_barrier((state, prompt_out))
     reads = read_states([messages[0]] + far, state)
-    prompt_out = prompt_norm(
-        prompt_lengths, norm_gain[None], mixed, squares, share, share, prompt_out, reads[-1]
+    prompt_out = norm(1, 2, prompt_out, reads[-1])
+    replies = exchange(reads)
+    early = widen([reads[0]])
+    replies, prompt_out = lax.optimization_barrier((replies, prompt_out))
+    prompt_out = norm(3, 1, prompt_out, replies[-1], room=12)
+    late = widen(replies)
+    spread = len(early)
+    pool = []
+    for index in range(spread):
+        pool = pool + [early[index]] + late[index * len(replies) : (index + 1) * len(replies)]
+    terms, first = step_terms(
+        parent_beam, step_decay, step_queries, step_keys, step_values, far, capacity, replies[-1]
     )
-    reads = [reads[0]] + [swap(reads[bit], "dec", bit) for bit in range(1, block_count)]
-    reads, prompt_out = lax.optimization_barrier((reads, prompt_out))
-    pool = widen(reads)
-    sent = reply(decode_owner, place, pool, near, slots)
-    came = swap(sent, "grp", near)
-    terms, first = step_terms(
-        place, parent_beam, step_decay, queries, keys, values, far, capacity, sent
-    )
-    step_mixed, step_sums = steps_mix(decode_owner, place, pool, near, came, terms, first)
-    step_total = functools.reduce(jnp.add, over_pre(step_sums[:, :1]))
-    scale = lax.rsqrt(step_total / (HEAD_COUNT * HD) + epsilon)
-    step_out = (step_mixed * scale * norm_gain).astype(bf16)
-    step_out = jnp.swapaxes(step_out.reshape(slots, steps, per_block, columns), 0, 1)
+    pool, terms, prompt_out = lax.optimization_barrier((pool, terms, prompt_out))
+    sent = reply(decode_owner, pool, near, slots)
+    came = swap(sent, "grp", 1)
+    step_mixed, step_sums = steps_mix(decode_owner, pool, near, came, terms, first)
+    step_out = finish(gain, step_mixed, over_pre(step_sums), step_queries.shape)
     return (prompt_out[None], step_out)
 
 

time: 75.5 us -> 67.6 us (0.90)
  local copies, waits for them, and re-layouts: 9.97 us -> 0.93 us
  waiting for transfers between devices: 12.9 us -> 8.55 us
  Pallas kernels: 33.6 us -> 37.3 us
  starting transfers between devices: 17 us -> 19.3 us
    pallas_call x2 -> x3, Pallas kernels: 6.24 us -> 10.7 us  [prompt_norm(): pl.pallas_call(functools.partial(norm_kernel, HEAD_COUNT * HD, len(sums),...]
    ppermute x15 -> x16, waiting for transfers between devices: 12.9 us -> 8.55 us  [swap(): lax.ppermute(array, axis, [(index, index ^ bit) for index in range(size)])]
    unnamed x22 -> x20, local copies, waits for them, and re-layouts: 4.97 us -> 0.93 us
    transpose x3 -> x0, local copies, waits for them, and re-layouts: 2.88 us -> none  [slot_major(): return jnp.swapaxes(array, 0, 1).reshape(slots, rows, columns)]
    ppermute x15 -> x16, starting transfers between devices: 17 us -> 19.3 us  [swap(): lax.ppermute(array, axis, [(index, index ^ bit) for index in range(size)])]
    another operation x3 -> x0, local copies, waits for them, and re-layouts: 1.14 us -> none  [the longest x1 1.01 us: local(): values = slot_major(step_values).reshape(slots * rows, columns)]
    pallas_call x1, Pallas kernels: 18.6 us -> 17.4 us  [prompt_pass(): pl.pallas_call(functools.partial(pass_kernel, heads, subs, each), grid=(s...]
    reshape x3 -> x0, local copies, waits for them, and re-layouts: 0.97 us -> none  [the longest x2 0.91 us: local(): step_out.reshape(slots, steps, per_block, columns)]
  transfers between devices with their start and end apart: 15 -> 16, of which waited for: 10 -> 5; matrix products, arithmetic and copies ran while one was open for 0% -> 0% of each run, Pallas kernels for 38% -> 47%
where the time goes in v3:
time: 67.6 us; the launch traced here: 67.5 us
  Pallas kernels  37.3 us (55%)
  starting transfers between devices  19.3 us (29%)
  waiting for transfers between devices  8.55 us (13%)
  between operations  1.44 us (2%)
  local copies, waits for them, and re-layouts  0.93 us (1%)
    ppermute x16, starting transfers between devices, swap(): lax.ppermute(array, axis, [(index, index ^ bit) for index in range(size)])  19.3 us
    pallas_call x1, Pallas kernels, prompt_pass(): pl.pallas_call(functools.partial(pass_kernel, heads, subs, each), grid=(s...  17.4 us
    pallas_call x3, Pallas kernels, prompt_norm(): pl.pallas_call(functools.partial(norm_kernel, HEAD_COUNT * HD, len(sums),...  10.7 us
    ppermute x16, waiting for transfers between devices, swap(): lax.ppermute(array, axis, [(index, index ^ bit) for index in range(size)])  8.55 us
    pallas_call x1, Pallas kernels, step_terms(): pl.pallas_call(functools.partial(terms_kernel, capacity, len(far)), in_sp...  3.95 us
    pallas_call x1, Pallas kernels, parcels(): pl.pallas_call(functools.partial(parcel_kernel, len(pool) // 2, capacity)...  1.64 us
  transfers between devices with their start and end apart: 16, of which 5 were waited for; matrix products, arithmetic and copies ran while one was open for 0% of the time, Pallas kernels for 47%

profile of v3, /device:TPU:0, one launch (start us, length us, event | category | flops | bytes accessed | tf_op | source)
XLA Modules:
  0.0 67.5 jit_solution(5217276310623507380)
XLA Ops:
  0.6 0.5 collective-permute-start.1
  1.2 2.6 %collective-permute-start = (bf16[2,4,4,4096]{3,2,1,0:T(4,128)(2,1)}, bf16[2,4,4,4096]{3,2,1,0:T(4,128)(2,1)S(1)}, u32[]{:S(2)}, u32[]{:S(2)}) collective-permute-start(bf16[2,4,4,4096]{3,2,1,0:T(4,128)(2,1)} %queries_ref.1), channel_id=1, source_target_pairs={{0,8},{4,12},{8,0},{12,4},{1,9},{5,13},{9,1},{13,5},{2,10},{6,14},... | collective-permute-start | bytes 786440 | tf_op jit(solution)/shard_map/ppermute | solution.py:550
  4.4 0.0 collective-permute-done.1.after_ref.refs_2_
  4.4 0.9 %copy-done.4 = f32[1,32,1024]{2,1,0:T(8,128)S(1)} copy-done((f32[1,32,1024]{2,1,0:T(8,128)S(1)}, f32[1,32,1024]{2,1,0:T(8,128)}, u32[]{:S(2)}) %copy-start.4) | copy-done | bytes 131096
  5.3 17.4 %prompt_pass.1 = (bf16[1024,4096]{1,0:T(8,128)(2,1)}, f32[8,1024]{1,0:T(8,128)S(1)}, f32[32,128,128]{2,1,0:T(8,128)S(1)}) custom-call(s32[1]{0:T(128)S(6)} %copy.18.length_ref, f32[32,1024]{1,0:T(8,128)S(1)} %bitcast.12, bf16[1024,4096]{1,0:T(8,128)(2,1)} %bitcast.14, bf16[1024,4096]{1,0:T(8,128)(2,1)} %bitcast.15, bf16[1024,4096]{1,0:T(8,128)(2,1)} %bitcast.16, ...), custom_call_target="tpu_custom_call" | custom-call | flops 4294967296 | bytes 33554432 | tf_op jit(solution)/shard_map/prompt_pass/pallas_call | solution.py:117
  22.8 0.2 collective-permute-start.2
  23.0 1.4 %collective-permute-done.2.refs_3_ = bf16[2,4,4,4096]{3,2,1,0:T(4,128)(2,1)S(1)} collective-permute-done((bf16[2,4,4,4096]{3,2,1,0:T(4,128)(2,1)S(1)}, bf16[2,4,4,4096]{3,2,1,0:T(4,128)(2,1)S(1)}, u32[]{:S(2)}, u32[]{:S(2)}) %collective-permute-start.2) | collective-permute-done | bytes 262176 | tf_op jit(solution)/shard_map/ppermute | solution.py:550
  24.4 1.6 %parcels.1 = (bf16[8,4096]{1,0:T(8,128)(2,1)S(1)}, bf16[8,6144]{1,0:T(8,128)(2,1)S(1)}, bf16[8,6144]{1,0:T(8,128)(2,1)S(1)}, bf16[8,6144]{1,0:T(8,128)(2,1)S(1)}) custom-call(s32[16]{0:T(128)S(1)} %copy-done.7, s32[4,16]{1,0:T(4,128)S(1)} %copy-done.6, bf16[2,4,4,4096]{3,2,1,0:T(4,128)(2,1)S(1)} %copy-done, ...), custom_call_target="tpu_custom_call" | custom-call | tf_op jit(solution)/shard_map/parcels/pallas_call | solution.py:346
  26.0 3.7 %collective-permute-start.5 = (bf16[8,6144]{1,0:T(8,128)(2,1)S(1)}, bf16[8,6144]{1,0:T(8,128)(2,1)S(1)}, u32[]{:S(2)}, u32[]{:S(2)}) collective-permute-start(bf16[8,6144]{1,0:T(8,128)(2,1)S(1)} %get-tuple-element.40.refs_2_), channel_id=1, source_target_pairs={{0,3},{1,2},{2,1},{3,0},{4,7},{5,6},{6,5},{7,4},{8,11},{9,10},{10,... | collective-permute-start | bytes 294920 | tf_op jit(solution)/shard_map/ppermute | solution.py:550
  29.7 0.8 %collective-permute-start.4 = (bf16[8,6144]{1,0:T(8,128)(2,1)S(1)}, bf16[8,6144]{1,0:T(8,128)(2,1)S(1)}, u32[]{:S(2)}, u32[]{:S(2)}) collective-permute-start(bf16[8,6144]{1,0:T(8,128)(2,1)S(1)} %get-tuple-element.39), channel_id=1, source_target_pairs={{0,2},{1,3},{2,0},{3,1},{4,6},{5,7},{6,4},{7,5},{8,10},{9,11},{10,... | collective-permute-start | bytes 294920 | tf_op jit(solution)/shard_map/ppermute | solution.py:550
  30.5 1.5 %collective-permute-start.6 = (f32[8,1024]{1,0:T(8,128)S(1)}, f32[8,1024]{1,0:T(8,128)S(1)}, u32[]{:S(2)}, u32[]{:S(2)}) collective-permute-start(f32[8,1024]{1,0:T(8,128)S(1)} %get-tuple-element.43.refs_0_), channel_id=1, source_target_pairs={{0,16},{16,0},{1,17},{17,1},{2,18},{18,2},{3,19},{19,3},{4,20},{20... | collective-permute-start | bytes 98312 | tf_op jit(solution)/shard_map/ppermute | solution.py:550
  32.0 2.4 %collective-permute-done.6.refs_1_ = f32[8,1024]{1,0:T(8,128)S(1)} collective-permute-done((f32[8,1024]{1,0:T(8,128)S(1)}, f32[8,1024]{1,0:T(8,128)S(1)}, u32[]{:S(2)}, u32[]{:S(2)}) %collective-permute-start.6) | collective-permute-done | bytes 32800 | tf_op jit(solution)/shard_map/ppermute | solution.py:550
  34.4 3.0 %prompt_norm.3.refs_3_ = bf16[1024,4096]{1,0:T(8,128)(2,1)} custom-call(s32[1]{0:T(128)S(6)} %copy.18.length_ref, f32[1,4096]{1,0:T(1,128)S(1)} %bitcast.8, bf16[1024,4096]{1,0:T(8,128)(2,1)} %get-tuple-element.42.mixed_ref, f32[8,1024]{1,0:T(8,128)S(1)} %get-tuple-element.43.refs_0_, f32[8,1024]{1,0:T(8,128)S(1)} %collective-permute-done.6.refs_1_, ...), custom_call_target="tpu_custom_call" | custom-call | flops 3145728 | bytes 4194304 | tf_op jit(solution)/shard_map/prompt_norm/pallas_call | solution.py:174
  37.4 0.9 %collective-permute-done.4.refs_2_.refs_1_ = bf16[8,6144]{1,0:T(8,128)(2,1)S(1)} collective-permute-done((bf16[8,6144]{1,0:T(8,128)(2,1)S(1)}, bf16[8,6144]{1,0:T(8,128)(2,1)S(1)}, u32[]{:S(2)}, u32[]{:S(2)}) %collective-permute-start.4) | collective-permute-done | bytes 98336 | tf_op jit(solution)/shard_map/ppermute | solution.py:550
  38.3 0.9 %read_states.1 = (bf16[8,4096]{1,0:T(8,128)(2,1)S(1)}, bf16[8,4096]{1,0:T(8,128)(2,1)S(1)}, bf16[8,4096]{1,0:T(8,128)(2,1)S(1)}, bf16[8,4096]{1,0:T(8,128)(2,1)S(1)}) custom-call(bf16[8,4096]{1,0:T(8,128)(2,1)S(1)} %get-tuple-element.37.refs_0_, bf16[8,6144]{1,0:T(8,128)(2,1)S(1)} %collective-permute-done.3.refs_1_.refs_0_, ...), custom_call_target="tpu_custom_call" | custom-call | flops 67108864 | bytes 2621440 | tf_op jit(solution)/shard_map/read_states/pallas_call | solution.py:217
  39.2 0.4 collective-permute-start.7
  39.6 2.9 %collective-permute-start.8 = (bf16[8,4096]{1,0:T(8,128)(2,1)S(1)}, bf16[8,4096]{1,0:T(8,128)(2,1)S(1)}, u32[]{:S(2)}, u32[]{:S(2)}) collective-permute-start(bf16[8,4096]{1,0:T(8,128)(2,1)S(1)} %get-tuple-element.47), channel_id=1, source_target_pairs={{0,2},{1,3},{2,0},{3,1},{4,6},{5,7},{6,4},{7,5},{8,10},{9,11},{10,... | collective-permute-start | bytes 196616 | tf_op jit(solution)/shard_map/ppermute | solution.py:550
  42.5 1.1 %collective-permute-start.9 = (bf16[8,4096]{1,0:T(8,128)(2,1)S(1)}, bf16[8,4096]{1,0:T(8,128)(2,1)S(1)}, u32[]{:S(2)}, u32[]{:S(2)}) collective-permute-start(bf16[8,4096]{1,0:T(8,128)(2,1)S(1)} %get-tuple-element.48.refs_2_), channel_id=1, source_target_pairs={{0,3},{1,2},{2,1},{3,0},{4,7},{5,6},{6,5},{7,4},{8,11},{9,10},{10,... | collective-permute-start | bytes 196616 | tf_op jit(solution)/shard_map/ppermute | solution.py:550
  43.6 1.0 %collective-permute-start.10 = (bf16[8,4096]{1,0:T(8,128)(2,1)S(1)}, bf16[8,4096]{1,0:T(8,128)(2,1)S(1)}, u32[]{:S(2)}, u32[]{:S(2)}) collective-permute-start(bf16[8,4096]{1,0:T(8,128)(2,1)S(1)} %get-tuple-element.56.refs_0_), channel_id=1, source_target_pairs={{0,8},{4,12},{8,0},{12,4},{1,9},{5,13},{9,1},{13,5},{2,10},{6,14},... | collective-permute-start | bytes 196616 | tf_op jit(solution)/shard_map/ppermute | solution.py:550
  44.6 5.9 %prompt_norm.4.refs_3_ = bf16[1024,4096]{1,0:T(8,128)(2,1)} custom-call(s32[1]{0:T(128)S(6)} %copy.18.length_ref, f32[1,4096]{1,0:T(1,128)S(1)} %bitcast.9, bf16[1024,4096]{1,0:T(8,128)(2,1)} %get-tuple-element.42.mixed_ref, f32[8,1024]{1,0:T(8,128)S(1)} %get-tuple-element.43.refs_0_, ...), custom_call_target="tpu_custom_call", output_to_operand_aliasing={{}: (6, {})} | custom-call | flops 6291456 | bytes 8388608 | tf_op jit(solution)/shard_map/prompt_norm/pallas_call | solution.py:174
  50.5 1.1 %collective-permute-start.11 = (bf16[8,4096]{1,0:T(8,128)(2,1)S(1)}, bf16[8,4096]{1,0:T(8,128)(2,1)S(1)}, u32[]{:S(2)}, u32[]{:S(2)}) collective-permute-start(bf16[8,4096]{1,0:T(8,128)(2,1)S(1)} %collective-permute-done.7.refs_1_), channel_id=1, source_target_pairs={{0,8},{4,12},{8,0},{12,4},{1,9},{5,13},{9,1},{13,5},{2,10},{6,14},... | collective-permute-start | bytes 196616 | tf_op jit(solution)/shard_map/ppermute | solution.py:550
  51.6 1.0 %collective-permute-start.12 = (bf16[8,4096]{1,0:T(8,128)(2,1)S(1)}, bf16[8,4096]{1,0:T(8,128)(2,1)S(1)}, u32[]{:S(2)}, u32[]{:S(2)}) collective-permute-start(bf16[8,4096]{1,0:T(8,128)(2,1)S(1)} %collective-permute-done.8.refs_2_), channel_id=1, source_target_pairs={{0,8},{4,12},{8,0},{12,4},{1,9},{5,13},{9,1},{13,5},{2,10},{6,14},... | collective-permute-start | bytes 196616 | tf_op jit(solution)/shard_map/ppermute | solution.py:550
  52.6 1.1 %collective-permute-start.13 = (bf16[8,4096]{1,0:T(8,128)(2,1)S(1)}, bf16[8,4096]{1,0:T(8,128)(2,1)S(1)}, u32[]{:S(2)}, u32[]{:S(2)}) collective-permute-start(bf16[8,4096]{1,0:T(8,128)(2,1)S(1)} %collective-permute-done.9.refs_3_.refs_2_), channel_id=1, source_target_pairs={{0,8},{4,12},{8,0},{12,4},{1,9},{5,13},{9,1},{13,5},{2,10},{6,14},... | collective-permute-start | bytes 196616 | tf_op jit(solution)/shard_map/ppermute | solution.py:550
  53.6 3.9 %step_terms.1 = (f32[32,4096]{1,0:T(8,128)S(1)}, f32[32,32]{1,0:T(8,128)S(1)}) custom-call(s32[4,16]{1,0:T(4,128)S(1)} %copy-done.6, f32[2,4,16,32]{3,2,1,0:T(8,128)S(1)} %copy-done.5, bf16[2,4,4,4096]{3,2,1,0:T(4,128)(2,1)S(1)} %copy-done, bf16[2,4,4,4096]{3,2,1,0:T(4,128)(2,1)S(1)} %copy-done.1, bf16[2,4,4,4096]{3,2,1,0:T(4,128)(2,1)S(1)} %copy-done.2, ...), custom_call_target="tpu_custom_call" | custom-call | tf_op jit(solution)/shard_map/step_terms/pallas_call | solution.py:461
  57.6 1.8 %prompt_norm.5 = bf16[1024,4096]{1,0:T(8,128)(2,1)} custom-call(s32[1]{0:T(128)S(6)} %copy.18.length_ref, f32[1,4096]{1,0:T(1,128)S(1)} %bitcast.10, bf16[1024,4096]{1,0:T(8,128)(2,1)S(1)} %bitcast.7, f32[8,1024]{1,0:T(8,128)S(1)} %get-tuple-element.43.refs_0_, f32[8,1024]{1,0:T(8,128)S(1)} %collective-permute-done.6.refs_1_, ...), custom_call_target="tpu_custom_call", output_to_operand_aliasing={{}: (6, {})} | custom-call | flops 3145728 | bytes 4194304 | tf_op jit(solution)/shard_map/prompt_norm/pallas_call | solution.py:174
  59.4 0.8 %reply.1 = bf16[4,8,4096]{2,1,0:T(8,128)(2,1)S(1)} custom-call(s32[16]{0:T(128)S(1)} %copy-done.7, bf16[8,4096]{1,0:T(8,128)(2,1)S(1)} %get-tuple-element.56.refs_0_, bf16[8,4096]{1,0:T(8,128)(2,1)S(1)} %collective-permute-done.7.refs_1_, bf16[8,4096]{1,0:T(8,128)(2,1)S(1)} %collective-permute-done.8.refs_2_, ...), custom_call_target="tpu_custom_call" | custom-call | tf_op jit(solution)/shard_map/reply/pallas_call | solution.py:375
  60.2 0.1 collective-permute-start.14
  60.3 1.5 %collective-permute-done.14.refs_8_ = bf16[4,8,4096]{2,1,0:T(8,128)(2,1)S(1)} collective-permute-done((bf16[4,8,4096]{2,1,0:T(8,128)(2,1)S(1)}, bf16[4,8,4096]{2,1,0:T(8,128)(2,1)S(1)}, u32[]{:S(2)}, u32[]{:S(2)}) %collective-permute-start.14) | collective-permute-done | bytes 262176 | tf_op jit(solution)/shard_map/ppermute | solution.py:550
  61.8 1.1 %steps_mix.1 = (f32[32,4096]{1,0:T(8,128)S(1)}, f32[32,128]{1,0:T(8,128)S(1)}) custom-call(s32[16]{0:T(128)S(1)} %copy-done.7, bf16[8,4096]{1,0:T(8,128)(2,1)S(1)} %get-tuple-element.56.refs_0_, bf16[8,4096]{1,0:T(8,128)(2,1)S(1)} %collective-permute-done.7.refs_1_, bf16[8,4096]{1,0:T(8,128)(2,1)S(1)} %collective-permute-done.8.refs_2_, ...), custom_call_target="tpu_custom_call" | custom-call | tf_op jit(solution)/shard_map/steps_mix/pallas_call | solution.py:509
  62.9 1.4 %collective-permute-start.15 = (f32[32,128]{1,0:T(8,128)S(1)}, f32[32,128]{1,0:T(8,128)S(1)}, u32[]{:S(2)}, u32[]{:S(2)}) collective-permute-start(f32[32,128]{1,0:T(8,128)S(1)} %get-tuple-element.67.refs_0_), channel_id=1, source_target_pairs={{0,16},{16,0},{1,17},{17,1},{2,18},{18,2},{3,19},{19,3},{4,20},{20... | collective-permute-start | bytes 49160 | tf_op jit(solution)/shard_map/ppermute | solution.py:550
  64.4 2.3 %collective-permute-done.15.refs_1_ = f32[32,128]{1,0:T(8,128)S(1)} collective-permute-done((f32[32,128]{1,0:T(8,128)S(1)}, f32[32,128]{1,0:T(8,128)S(1)}, u32[]{:S(2)}, u32[]{:S(2)}) %collective-permute-start.15) | collective-permute-done | bytes 16416 | tf_op jit(solution)/shard_map/ppermute | solution.py:550
  66.7 0.8 %finish.1 = bf16[2,4,4,4096]{3,2,1,0:T(4,128)(2,1)} custom-call(f32[1,4096]{1,0:T(1,128)S(1)} %bitcast.11, f32[32,4096]{1,0:T(8,128)S(1)} %get-tuple-element.66.mixed_ref, f32[32,128]{1,0:T(8,128)S(1)} %get-tuple-element.67.refs_0_, f32[32,128]{1,0:T(8,128)S(1)} %collective-permute-done.15.refs_1_), custom_call_target="tpu_custom_call" | custom-call | tf_op jit(solution)/shard_map/finish/pallas_call | solution.py:539
  (31 shorter events, 0.1 us)
Async XLA Ops:
  0.6 3.8 %collective-permute-start.1 = (bf16[2,4,4,4096]{3,2,1,0:T(4,128)(2,1)}, bf16[2,4,4,4096]{3,2,1,0:T(4,128)(2,1)S(1)}, u32[]{:S(2)}, u32[]{:S(2)}) collective-permute-start(bf16[2,4,4,4096]{3,2,1,0:T(4,128)(2,1)} %queries_ref.1), channel_id=1, source_target_pairs={{0,4},{4,0},{8,12},{12,8},{1,5},{5,1},{9,13},{13,9},{2,6},{6,2},{1... | collective-permute-start | bytes 786440 | tf_op jit(solution)/shard_map/ppermute | solution.py:550
  1.2 21.6 %collective-permute-start = (bf16[2,4,4,4096]{3,2,1,0:T(4,128)(2,1)}, bf16[2,4,4,4096]{3,2,1,0:T(4,128)(2,1)S(1)}, u32[]{:S(2)}, u32[]{:S(2)}) collective-permute-start(bf16[2,4,4,4096]{3,2,1,0:T(4,128)(2,1)} %queries_ref.1), channel_id=1, source_target_pairs={{0,8},{4,12},{8,0},{12,4},{1,9},{5,13},{9,1},{13,5},{2,10},{6,14},... | collective-permute-start | bytes 786440 | tf_op jit(solution)/shard_map/ppermute | solution.py:550
  4.4 0.9 %copy-start.4 = (f32[1,32,1024]{2,1,0:T(8,128)S(1)}, f32[1,32,1024]{2,1,0:T(8,128)}, u32[]{:S(2)}) copy-start(f32[1,32,1024]{2,1,0:T(8,128)} %param.15) | copy-start | bytes 393220
  5.3 19.0 %copy-start = (bf16[2,4,4,4096]{3,2,1,0:T(4,128)(2,1)S(1)}, bf16[2,4,4,4096]{3,2,1,0:T(4,128)(2,1)}, u32[]{:S(2)}) copy-start(bf16[2,4,4,4096]{3,2,1,0:T(4,128)(2,1)} %queries_ref.1) | copy-start | bytes 786436
  5.3 19.0 %copy-start.1 = (bf16[2,4,4,4096]{3,2,1,0:T(4,128)(2,1)S(1)}, bf16[2,4,4,4096]{3,2,1,0:T(4,128)(2,1)}, u32[]{:S(2)}) copy-start(bf16[2,4,4,4096]{3,2,1,0:T(4,128)(2,1)} %keys_ref.1) | copy-start | bytes 786436
  5.3 19.0 %copy-start.2 = (bf16[2,4,4,4096]{3,2,1,0:T(4,128)(2,1)S(1)}, bf16[2,4,4,4096]{3,2,1,0:T(4,128)(2,1)}, u32[]{:S(2)}) copy-start(bf16[2,4,4,4096]{3,2,1,0:T(4,128)(2,1)} %values_ref.1) | copy-start | bytes 786436
  5.3 19.0 %copy-start.6 = (s32[4,16]{1,0:T(4,128)S(1)}, s32[4,16]{1,0:T(4,128)}, u32[]{:S(2)}) copy-start(s32[4,16]{1,0:T(4,128)} %parent_ref.3) | copy-start | bytes 772
  5.3 19.0 %copy-start.7 = (s32[16]{0:T(128)S(1)}, s32[16]{0:T(128)}, u32[]{:S(2)}) copy-start(s32[16]{0:T(128)} %owner_ref.5) | copy-start | bytes 196
  5.3 29.1 %copy-start.3 = (f32[4096]{0:T(1024)S(1)}, f32[4096]{0:T(1024)}, u32[]{:S(2)}) copy-start(f32[4096]{0:T(1024)} %param.17) | copy-start | bytes 49156
  22.8 1.5 %collective-permute-start.2 = (bf16[2,4,4,4096]{3,2,1,0:T(4,128)(2,1)S(1)}, bf16[2,4,4,4096]{3,2,1,0:T(4,128)(2,1)S(1)}, u32[]{:S(2)}, u32[]{:S(2)}) collective-permute-start(bf16[2,4,4,4096]{3,2,1,0:T(4,128)(2,1)S(1)} %collective-permute-done.refs_1_), channel_id=1, source_target_pairs={{0,4},{4,0},{8,12},{12,8},{1,5},{5,1},{9,13},{13,9},{2,6},{6,2},{1... | collective-permute-start | bytes 786440 | tf_op jit(solution)/shard_map/ppermute | solution.py:550
  26.0 11.4 %collective-permute-start.5 = (bf16[8,6144]{1,0:T(8,128)(2,1)S(1)}, bf16[8,6144]{1,0:T(8,128)(2,1)S(1)}, u32[]{:S(2)}, u32[]{:S(2)}) collective-permute-start(bf16[8,6144]{1,0:T(8,128)(2,1)S(1)} %get-tuple-element.40.refs_2_), channel_id=1, source_target_pairs={{0,3},{1,2},{2,1},{3,0},{4,7},{5,6},{6,5},{7,4},{8,11},{9,10},{10,... | collective-permute-start | bytes 294920 | tf_op jit(solution)/shard_map/ppermute | solution.py:550
  29.7 7.7 %collective-permute-start.3 = (bf16[8,6144]{1,0:T(8,128)(2,1)S(1)}, bf16[8,6144]{1,0:T(8,128)(2,1)S(1)}, u32[]{:S(2)}, u32[]{:S(2)}) collective-permute-start(bf16[8,6144]{1,0:T(8,128)(2,1)S(1)} %get-tuple-element.38), channel_id=1, source_target_pairs={{0,1},{1,0},{2,3},{3,2},{4,5},{5,4},{6,7},{7,6},{8,9},{9,8},{10,11... | collective-permute-start | bytes 294920 | tf_op jit(solution)/shard_map/ppermute | solution.py:550
  29.7 8.6 %collective-permute-start.4 = (bf16[8,6144]{1,0:T(8,128)(2,1)S(1)}, bf16[8,6144]{1,0:T(8,128)(2,1)S(1)}, u32[]{:S(2)}, u32[]{:S(2)}) collective-permute-start(bf16[8,6144]{1,0:T(8,128)(2,1)S(1)} %get-tuple-element.39), channel_id=1, source_target_pairs={{0,2},{1,3},{2,0},{3,1},{4,6},{5,7},{6,4},{7,5},{8,10},{9,11},{10,... | collective-permute-start | bytes 294920 | tf_op jit(solution)/shard_map/ppermute | solution.py:550
  30.5 3.9 %collective-permute-start.6 = (f32[8,1024]{1,0:T(8,128)S(1)}, f32[8,1024]{1,0:T(8,128)S(1)}, u32[]{:S(2)}, u32[]{:S(2)}) collective-permute-start(f32[8,1024]{1,0:T(8,128)S(1)} %get-tuple-element.43.refs_0_), channel_id=1, source_target_pairs={{0,16},{16,0},{1,17},{17,1},{2,18},{18,2},{3,19},{19,3},{4,20},{20... | collective-permute-start | bytes 98312 | tf_op jit(solution)/shard_map/ppermute | solution.py:550
  39.2 11.3 %collective-permute-start.7 = (bf16[8,4096]{1,0:T(8,128)(2,1)S(1)}, bf16[8,4096]{1,0:T(8,128)(2,1)S(1)}, u32[]{:S(2)}, u32[]{:S(2)}) collective-permute-start(bf16[8,4096]{1,0:T(8,128)(2,1)S(1)} %get-tuple-element.46), channel_id=1, source_target_pairs={{0,1},{1,0},{2,3},{3,2},{4,5},{5,4},{6,7},{7,6},{8,9},{9,8},{10,11... | collective-permute-start | bytes 196616 | tf_op jit(solution)/shard_map/ppermute | solution.py:550
  39.6 10.9 %collective-permute-start.8 = (bf16[8,4096]{1,0:T(8,128)(2,1)S(1)}, bf16[8,4096]{1,0:T(8,128)(2,1)S(1)}, u32[]{:S(2)}, u32[]{:S(2)}) collective-permute-start(bf16[8,4096]{1,0:T(8,128)(2,1)S(1)} %get-tuple-element.47), channel_id=1, source_target_pairs={{0,2},{1,3},{2,0},{3,1},{4,6},{5,7},{6,4},{7,5},{8,10},{9,11},{10,... | collective-permute-start | bytes 196616 | tf_op jit(solution)/shard_map/ppermute | solution.py:550
  42.5 8.0 %collective-permute-start.9 = (bf16[8,4096]{1,0:T(8,128)(2,1)S(1)}, bf16[8,4096]{1,0:T(8,128)(2,1)S(1)}, u32[]{:S(2)}, u32[]{:S(2)}) collective-permute-start(bf16[8,4096]{1,0:T(8,128)(2,1)S(1)} %get-tuple-element.48.refs_2_), channel_id=1, source_target_pairs={{0,3},{1,2},{2,1},{3,0},{4,7},{5,6},{6,5},{7,4},{8,11},{9,10},{10,... | collective-permute-start | bytes 196616 | tf_op jit(solution)/shard_map/ppermute | solution.py:550
  43.6 14.0 %slice-start = ((s8[8388608]{0:T(1024)(128)(4,1)}), s8[4194304]{0:T(1024)(128)(4,1)S(1)}, s32[]{:S(2)}) async-start(s8[8388608]{0:T(1024)(128)(4,1)} %bitcast.6), calls=%async_computation | async-start | bytes 8388608
  43.6 10.0 %copy-start.5 = (f32[2,4,16,32]{3,2,1,0:T(8,128)S(1)}, f32[2,4,16,32]{3,2,1,0:T(8,128)}, u32[]{:S(2)}) copy-start(f32[2,4,16,32]{3,2,1,0:T(8,128)} %decay_ref.1) | copy-start | bytes 49156
  43.6 14.0 %slice-start.1 = ((s8[8388608]{0:T(1024)(128)(4,1)}), s8[4194304]{0:T(1024)(128)(4,1)S(1)}, s32[]{:S(2)}) async-start(s8[8388608]{0:T(1024)(128)(4,1)} %bitcast.6), calls=%async_computation.1 | async-start | bytes 8388608
  43.6 15.8 %collective-permute-start.10 = (bf16[8,4096]{1,0:T(8,128)(2,1)S(1)}, bf16[8,4096]{1,0:T(8,128)(2,1)S(1)}, u32[]{:S(2)}, u32[]{:S(2)}) collective-permute-start(bf16[8,4096]{1,0:T(8,128)(2,1)S(1)} %get-tuple-element.56.refs_0_), channel_id=1, source_target_pairs={{0,8},{4,12},{8,0},{12,4},{1,9},{5,13},{9,1},{13,5},{2,10},{6,14},... | collective-permute-start | bytes 196616 | tf_op jit(solution)/shard_map/ppermute | solution.py:550
  50.5 8.9 %collective-permute-start.11 = (bf16[8,4096]{1,0:T(8,128)(2,1)S(1)}, bf16[8,4096]{1,0:T(8,128)(2,1)S(1)}, u32[]{:S(2)}, u32[]{:S(2)}) collective-permute-start(bf16[8,4096]{1,0:T(8,128)(2,1)S(1)} %collective-permute-done.7.refs_1_), channel_id=1, source_target_pairs={{0,8},{4,12},{8,0},{12,4},{1,9},{5,13},{9,1},{13,5},{2,10},{6,14},... | collective-permute-start | bytes 196616 | tf_op jit(solution)/shard_map/ppermute | solution.py:550
  51.6 7.8 %collective-permute-start.12 = (bf16[8,4096]{1,0:T(8,128)(2,1)S(1)}, bf16[8,4096]{1,0:T(8,128)(2,1)S(1)}, u32[]{:S(2)}, u32[]{:S(2)}) collective-permute-start(bf16[8,4096]{1,0:T(8,128)(2,1)S(1)} %collective-permute-done.8.refs_2_), channel_id=1, source_target_pairs={{0,8},{4,12},{8,0},{12,4},{1,9},{5,13},{9,1},{13,5},{2,10},{6,14},... | collective-permute-start | bytes 196616 | tf_op jit(solution)/shard_map/ppermute | solution.py:550
  52.6 6.8 %collective-permute-start.13 = (bf16[8,4096]{1,0:T(8,128)(2,1)S(1)}, bf16[8,4096]{1,0:T(8,128)(2,1)S(1)}, u32[]{:S(2)}, u32[]{:S(2)}) collective-permute-start(bf16[8,4096]{1,0:T(8,128)(2,1)S(1)} %collective-permute-done.9.refs_3_.refs_2_), channel_id=1, source_target_pairs={{0,8},{4,12},{8,0},{12,4},{1,9},{5,13},{9,1},{13,5},{2,10},{6,14},... | collective-permute-start | bytes 196616 | tf_op jit(solution)/shard_map/ppermute | solution.py:550
  60.2 1.6 %collective-permute-start.14 = (bf16[4,8,4096]{2,1,0:T(8,128)(2,1)S(1)}, bf16[4,8,4096]{2,1,0:T(8,128)(2,1)S(1)}, u32[]{:S(2)}, u32[]{:S(2)}) collective-permute-start(bf16[4,8,4096]{2,1,0:T(8,128)(2,1)S(1)} %reply.1), channel_id=1, source_target_pairs={{0,4},{4,0},{8,12},{12,8},{1,5},{5,1},{9,13},{13,9},{2,6},{6,2},{1... | collective-permute-start | bytes 786440 | tf_op jit(solution)/shard_map/ppermute | solution.py:550
  62.9 3.7 %collective-permute-start.15 = (f32[32,128]{1,0:T(8,128)S(1)}, f32[32,128]{1,0:T(8,128)S(1)}, u32[]{:S(2)}, u32[]{:S(2)}) collective-permute-start(f32[32,128]{1,0:T(8,128)S(1)} %get-tuple-element.67.refs_0_), channel_id=1, source_target_pairs={{0,16},{16,0},{1,17},{17,1},{2,18},{18,2},{3,19},{19,3},{4,20},{20... | collective-permute-start | bytes 49160 | tf_op jit(solution)/shard_map/ppermute | solution.py:550

commit v4 on v3

--- a/solution.py
+++ b/solution.py
@@ -141,7 +141,7 @@
             pltpu.VMEM((subs, heads, LANES), f32),
             pltpu.VMEM((tokens, HD), f32),
         ],
-        compiler_params=pltpu.CompilerParams(vmem_limit_bytes=48 * MIB),
+        compiler_params=pltpu.CompilerParams(vmem_limit_bytes=40 * MIB),
         cost_estimate=pl.CostEstimate(
             flops=8 * tokens * columns * HD, bytes_accessed=8 * tokens * columns, transcendentals=0
         ),
@@ -166,22 +166,22 @@
         ).astype(bf16)
 
 
-def prompt_norm(lengths, gain, mixed, sums, base, rows, out, after, room=50):
+def prompt_norm(lengths, gain, mixed, sums, base, rows, out, after, room=12, lines=SUB):
     tokens, columns = mixed.shape
-    skip = base // SUB
+    skip = base // lines
     spare = pl.BlockSpec(memory_space=pl.ANY)
     more = [after] if out is None else [after, out]
     return pl.pallas_call(
         functools.partial(norm_kernel, HEAD_COUNT * HD, len(sums), base),
-        grid=(rows // SUB,),
+        grid=(rows // lines,),
         in_specs=[
             pl.BlockSpec(memory_space=pltpu.SMEM),
             pl.BlockSpec((1, columns), lambda b: (0, 0)),
-            pl.BlockSpec((SUB, columns), lambda b: (b + skip, 0)),
+            pl.BlockSpec((lines, columns), lambda b: (b + skip, 0)),
         ]
-        + [pl.BlockSpec((8, SUB), lambda b: (0, b + skip))] * len(sums)
+        + [pl.BlockSpec((8, lines), lambda b: (0, b + skip))] * len(sums)
         + [spare] * len(more),
-        out_specs=pl.BlockSpec((SUB, columns), lambda b: (b + skip, 0)),
+        out_specs=pl.BlockSpec((lines, columns), lambda b: (b + skip, 0)),
         out_shape=jax.ShapeDtypeStruct((tokens, columns), bf16),
         input_output_aliases={} if out is None else {4 + len(sums): 0},
         compiler_params=pltpu.CompilerParams(vmem_limit_bytes=room * MIB),
@@ -380,6 +380,11 @@
         compiler_params=pltpu.CompilerParams(vmem_limit_bytes=8 * MIB),
         name="reply",
     )(owner, *pool)
+
+
+def lane_sum(array):
+    halves = jnp.concatenate(pieces(array, 2), axis=1)
+    return dot(halves, jnp.ones((2 * HD, HD), bf16))
 
 
 def terms_kernel(capacity, count, parent_ref, decay_ref, queries_ref, keys_ref, values_ref, *refs):
@@ -445,8 +450,8 @@
             stack_rows([ref[step, slot, :, span] for slot in range(slots) for step in range(steps)])
             for ref in (queries_ref, keys_ref, values_ref)
         ]
-        own = jnp.sum(queries * keys, axis=1, keepdims=True)
-        parent = jnp.sum(queries * parent_keys[:, span], axis=1, keepdims=True)
+        own = lane_sum(queries * keys)
+        parent = lane_sum(queries * parent_keys[:, span])
         terms_ref[:, span] = own * values + (
             second[:, head : head + 1] * parent
         ) * parent_values[:, span]
@@ -602,7 +607,7 @@
     )
     far = exchange(messages)
     squares = over_pre(sums)
-    share = tokens // 4
+    share = tokens // 8
 
     def norm(first, count, out, after, **more):
         return prompt_norm(
@@ -617,14 +622,13 @@
             **more,
         )
 
-    prompt_out = norm(0, 1, None, messages[-1])
+    prompt_out = norm(0, 2, None, messages[-1])
     state, prompt_out = lax.optimization_barrier((state, prompt_out))
     reads = read_states([messages[0]] + far, state)
-    prompt_out = norm(1, 2, prompt_out, reads[-1])
+    prompt_out = norm(2, 4, prompt_out, reads[-1], lines=2 * SUB)
     replies = exchange(reads)
     early = widen([reads[0]])
     replies, prompt_out = lax.optimization_barrier((replies, prompt_out))
-    prompt_out = norm(3, 1, prompt_out, replies[-1], room=12)
     late = widen(replies)
     spread = len(early)
     pool = []
@@ -637,7 +641,9 @@
     sent = reply(decode_owner, pool, near, slots)
     came = swap(sent, "grp", 1)
     step_mixed, step_sums = steps_mix(decode_owner, pool, near, came, terms, first)
-    step_out = finish(gain, step_mixed, over_pre(step_sums), step_queries.shape)
+    step_squares = over_pre(step_sums)
+    prompt_out = norm(6, 2, prompt_out, step_sums, room=12)
+    step_out = finish(gain, step_mixed, step_squares, step_queries.shape)
     return (prompt_out[None], step_out)
 
 

time: 67.6 us -> 60.8 us (0.90)
  Pallas kernels: 37.3 us -> 28.6 us
  waiting for transfers between devices: 8.55 us -> 10.4 us
    pallas_call x3, Pallas kernels: 10.7 us -> 6.17 us  [prompt_norm(): pl.pallas_call(functools.partial(norm_kernel, HEAD_COUNT * HD, len(sums),...]
    pallas_call x1, Pallas kernels: 17.4 us -> 15.2 us  [prompt_pass(): pl.pallas_call(functools.partial(pass_kernel, heads, subs, each), grid=(s...]
    pallas_call x1, Pallas kernels: 3.95 us -> 2.06 us  [step_terms(): pl.pallas_call(functools.partial(terms_kernel, capacity, len(far)), in_sp...]
    ppermute x16, waiting for transfers between devices: 8.55 us -> 10.4 us  [swap(): lax.ppermute(array, axis, [(index, index ^ bit) for index in range(size)])]
  transfers between devices with their start and end apart: 16 -> 16, of which waited for: 5 -> 9; matrix products, arithmetic and copies ran while one was open for 0% -> 0% of each run, Pallas kernels for 47% -> 39%
where the time goes in v4:
time: 60.8 us; the launch traced here: 60.7 us
  Pallas kernels  28.6 us (47%)
  starting transfers between devices  19.4 us (32%)
  waiting for transfers between devices  10.4 us (17%)
  between operations  1.42 us (2%)
  local copies, waits for them, and re-layouts  0.92 us (2%)
    ppermute x16, starting transfers between devices, swap(): lax.ppermute(array, axis, [(index, index ^ bit) for index in range(size)])  19.4 us
    pallas_call x1, Pallas kernels, prompt_pass(): pl.pallas_call(functools.partial(pass_kernel, heads, subs, each), grid=(s...  15.2 us
    ppermute x16, waiting for transfers between devices, swap(): lax.ppermute(array, axis, [(index, index ^ bit) for index in range(size)])  10.4 us
    pallas_call x3, Pallas kernels, prompt_norm(): pl.pallas_call(functools.partial(norm_kernel, HEAD_COUNT * HD, len(sums),...  6.17 us
    pallas_call x1, Pallas kernels, step_terms(): pl.pallas_call(functools.partial(terms_kernel, capacity, len(far)), in_sp...  2.06 us
    pallas_call x1, Pallas kernels, parcels(): pl.pallas_call(functools.partial(parcel_kernel, len(pool) // 2, capacity)...  1.64 us
  transfers between devices with their start and end apart: 16, of which 9 were waited for; matrix products, arithmetic and copies ran while one was open for 0% of the time, Pallas kernels for 39%

profile of v4, /device:TPU:0, one launch (start us, length us, event | category | flops | bytes accessed | tf_op | source)
XLA Modules:
  0.0 60.7 jit_solution(1909820327242903022)
XLA Ops:
  0.6 0.5 collective-permute-start
  1.2 2.6 %collective-permute-start.1 = (bf16[2,4,4,4096]{3,2,1,0:T(4,128)(2,1)}, bf16[2,4,4,4096]{3,2,1,0:T(4,128)(2,1)S(1)}, u32[]{:S(2)}, u32[]{:S(2)}) collective-permute-start(bf16[2,4,4,4096]{3,2,1,0:T(4,128)(2,1)} %queries_ref.1), channel_id=1, source_target_pairs={{0,8},{4,12},{8,0},{12,4},{1,9},{5,13},{9,1},{13,5},{2,10},{6,14},... | collective-permute-start | bytes 786440 | tf_op jit(solution)/shard_map/ppermute | solution.py:555
  4.4 0.9 %copy-done.4 = f32[1,32,1024]{2,1,0:T(8,128)S(1)} copy-done((f32[1,32,1024]{2,1,0:T(8,128)S(1)}, f32[1,32,1024]{2,1,0:T(8,128)}, u32[]{:S(2)}) %copy-start.4) | copy-done | bytes 131096
  5.3 15.2 %prompt_pass.1 = (bf16[1024,4096]{1,0:T(8,128)(2,1)S(1)}, f32[8,1024]{1,0:T(8,128)S(1)}, f32[32,128,128]{2,1,0:T(8,128)S(1)}) custom-call(s32[1]{0:T(128)S(6)} %copy.18.length_ref, f32[32,1024]{1,0:T(8,128)S(1)} %bitcast.10, bf16[1024,4096]{1,0:T(8,128)(2,1)} %bitcast.12, bf16[1024,4096]{1,0:T(8,128)(2,1)} %bitcast.13, bf16[1024,4096]{1,0:T(8,128)(2,1)} %bitcast.14, ...), custom_call_target="tpu_custom_call" | custom-call | flops 4294967296 | bytes 33554432 | tf_op jit(solution)/shard_map/prompt_pass/pallas_call | solution.py:117
  20.7 1.4 %collective-permute-done.3.refs_3_ = bf16[2,4,4,4096]{3,2,1,0:T(4,128)(2,1)S(1)} collective-permute-done((bf16[2,4,4,4096]{3,2,1,0:T(4,128)(2,1)S(1)}, bf16[2,4,4,4096]{3,2,1,0:T(4,128)(2,1)S(1)}, u32[]{:S(2)}, u32[]{:S(2)}) %collective-permute-start.3) | collective-permute-done | bytes 262176 | tf_op jit(solution)/shard_map/ppermute | solution.py:555
  22.1 1.6 %parcels.1 = (bf16[8,4096]{1,0:T(8,128)(2,1)S(1)}, bf16[8,6144]{1,0:T(8,128)(2,1)S(1)}, bf16[8,6144]{1,0:T(8,128)(2,1)S(1)}, bf16[8,6144]{1,0:T(8,128)(2,1)S(1)}) custom-call(s32[16]{0:T(128)S(1)} %copy-done.7, s32[4,16]{1,0:T(4,128)S(1)} %copy-done.6, bf16[2,4,4,4096]{3,2,1,0:T(4,128)(2,1)S(1)} %copy-done, ...), custom_call_target="tpu_custom_call" | custom-call | tf_op jit(solution)/shard_map/parcels/pallas_call | solution.py:346
  23.8 1.6 %collective-permute-start.4 = (bf16[8,6144]{1,0:T(8,128)(2,1)S(1)}, bf16[8,6144]{1,0:T(8,128)(2,1)S(1)}, u32[]{:S(2)}, u32[]{:S(2)}) collective-permute-start(bf16[8,6144]{1,0:T(8,128)(2,1)S(1)} %get-tuple-element.40), channel_id=1, source_target_pairs={{0,1},{1,0},{2,3},{3,2},{4,5},{5,4},{6,7},{7,6},{8,9},{9,8},{10,11... | collective-permute-start | bytes 294920 | tf_op jit(solution)/shard_map/ppermute | solution.py:555
  25.4 2.6 %collective-permute-start.5 = (bf16[8,6144]{1,0:T(8,128)(2,1)S(1)}, bf16[8,6144]{1,0:T(8,128)(2,1)S(1)}, u32[]{:S(2)}, u32[]{:S(2)}) collective-permute-start(bf16[8,6144]{1,0:T(8,128)(2,1)S(1)} %get-tuple-element.41), channel_id=1, source_target_pairs={{0,2},{1,3},{2,0},{3,1},{4,6},{5,7},{6,4},{7,5},{8,10},{9,11},{10,... | collective-permute-start | bytes 294920 | tf_op jit(solution)/shard_map/ppermute | solution.py:555
  28.2 1.5 %collective-permute-start.2 = (f32[8,1024]{1,0:T(8,128)S(1)}, f32[8,1024]{1,0:T(8,128)S(1)}, u32[]{:S(2)}, u32[]{:S(2)}) collective-permute-start(f32[8,1024]{1,0:T(8,128)S(1)} %get-tuple-element.37.refs_0_), channel_id=1, source_target_pairs={{0,16},{16,0},{1,17},{17,1},{2,18},{18,2},{3,19},{19,3},{4,20},{20... | collective-permute-start | bytes 98312 | tf_op jit(solution)/shard_map/ppermute | solution.py:555
  29.7 2.4 %collective-permute-done.2.refs_1_ = f32[8,1024]{1,0:T(8,128)S(1)} collective-permute-done((f32[8,1024]{1,0:T(8,128)S(1)}, f32[8,1024]{1,0:T(8,128)S(1)}, u32[]{:S(2)}, u32[]{:S(2)}) %collective-permute-start.2) | collective-permute-done | bytes 32800 | tf_op jit(solution)/shard_map/ppermute | solution.py:555
  32.2 1.8 %prompt_norm.3.refs_3_ = bf16[1024,4096]{1,0:T(8,128)(2,1)} custom-call(s32[1]{0:T(128)S(6)} %copy.18.length_ref, f32[1,4096]{1,0:T(1,128)S(1)} %bitcast.6, bf16[1024,4096]{1,0:T(8,128)(2,1)S(1)} %get-tuple-element.35.mixed_ref, f32[8,1024]{1,0:T(8,128)S(1)} %get-tuple-element.37.refs_0_, f32[8,1024]{1,0:T(8,128)S(1)} %collective-permute-done.2.refs_1_, ...), custom_call_target="tpu_custom_call" | custom-call | flops 3145728 | bytes 4194304 | tf_op jit(solution)/shard_map/prompt_norm/pallas_call | solution.py:174
  33.9 2.1 %collective-permute-done.5.refs_2_.refs_1_ = bf16[8,6144]{1,0:T(8,128)(2,1)S(1)} collective-permute-done((bf16[8,6144]{1,0:T(8,128)(2,1)S(1)}, bf16[8,6144]{1,0:T(8,128)(2,1)S(1)}, u32[]{:S(2)}, u32[]{:S(2)}) %collective-permute-start.5) | collective-permute-done | bytes 98336 | tf_op jit(solution)/shard_map/ppermute | solution.py:555
  36.1 0.9 %read_states.1 = (bf16[8,4096]{1,0:T(8,128)(2,1)S(1)}, bf16[8,4096]{1,0:T(8,128)(2,1)S(1)}, bf16[8,4096]{1,0:T(8,128)(2,1)S(1)}, bf16[8,4096]{1,0:T(8,128)(2,1)S(1)}) custom-call(bf16[8,4096]{1,0:T(8,128)(2,1)S(1)} %get-tuple-element.39.refs_0_, bf16[8,6144]{1,0:T(8,128)(2,1)S(1)} %collective-permute-done.4.refs_1_.refs_0_, ...), custom_call_target="tpu_custom_call" | custom-call | flops 67108864 | bytes 2621440 | tf_op jit(solution)/shard_map/read_states/pallas_call | solution.py:217
  36.9 1.8 %collective-permute-start.7 = (bf16[8,4096]{1,0:T(8,128)(2,1)S(1)}, bf16[8,4096]{1,0:T(8,128)(2,1)S(1)}, u32[]{:S(2)}, u32[]{:S(2)}) collective-permute-start(bf16[8,4096]{1,0:T(8,128)(2,1)S(1)} %get-tuple-element.46), channel_id=1, source_target_pairs={{0,1},{1,0},{2,3},{3,2},{4,5},{5,4},{6,7},{7,6},{8,9},{9,8},{10,11... | collective-permute-start | bytes 196616 | tf_op jit(solution)/shard_map/ppermute | solution.py:555
  38.8 1.4 %collective-permute-start.8 = (bf16[8,4096]{1,0:T(8,128)(2,1)S(1)}, bf16[8,4096]{1,0:T(8,128)(2,1)S(1)}, u32[]{:S(2)}, u32[]{:S(2)}) collective-permute-start(bf16[8,4096]{1,0:T(8,128)(2,1)S(1)} %get-tuple-element.47), channel_id=1, source_target_pairs={{0,2},{1,3},{2,0},{3,1},{4,6},{5,7},{6,4},{7,5},{8,10},{9,11},{10,... | collective-permute-start | bytes 196616 | tf_op jit(solution)/shard_map/ppermute | solution.py:555
  40.2 1.2 %collective-permute-start.9 = (bf16[8,4096]{1,0:T(8,128)(2,1)S(1)}, bf16[8,4096]{1,0:T(8,128)(2,1)S(1)}, u32[]{:S(2)}, u32[]{:S(2)}) collective-permute-start(bf16[8,4096]{1,0:T(8,128)(2,1)S(1)} %get-tuple-element.48.refs_2_), channel_id=1, source_target_pairs={{0,3},{1,2},{2,1},{3,0},{4,7},{5,6},{6,5},{7,4},{8,11},{9,10},{10,... | collective-permute-start | bytes 196616 | tf_op jit(solution)/shard_map/ppermute | solution.py:555
  41.4 1.1 %collective-permute-start.10 = (bf16[8,4096]{1,0:T(8,128)(2,1)S(1)}, bf16[8,4096]{1,0:T(8,128)(2,1)S(1)}, u32[]{:S(2)}, u32[]{:S(2)}) collective-permute-start(bf16[8,4096]{1,0:T(8,128)(2,1)S(1)} %get-tuple-element.55.refs_0_), channel_id=1, source_target_pairs={{0,8},{4,12},{8,0},{12,4},{1,9},{5,13},{9,1},{13,5},{2,10},{6,14},... | collective-permute-start | bytes 196616 | tf_op jit(solution)/shard_map/ppermute | solution.py:555
  42.4 2.7 %prompt_norm.4.refs_3_ = bf16[1024,4096]{1,0:T(8,128)(2,1)} custom-call(s32[1]{0:T(128)S(6)} %copy.18.length_ref, f32[1,4096]{1,0:T(1,128)S(1)} %bitcast.7, bf16[1024,4096]{1,0:T(8,128)(2,1)S(1)} %get-tuple-element.35.mixed_ref, f32[8,1024]{1,0:T(8,128)S(1)} %get-tuple-element.37.refs_0_, ...), custom_call_target="tpu_custom_call", output_to_operand_aliasing={{}: (6, {})} | custom-call | flops 6291456 | bytes 8388608 | tf_op jit(solution)/shard_map/prompt_norm/pallas_call | solution.py:174
  45.1 0.3 collective-permute-done.8.refs_2_
  45.4 1.0 %collective-permute-done.9.refs_3_ = bf16[8,4096]{1,0:T(8,128)(2,1)S(1)} collective-permute-done((bf16[8,4096]{1,0:T(8,128)(2,1)S(1)}, bf16[8,4096]{1,0:T(8,128)(2,1)S(1)}, u32[]{:S(2)}, u32[]{:S(2)}) %collective-permute-start.9) | collective-permute-done | bytes 65568 | tf_op jit(solution)/shard_map/ppermute | solution.py:555
  46.4 1.0 %collective-permute-start.11 = (bf16[8,4096]{1,0:T(8,128)(2,1)S(1)}, bf16[8,4096]{1,0:T(8,128)(2,1)S(1)}, u32[]{:S(2)}, u32[]{:S(2)}) collective-permute-start(bf16[8,4096]{1,0:T(8,128)(2,1)S(1)} %collective-permute-done.7.refs_1_), channel_id=1, source_target_pairs={{0,8},{4,12},{8,0},{12,4},{1,9},{5,13},{9,1},{13,5},{2,10},{6,14},... | collective-permute-start | bytes 196616 | tf_op jit(solution)/shard_map/ppermute | solution.py:555
  47.4 1.0 %collective-permute-start.12 = (bf16[8,4096]{1,0:T(8,128)(2,1)S(1)}, bf16[8,4096]{1,0:T(8,128)(2,1)S(1)}, u32[]{:S(2)}, u32[]{:S(2)}) collective-permute-start(bf16[8,4096]{1,0:T(8,128)(2,1)S(1)} %collective-permute-done.8.refs_2_), channel_id=1, source_target_pairs={{0,8},{4,12},{8,0},{12,4},{1,9},{5,13},{9,1},{13,5},{2,10},{6,14},... | collective-permute-start | bytes 196616 | tf_op jit(solution)/shard_map/ppermute | solution.py:555
  48.4 1.0 %collective-permute-start.13 = (bf16[8,4096]{1,0:T(8,128)(2,1)S(1)}, bf16[8,4096]{1,0:T(8,128)(2,1)S(1)}, u32[]{:S(2)}, u32[]{:S(2)}) collective-permute-start(bf16[8,4096]{1,0:T(8,128)(2,1)S(1)} %collective-permute-done.9.refs_3_), channel_id=1, source_target_pairs={{0,8},{4,12},{8,0},{12,4},{1,9},{5,13},{9,1},{13,5},{2,10},{6,14},... | collective-permute-start | bytes 196616 | tf_op jit(solution)/shard_map/ppermute | solution.py:555
  49.4 2.1 %step_terms.1 = (f32[32,4096]{1,0:T(8,128)S(1)}, f32[32,32]{1,0:T(8,128)S(1)}) custom-call(s32[4,16]{1,0:T(4,128)S(1)} %copy-done.6, f32[2,4,16,32]{3,2,1,0:T(8,128)S(1)} %copy-done.5, bf16[2,4,4,4096]{3,2,1,0:T(4,128)(2,1)S(1)} %copy-done, bf16[2,4,4,4096]{3,2,1,0:T(4,128)(2,1)S(1)} %copy-done.1, bf16[2,4,4,4096]{3,2,1,0:T(4,128)(2,1)S(1)} %copy-done.2, ...), custom_call_target="tpu_custom_call" | custom-call | tf_op jit(solution)/shard_map/step_terms/pallas_call | solution.py:466
  51.6 1.0 %collective-permute-done.13.refs_7_ = bf16[8,4096]{1,0:T(8,128)(2,1)S(1)} collective-permute-done((bf16[8,4096]{1,0:T(8,128)(2,1)S(1)}, bf16[8,4096]{1,0:T(8,128)(2,1)S(1)}, u32[]{:S(2)}, u32[]{:S(2)}) %collective-permute-start.13) | collective-permute-done | bytes 65568 | tf_op jit(solution)/shard_map/ppermute | solution.py:555
  52.6 0.8 %reply.1 = bf16[4,8,4096]{2,1,0:T(8,128)(2,1)S(1)} custom-call(s32[16]{0:T(128)S(1)} %copy-done.7, bf16[8,4096]{1,0:T(8,128)(2,1)S(1)} %get-tuple-element.55.refs_0_, bf16[8,4096]{1,0:T(8,128)(2,1)S(1)} %collective-permute-done.7.refs_1_, bf16[8,4096]{1,0:T(8,128)(2,1)S(1)} %collective-permute-done.8.refs_2_, ...), custom_call_target="tpu_custom_call" | custom-call | tf_op jit(solution)/shard_map/reply/pallas_call | solution.py:375
  53.5 1.5 %collective-permute-done.14.refs_8_ = bf16[4,8,4096]{2,1,0:T(8,128)(2,1)S(1)} collective-permute-done((bf16[4,8,4096]{2,1,0:T(8,128)(2,1)S(1)}, bf16[4,8,4096]{2,1,0:T(8,128)(2,1)S(1)}, u32[]{:S(2)}, u32[]{:S(2)}) %collective-permute-start.14) | collective-permute-done | bytes 262176 | tf_op jit(solution)/shard_map/ppermute | solution.py:555
  55.1 1.1 %steps_mix.1 = (f32[32,4096]{1,0:T(8,128)S(1)}, f32[32,128]{1,0:T(8,128)S(1)}) custom-call(s32[16]{0:T(128)S(1)} %copy-done.7, bf16[8,4096]{1,0:T(8,128)(2,1)S(1)} %get-tuple-element.55.refs_0_, bf16[8,4096]{1,0:T(8,128)(2,1)S(1)} %collective-permute-done.7.refs_1_, bf16[8,4096]{1,0:T(8,128)(2,1)S(1)} %collective-permute-done.8.refs_2_, ...), custom_call_target="tpu_custom_call" | custom-call | tf_op jit(solution)/shard_map/steps_mix/pallas_call | solution.py:514
  56.1 1.5 %collective-permute-start.15 = (f32[32,128]{1,0:T(8,128)S(1)}, f32[32,128]{1,0:T(8,128)S(1)}, u32[]{:S(2)}, u32[]{:S(2)}) collective-permute-start(f32[32,128]{1,0:T(8,128)S(1)} %get-tuple-element.65.refs_2_.refs_0_), channel_id=1, source_target_pairs={{0,16},{16,0},{1,17},{17,1},{2,18},{18,2},{3,19},{19,3},{4,20},{20... | collective-permute-start | bytes 49160 | tf_op jit(solution)/shard_map/ppermute | solution.py:555
  57.6 1.8 %prompt_norm.5 = bf16[1024,4096]{1,0:T(8,128)(2,1)} custom-call(s32[1]{0:T(128)S(6)} %copy.18.length_ref, f32[1,4096]{1,0:T(1,128)S(1)} %bitcast.8, bf16[1024,4096]{1,0:T(8,128)(2,1)S(1)} %get-tuple-element.35.mixed_ref, f32[8,1024]{1,0:T(8,128)S(1)} %get-tuple-element.37.refs_0_, ...), custom_call_target="tpu_custom_call", output_to_operand_aliasing={{}: (6, {})} | custom-call | flops 3145728 | bytes 4194304 | tf_op jit(solution)/shard_map/prompt_norm/pallas_call | solution.py:174
  59.4 0.5 collective-permute-done.15.refs_1_
  59.9 0.8 %finish.1 = bf16[2,4,4,4096]{3,2,1,0:T(4,128)(2,1)} custom-call(f32[1,4096]{1,0:T(1,128)S(1)} %bitcast.9, f32[32,4096]{1,0:T(8,128)S(1)} %get-tuple-element.67.mixed_ref, f32[32,128]{1,0:T(8,128)S(1)} %get-tuple-element.65.refs_2_.refs_0_, f32[32,128]{1,0:T(8,128)S(1)} %collective-permute-done.15.refs_1_), custom_call_target="tpu_custom_call" | custom-call | tf_op jit(solution)/shard_map/finish/pallas_call | solution.py:544
  (26 shorter events, 0.7 us)
Async XLA Ops:
  0.6 3.8 %collective-permute-start = (bf16[2,4,4,4096]{3,2,1,0:T(4,128)(2,1)}, bf16[2,4,4,4096]{3,2,1,0:T(4,128)(2,1)S(1)}, u32[]{:S(2)}, u32[]{:S(2)}) collective-permute-start(bf16[2,4,4,4096]{3,2,1,0:T(4,128)(2,1)} %queries_ref.1), channel_id=1, source_target_pairs={{0,4},{4,0},{8,12},{12,8},{1,5},{5,1},{9,13},{13,9},{2,6},{6,2},{1... | collective-permute-start | bytes 786440 | tf_op jit(solution)/shard_map/ppermute | solution.py:555
  1.2 19.4 %collective-permute-start.1 = (bf16[2,4,4,4096]{3,2,1,0:T(4,128)(2,1)}, bf16[2,4,4,4096]{3,2,1,0:T(4,128)(2,1)S(1)}, u32[]{:S(2)}, u32[]{:S(2)}) collective-permute-start(bf16[2,4,4,4096]{3,2,1,0:T(4,128)(2,1)} %queries_ref.1), channel_id=1, source_target_pairs={{0,8},{4,12},{8,0},{12,4},{1,9},{5,13},{9,1},{13,5},{2,10},{6,14},... | collective-permute-start | bytes 786440 | tf_op jit(solution)/shard_map/ppermute | solution.py:555
  4.4 0.9 %copy-start.4 = (f32[1,32,1024]{2,1,0:T(8,128)S(1)}, f32[1,32,1024]{2,1,0:T(8,128)}, u32[]{:S(2)}) copy-start(f32[1,32,1024]{2,1,0:T(8,128)} %param.15) | copy-start | bytes 393220
  5.3 16.8 %copy-start = (bf16[2,4,4,4096]{3,2,1,0:T(4,128)(2,1)S(1)}, bf16[2,4,4,4096]{3,2,1,0:T(4,128)(2,1)}, u32[]{:S(2)}) copy-start(bf16[2,4,4,4096]{3,2,1,0:T(4,128)(2,1)} %queries_ref.1) | copy-start | bytes 786436
  5.3 16.8 %copy-start.1 = (bf16[2,4,4,4096]{3,2,1,0:T(4,128)(2,1)S(1)}, bf16[2,4,4,4096]{3,2,1,0:T(4,128)(2,1)}, u32[]{:S(2)}) copy-start(bf16[2,4,4,4096]{3,2,1,0:T(4,128)(2,1)} %keys_ref.1) | copy-start | bytes 786436
  5.3 16.8 %copy-start.2 = (bf16[2,4,4,4096]{3,2,1,0:T(4,128)(2,1)S(1)}, bf16[2,4,4,4096]{3,2,1,0:T(4,128)(2,1)}, u32[]{:S(2)}) copy-start(bf16[2,4,4,4096]{3,2,1,0:T(4,128)(2,1)} %values_ref.1) | copy-start | bytes 786436
  5.3 16.8 %copy-start.6 = (s32[4,16]{1,0:T(4,128)S(1)}, s32[4,16]{1,0:T(4,128)}, u32[]{:S(2)}) copy-start(s32[4,16]{1,0:T(4,128)} %parent_ref.3) | copy-start | bytes 772
  5.3 16.8 %copy-start.7 = (s32[16]{0:T(128)S(1)}, s32[16]{0:T(128)}, u32[]{:S(2)}) copy-start(s32[16]{0:T(128)} %owner_ref.5) | copy-start | bytes 196
  5.3 26.8 %copy-start.3 = (f32[4096]{0:T(1024)S(1)}, f32[4096]{0:T(1024)}, u32[]{:S(2)}) copy-start(f32[4096]{0:T(1024)} %param.17) | copy-start | bytes 49156
  20.5 1.6 %collective-permute-start.3 = (bf16[2,4,4,4096]{3,2,1,0:T(4,128)(2,1)S(1)}, bf16[2,4,4,4096]{3,2,1,0:T(4,128)(2,1)S(1)}, u32[]{:S(2)}, u32[]{:S(2)}) collective-permute-start(bf16[2,4,4,4096]{3,2,1,0:T(4,128)(2,1)S(1)} %collective-permute-done.1.refs_1_), channel_id=1, source_target_pairs={{0,4},{4,0},{8,12},{12,8},{1,5},{5,1},{9,13},{13,9},{2,6},{6,2},{1... | collective-permute-start | bytes 786440 | tf_op jit(solution)/shard_map/ppermute | solution.py:555
  23.8 10.1 %collective-permute-start.4 = (bf16[8,6144]{1,0:T(8,128)(2,1)S(1)}, bf16[8,6144]{1,0:T(8,128)(2,1)S(1)}, u32[]{:S(2)}, u32[]{:S(2)}) collective-permute-start(bf16[8,6144]{1,0:T(8,128)(2,1)S(1)} %get-tuple-element.40), channel_id=1, source_target_pairs={{0,1},{1,0},{2,3},{3,2},{4,5},{5,4},{6,7},{7,6},{8,9},{9,8},{10,11... | collective-permute-start | bytes 294920 | tf_op jit(solution)/shard_map/ppermute | solution.py:555
  25.4 10.6 %collective-permute-start.5 = (bf16[8,6144]{1,0:T(8,128)(2,1)S(1)}, bf16[8,6144]{1,0:T(8,128)(2,1)S(1)}, u32[]{:S(2)}, u32[]{:S(2)}) collective-permute-start(bf16[8,6144]{1,0:T(8,128)(2,1)S(1)} %get-tuple-element.41), channel_id=1, source_target_pairs={{0,2},{1,3},{2,0},{3,1},{4,6},{5,7},{6,4},{7,5},{8,10},{9,11},{10,... | collective-permute-start | bytes 294920 | tf_op jit(solution)/shard_map/ppermute | solution.py:555
  28.0 8.0 %collective-permute-start.6 = (bf16[8,6144]{1,0:T(8,128)(2,1)S(1)}, bf16[8,6144]{1,0:T(8,128)(2,1)S(1)}, u32[]{:S(2)}, u32[]{:S(2)}) collective-permute-start(bf16[8,6144]{1,0:T(8,128)(2,1)S(1)} %get-tuple-element.42.refs_2_), channel_id=1, source_target_pairs={{0,3},{1,2},{2,1},{3,0},{4,7},{5,6},{6,5},{7,4},{8,11},{9,10},{10,... | collective-permute-start | bytes 294920 | tf_op jit(solution)/shard_map/ppermute | solution.py:555
  28.2 3.9 %collective-permute-start.2 = (f32[8,1024]{1,0:T(8,128)S(1)}, f32[8,1024]{1,0:T(8,128)S(1)}, u32[]{:S(2)}, u32[]{:S(2)}) collective-permute-start(f32[8,1024]{1,0:T(8,128)S(1)} %get-tuple-element.37.refs_0_), channel_id=1, source_target_pairs={{0,16},{16,0},{1,17},{17,1},{2,18},{18,2},{3,19},{19,3},{4,20},{20... | collective-permute-start | bytes 98312 | tf_op jit(solution)/shard_map/ppermute | solution.py:555
  36.9 8.2 %collective-permute-start.7 = (bf16[8,4096]{1,0:T(8,128)(2,1)S(1)}, bf16[8,4096]{1,0:T(8,128)(2,1)S(1)}, u32[]{:S(2)}, u32[]{:S(2)}) collective-permute-start(bf16[8,4096]{1,0:T(8,128)(2,1)S(1)} %get-tuple-element.46), channel_id=1, source_target_pairs={{0,1},{1,0},{2,3},{3,2},{4,5},{5,4},{6,7},{7,6},{8,9},{9,8},{10,11... | collective-permute-start | bytes 196616 | tf_op jit(solution)/shard_map/ppermute | solution.py:555
  38.8 6.6 %collective-permute-start.8 = (bf16[8,4096]{1,0:T(8,128)(2,1)S(1)}, bf16[8,4096]{1,0:T(8,128)(2,1)S(1)}, u32[]{:S(2)}, u32[]{:S(2)}) collective-permute-start(bf16[8,4096]{1,0:T(8,128)(2,1)S(1)} %get-tuple-element.47), channel_id=1, source_target_pairs={{0,2},{1,3},{2,0},{3,1},{4,6},{5,7},{6,4},{7,5},{8,10},{9,11},{10,... | collective-permute-start | bytes 196616 | tf_op jit(solution)/shard_map/ppermute | solution.py:555
  40.2 6.2 %collective-permute-start.9 = (bf16[8,4096]{1,0:T(8,128)(2,1)S(1)}, bf16[8,4096]{1,0:T(8,128)(2,1)S(1)}, u32[]{:S(2)}, u32[]{:S(2)}) collective-permute-start(bf16[8,4096]{1,0:T(8,128)(2,1)S(1)} %get-tuple-element.48.refs_2_), channel_id=1, source_target_pairs={{0,3},{1,2},{2,1},{3,0},{4,7},{5,6},{6,5},{7,4},{8,11},{9,10},{10,... | collective-permute-start | bytes 196616 | tf_op jit(solution)/shard_map/ppermute | solution.py:555
  41.4 8.0 %copy-start.5 = (f32[2,4,16,32]{3,2,1,0:T(8,128)S(1)}, f32[2,4,16,32]{3,2,1,0:T(8,128)}, u32[]{:S(2)}) copy-start(f32[2,4,16,32]{3,2,1,0:T(8,128)} %decay_ref.1) | copy-start | bytes 49156
  41.4 10.1 %collective-permute-start.10 = (bf16[8,4096]{1,0:T(8,128)(2,1)S(1)}, bf16[8,4096]{1,0:T(8,128)(2,1)S(1)}, u32[]{:S(2)}, u32[]{:S(2)}) collective-permute-start(bf16[8,4096]{1,0:T(8,128)(2,1)S(1)} %get-tuple-element.55.refs_0_), channel_id=1, source_target_pairs={{0,8},{4,12},{8,0},{12,4},{1,9},{5,13},{9,1},{13,5},{2,10},{6,14},... | collective-permute-start | bytes 196616 | tf_op jit(solution)/shard_map/ppermute | solution.py:555
  46.4 5.1 %collective-permute-start.11 = (bf16[8,4096]{1,0:T(8,128)(2,1)S(1)}, bf16[8,4096]{1,0:T(8,128)(2,1)S(1)}, u32[]{:S(2)}, u32[]{:S(2)}) collective-permute-start(bf16[8,4096]{1,0:T(8,128)(2,1)S(1)} %collective-permute-done.7.refs_1_), channel_id=1, source_target_pairs={{0,8},{4,12},{8,0},{12,4},{1,9},{5,13},{9,1},{13,5},{2,10},{6,14},... | collective-permute-start | bytes 196616 | tf_op jit(solution)/shard_map/ppermute | solution.py:555
  47.4 4.3 %collective-permute-start.12 = (bf16[8,4096]{1,0:T(8,128)(2,1)S(1)}, bf16[8,4096]{1,0:T(8,128)(2,1)S(1)}, u32[]{:S(2)}, u32[]{:S(2)}) collective-permute-start(bf16[8,4096]{1,0:T(8,128)(2,1)S(1)} %collective-permute-done.8.refs_2_), channel_id=1, source_target_pairs={{0,8},{4,12},{8,0},{12,4},{1,9},{5,13},{9,1},{13,5},{2,10},{6,14},... | collective-permute-start | bytes 196616 | tf_op jit(solution)/shard_map/ppermute | solution.py:555
  48.4 4.3 %collective-permute-start.13 = (bf16[8,4096]{1,0:T(8,128)(2,1)S(1)}, bf16[8,4096]{1,0:T(8,128)(2,1)S(1)}, u32[]{:S(2)}, u32[]{:S(2)}) collective-permute-start(bf16[8,4096]{1,0:T(8,128)(2,1)S(1)} %collective-permute-done.9.refs_3_), channel_id=1, source_target_pairs={{0,8},{4,12},{8,0},{12,4},{1,9},{5,13},{9,1},{13,5},{2,10},{6,14},... | collective-permute-start | bytes 196616 | tf_op jit(solution)/shard_map/ppermute | solution.py:555
  53.5 1.6 %collective-permute-start.14 = (bf16[4,8,4096]{2,1,0:T(8,128)(2,1)S(1)}, bf16[4,8,4096]{2,1,0:T(8,128)(2,1)S(1)}, u32[]{:S(2)}, u32[]{:S(2)}) collective-permute-start(bf16[4,8,4096]{2,1,0:T(8,128)(2,1)S(1)} %reply.1), channel_id=1, source_target_pairs={{0,4},{4,0},{8,12},{12,8},{1,5},{5,1},{9,13},{13,9},{2,6},{6,2},{1... | collective-permute-start | bytes 786440 | tf_op jit(solution)/shard_map/ppermute | solution.py:555
  56.1 3.7 %collective-permute-start.15 = (f32[32,128]{1,0:T(8,128)S(1)}, f32[32,128]{1,0:T(8,128)S(1)}, u32[]{:S(2)}, u32[]{:S(2)}) collective-permute-start(f32[32,128]{1,0:T(8,128)S(1)} %get-tuple-element.65.refs_2_.refs_0_), channel_id=1, source_target_pairs={{0,16},{16,0},{1,17},{17,1},{2,18},{18,2},{3,19},{19,3},{4,20},{20... | collective-permute-start | bytes 49160 | tf_op jit(solution)/shard_map/ppermute | solution.py:555

commit v5 on v4

--- a/solution.py
+++ b/solution.py
@@ -60,7 +60,7 @@
         rates, live = [], []
         for sub in range(subs):
             span = slice(sub * SUB, (sub + 1) * SUB)
-            alive = sub * SUB + iota((heads, SUB), 1) < length_ref[0]
+            alive = sub * SUB + iota((heads, SUB), 1) < length_ref[...]
             rates.append(jnp.where(alive, decay_ref[:, span] * LOG2E, 0.0))
             live.append(alive)
         rates = jnp.concatenate(pieces(jnp.concatenate(rates, axis=0), 3), axis=1)
@@ -118,7 +118,7 @@
         functools.partial(pass_kernel, heads, subs, each),
         grid=(subs // each,),
         in_specs=[
-            pl.BlockSpec(memory_space=pltpu.SMEM),
+            pl.BlockSpec((1, 1), lambda b: (0, 0)),
             pl.BlockSpec((heads, tokens), lambda b: (0, 0)),
             wide,
             wide,
@@ -146,7 +146,7 @@
             flops=8 * tokens * columns * HD, bytes_accessed=8 * tokens * columns, transcendentals=0
         ),
         name="prompt_pass",
-    )(lengths, decay, queries, keys, values, after)
+    )(lengths[None], decay, queries, keys, values, after)
 
 
 def norm_kernel(width, count, base, length_ref, gain_ref, mixed_ref, *refs):

time: 60.8 us -> 61.1 us (level)
  no operation moved by 1% of the time
where the time goes in v5:
time: 61.1 us; the launch traced here: 60.9 us
  Pallas kernels  28.9 us (47%)
  starting transfers between devices  19.4 us (32%)
  waiting for transfers between devices  10.4 us (17%)
  between operations  1.42 us (2%)
  local copies, waits for them, and re-layouts  0.92 us (2%)
    ppermute x16, starting transfers between devices, swap(): lax.ppermute(array, axis, [(index, index ^ bit) for index in range(size)])  19.4 us
    pallas_call x1, Pallas kernels, prompt_pass(): pl.pallas_call(functools.partial(pass_kernel, heads, subs, each), grid=(s...  15.4 us
    ppermute x16, waiting for transfers between devices, swap(): lax.ppermute(array, axis, [(index, index ^ bit) for index in range(size)])  10.4 us
    pallas_call x3, Pallas kernels, prompt_norm(): pl.pallas_call(functools.partial(norm_kernel, HEAD_COUNT * HD, len(sums),...  6.17 us
    pallas_call x1, Pallas kernels, step_terms(): pl.pallas_call(functools.partial(terms_kernel, capacity, len(far)), in_sp...  2.05 us
    pallas_call x1, Pallas kernels, parcels(): pl.pallas_call(functools.partial(parcel_kernel, len(pool) // 2, capacity)...  1.65 us
  transfers between devices with their start and end apart: 16, of which 9 were waited for; matrix products, arithmetic and copies ran while one was open for 0% of the time, Pallas kernels for 39%

profile of v5, /device:TPU:0, one launch (start us, length us, event | category | flops | bytes accessed | tf_op | source)
XLA Modules:
  0.0 60.9 jit_solution(12983006709306333933)
XLA Ops:
  0.6 0.5 collective-permute-start
  1.2 2.6 %collective-permute-start.1 = (bf16[2,4,4,4096]{3,2,1,0:T(4,128)(2,1)}, bf16[2,4,4,4096]{3,2,1,0:T(4,128)(2,1)S(1)}, u32[]{:S(2)}, u32[]{:S(2)}) collective-permute-start(bf16[2,4,4,4096]{3,2,1,0:T(4,128)(2,1)} %queries_ref.1), channel_id=1, source_target_pairs={{0,8},{4,12},{8,0},{12,4},{1,9},{5,13},{9,1},{13,5},{2,10},{6,14},... | collective-permute-start | bytes 786440 | tf_op jit(solution)/shard_map/ppermute | solution.py:555
  4.4 0.9 %copy-done.4 = f32[1,32,1024]{2,1,0:T(8,128)S(1)} copy-done((f32[1,32,1024]{2,1,0:T(8,128)S(1)}, f32[1,32,1024]{2,1,0:T(8,128)}, u32[]{:S(2)}) %copy-start.4) | copy-done | bytes 131096
  5.3 15.4 %prompt_pass.1 = (bf16[1024,4096]{1,0:T(8,128)(2,1)S(1)}, f32[8,1024]{1,0:T(8,128)S(1)}, f32[32,128,128]{2,1,0:T(8,128)S(1)}) custom-call(s32[1,1]{1,0:T(1,128)} %bitcast.7.length_ref, f32[32,1024]{1,0:T(8,128)S(1)} %bitcast.12, bf16[1024,4096]{1,0:T(8,128)(2,1)} %bitcast.14, bf16[1024,4096]{1,0:T(8,128)(2,1)} %bitcast.15, bf16[1024,4096]{1,0:T(8,128)(2,1)} %bitcast.16, ...), custom_call_target="tpu_custom_call" | custom-call | flops 4294967296 | bytes 33554432 | tf_op jit(solution)/shard_map/prompt_pass/pallas_call | solution.py:117
  21.0 1.4 %collective-permute-done.3.refs_3_ = bf16[2,4,4,4096]{3,2,1,0:T(4,128)(2,1)S(1)} collective-permute-done((bf16[2,4,4,4096]{3,2,1,0:T(4,128)(2,1)S(1)}, bf16[2,4,4,4096]{3,2,1,0:T(4,128)(2,1)S(1)}, u32[]{:S(2)}, u32[]{:S(2)}) %collective-permute-start.3) | collective-permute-done | bytes 262176 | tf_op jit(solution)/shard_map/ppermute | solution.py:555
  22.4 1.6 %parcels.1 = (bf16[8,4096]{1,0:T(8,128)(2,1)S(1)}, bf16[8,6144]{1,0:T(8,128)(2,1)S(1)}, bf16[8,6144]{1,0:T(8,128)(2,1)S(1)}, bf16[8,6144]{1,0:T(8,128)(2,1)S(1)}) custom-call(s32[16]{0:T(128)S(1)} %copy-done.7, s32[4,16]{1,0:T(4,128)S(1)} %copy-done.6, bf16[2,4,4,4096]{3,2,1,0:T(4,128)(2,1)S(1)} %copy-done, ...), custom_call_target="tpu_custom_call" | custom-call | tf_op jit(solution)/shard_map/parcels/pallas_call | solution.py:346
  24.0 1.6 %collective-permute-start.4 = (bf16[8,6144]{1,0:T(8,128)(2,1)S(1)}, bf16[8,6144]{1,0:T(8,128)(2,1)S(1)}, u32[]{:S(2)}, u32[]{:S(2)}) collective-permute-start(bf16[8,6144]{1,0:T(8,128)(2,1)S(1)} %get-tuple-element.40), channel_id=1, source_target_pairs={{0,1},{1,0},{2,3},{3,2},{4,5},{5,4},{6,7},{7,6},{8,9},{9,8},{10,11... | collective-permute-start | bytes 294920 | tf_op jit(solution)/shard_map/ppermute | solution.py:555
  25.7 2.6 %collective-permute-start.5 = (bf16[8,6144]{1,0:T(8,128)(2,1)S(1)}, bf16[8,6144]{1,0:T(8,128)(2,1)S(1)}, u32[]{:S(2)}, u32[]{:S(2)}) collective-permute-start(bf16[8,6144]{1,0:T(8,128)(2,1)S(1)} %get-tuple-element.41), channel_id=1, source_target_pairs={{0,2},{1,3},{2,0},{3,1},{4,6},{5,7},{6,4},{7,5},{8,10},{9,11},{10,... | collective-permute-start | bytes 294920 | tf_op jit(solution)/shard_map/ppermute | solution.py:555
  28.5 1.5 %collective-permute-start.2 = (f32[8,1024]{1,0:T(8,128)S(1)}, f32[8,1024]{1,0:T(8,128)S(1)}, u32[]{:S(2)}, u32[]{:S(2)}) collective-permute-start(f32[8,1024]{1,0:T(8,128)S(1)} %get-tuple-element.37.refs_0_), channel_id=1, source_target_pairs={{0,16},{16,0},{1,17},{17,1},{2,18},{18,2},{3,19},{19,3},{4,20},{20... | collective-permute-start | bytes 98312 | tf_op jit(solution)/shard_map/ppermute | solution.py:555
  30.0 2.4 %collective-permute-done.2.refs_1_ = f32[8,1024]{1,0:T(8,128)S(1)} collective-permute-done((f32[8,1024]{1,0:T(8,128)S(1)}, f32[8,1024]{1,0:T(8,128)S(1)}, u32[]{:S(2)}, u32[]{:S(2)}) %collective-permute-start.2) | collective-permute-done | bytes 32800 | tf_op jit(solution)/shard_map/ppermute | solution.py:555
  32.4 1.8 %prompt_norm.3.refs_3_ = bf16[1024,4096]{1,0:T(8,128)(2,1)} custom-call(s32[1]{0:T(128)} %copy.18.length_ref, f32[1,4096]{1,0:T(1,128)S(1)} %bitcast.8, bf16[1024,4096]{1,0:T(8,128)(2,1)S(1)} %get-tuple-element.35.mixed_ref, f32[8,1024]{1,0:T(8,128)S(1)} %get-tuple-element.37.refs_0_, f32[8,1024]{1,0:T(8,128)S(1)} %collective-permute-done.2.refs_1_, ...), custom_call_target="tpu_custom_call" | custom-call | flops 3145728 | bytes 4194304 | tf_op jit(solution)/shard_map/prompt_norm/pallas_call | solution.py:174
  34.2 2.1 %collective-permute-done.5.refs_2_.refs_1_ = bf16[8,6144]{1,0:T(8,128)(2,1)S(1)} collective-permute-done((bf16[8,6144]{1,0:T(8,128)(2,1)S(1)}, bf16[8,6144]{1,0:T(8,128)(2,1)S(1)}, u32[]{:S(2)}, u32[]{:S(2)}) %collective-permute-start.5) | collective-permute-done | bytes 98336 | tf_op jit(solution)/shard_map/ppermute | solution.py:555
  36.3 0.9 %read_states.1 = (bf16[8,4096]{1,0:T(8,128)(2,1)S(1)}, bf16[8,4096]{1,0:T(8,128)(2,1)S(1)}, bf16[8,4096]{1,0:T(8,128)(2,1)S(1)}, bf16[8,4096]{1,0:T(8,128)(2,1)S(1)}) custom-call(bf16[8,4096]{1,0:T(8,128)(2,1)S(1)} %get-tuple-element.39.refs_0_, bf16[8,6144]{1,0:T(8,128)(2,1)S(1)} %collective-permute-done.4.refs_1_.refs_0_, ...), custom_call_target="tpu_custom_call" | custom-call | flops 67108864 | bytes 2621440 | tf_op jit(solution)/shard_map/read_states/pallas_call | solution.py:217
  37.2 1.8 %collective-permute-start.7 = (bf16[8,4096]{1,0:T(8,128)(2,1)S(1)}, bf16[8,4096]{1,0:T(8,128)(2,1)S(1)}, u32[]{:S(2)}, u32[]{:S(2)}) collective-permute-start(bf16[8,4096]{1,0:T(8,128)(2,1)S(1)} %get-tuple-element.46), channel_id=1, source_target_pairs={{0,1},{1,0},{2,3},{3,2},{4,5},{5,4},{6,7},{7,6},{8,9},{9,8},{10,11... | collective-permute-start | bytes 196616 | tf_op jit(solution)/shard_map/ppermute | solution.py:555
  39.0 1.4 %collective-permute-start.8 = (bf16[8,4096]{1,0:T(8,128)(2,1)S(1)}, bf16[8,4096]{1,0:T(8,128)(2,1)S(1)}, u32[]{:S(2)}, u32[]{:S(2)}) collective-permute-start(bf16[8,4096]{1,0:T(8,128)(2,1)S(1)} %get-tuple-element.47), channel_id=1, source_target_pairs={{0,2},{1,3},{2,0},{3,1},{4,6},{5,7},{6,4},{7,5},{8,10},{9,11},{10,... | collective-permute-start | bytes 196616 | tf_op jit(solution)/shard_map/ppermute | solution.py:555
  40.4 1.2 %collective-permute-start.9 = (bf16[8,4096]{1,0:T(8,128)(2,1)S(1)}, bf16[8,4096]{1,0:T(8,128)(2,1)S(1)}, u32[]{:S(2)}, u32[]{:S(2)}) collective-permute-start(bf16[8,4096]{1,0:T(8,128)(2,1)S(1)} %get-tuple-element.48.refs_2_), channel_id=1, source_target_pairs={{0,3},{1,2},{2,1},{3,0},{4,7},{5,6},{6,5},{7,4},{8,11},{9,10},{10,... | collective-permute-start | bytes 196616 | tf_op jit(solution)/shard_map/ppermute | solution.py:555
  41.6 1.1 %collective-permute-start.10 = (bf16[8,4096]{1,0:T(8,128)(2,1)S(1)}, bf16[8,4096]{1,0:T(8,128)(2,1)S(1)}, u32[]{:S(2)}, u32[]{:S(2)}) collective-permute-start(bf16[8,4096]{1,0:T(8,128)(2,1)S(1)} %get-tuple-element.55.refs_0_), channel_id=1, source_target_pairs={{0,8},{4,12},{8,0},{12,4},{1,9},{5,13},{9,1},{13,5},{2,10},{6,14},... | collective-permute-start | bytes 196616 | tf_op jit(solution)/shard_map/ppermute | solution.py:555
  42.7 2.7 %prompt_norm.4.refs_3_ = bf16[1024,4096]{1,0:T(8,128)(2,1)} custom-call(s32[1]{0:T(128)} %copy.18.length_ref, f32[1,4096]{1,0:T(1,128)S(1)} %bitcast.9, bf16[1024,4096]{1,0:T(8,128)(2,1)S(1)} %get-tuple-element.35.mixed_ref, f32[8,1024]{1,0:T(8,128)S(1)} %get-tuple-element.37.refs_0_, ...), custom_call_target="tpu_custom_call", output_to_operand_aliasing={{}: (6, {})} | custom-call | flops 6291456 | bytes 8388608 | tf_op jit(solution)/shard_map/prompt_norm/pallas_call | solution.py:174
  45.4 0.3 collective-permute-done.8.refs_2_
  45.6 0.9 %collective-permute-done.9.refs_3_ = bf16[8,4096]{1,0:T(8,128)(2,1)S(1)} collective-permute-done((bf16[8,4096]{1,0:T(8,128)(2,1)S(1)}, bf16[8,4096]{1,0:T(8,128)(2,1)S(1)}, u32[]{:S(2)}, u32[]{:S(2)}) %collective-permute-start.9) | collective-permute-done | bytes 65568 | tf_op jit(solution)/shard_map/ppermute | solution.py:555
  46.6 1.0 %collective-permute-start.11 = (bf16[8,4096]{1,0:T(8,128)(2,1)S(1)}, bf16[8,4096]{1,0:T(8,128)(2,1)S(1)}, u32[]{:S(2)}, u32[]{:S(2)}) collective-permute-start(bf16[8,4096]{1,0:T(8,128)(2,1)S(1)} %collective-permute-done.7.refs_1_), channel_id=1, source_target_pairs={{0,8},{4,12},{8,0},{12,4},{1,9},{5,13},{9,1},{13,5},{2,10},{6,14},... | collective-permute-start | bytes 196616 | tf_op jit(solution)/shard_map/ppermute | solution.py:555
  47.6 1.0 %collective-permute-start.12 = (bf16[8,4096]{1,0:T(8,128)(2,1)S(1)}, bf16[8,4096]{1,0:T(8,128)(2,1)S(1)}, u32[]{:S(2)}, u32[]{:S(2)}) collective-permute-start(bf16[8,4096]{1,0:T(8,128)(2,1)S(1)} %collective-permute-done.8.refs_2_), channel_id=1, source_target_pairs={{0,8},{4,12},{8,0},{12,4},{1,9},{5,13},{9,1},{13,5},{2,10},{6,14},... | collective-permute-start | bytes 196616 | tf_op jit(solution)/shard_map/ppermute | solution.py:555
  48.6 1.0 %collective-permute-start.13 = (bf16[8,4096]{1,0:T(8,128)(2,1)S(1)}, bf16[8,4096]{1,0:T(8,128)(2,1)S(1)}, u32[]{:S(2)}, u32[]{:S(2)}) collective-permute-start(bf16[8,4096]{1,0:T(8,128)(2,1)S(1)} %collective-permute-done.9.refs_3_), channel_id=1, source_target_pairs={{0,8},{4,12},{8,0},{12,4},{1,9},{5,13},{9,1},{13,5},{2,10},{6,14},... | collective-permute-start | bytes 196616 | tf_op jit(solution)/shard_map/ppermute | solution.py:555
  49.6 2.1 %step_terms.1 = (f32[32,4096]{1,0:T(8,128)S(1)}, f32[32,32]{1,0:T(8,128)S(1)}) custom-call(s32[4,16]{1,0:T(4,128)S(1)} %copy-done.6, f32[2,4,16,32]{3,2,1,0:T(8,128)S(1)} %copy-done.5, bf16[2,4,4,4096]{3,2,1,0:T(4,128)(2,1)S(1)} %copy-done, bf16[2,4,4,4096]{3,2,1,0:T(4,128)(2,1)S(1)} %copy-done.1, bf16[2,4,4,4096]{3,2,1,0:T(4,128)(2,1)S(1)} %copy-done.2, ...), custom_call_target="tpu_custom_call" | custom-call | tf_op jit(solution)/shard_map/step_terms/pallas_call | solution.py:466
  51.9 1.0 %collective-permute-done.13.refs_7_ = bf16[8,4096]{1,0:T(8,128)(2,1)S(1)} collective-permute-done((bf16[8,4096]{1,0:T(8,128)(2,1)S(1)}, bf16[8,4096]{1,0:T(8,128)(2,1)S(1)}, u32[]{:S(2)}, u32[]{:S(2)}) %collective-permute-start.13) | collective-permute-done | bytes 65568 | tf_op jit(solution)/shard_map/ppermute | solution.py:555
  52.9 0.8 %reply.1 = bf16[4,8,4096]{2,1,0:T(8,128)(2,1)S(1)} custom-call(s32[16]{0:T(128)S(1)} %copy-done.7, bf16[8,4096]{1,0:T(8,128)(2,1)S(1)} %get-tuple-element.55.refs_0_, bf16[8,4096]{1,0:T(8,128)(2,1)S(1)} %collective-permute-done.7.refs_1_, bf16[8,4096]{1,0:T(8,128)(2,1)S(1)} %collective-permute-done.8.refs_2_, ...), custom_call_target="tpu_custom_call" | custom-call | tf_op jit(solution)/shard_map/reply/pallas_call | solution.py:375
  53.8 1.5 %collective-permute-done.14.refs_8_ = bf16[4,8,4096]{2,1,0:T(8,128)(2,1)S(1)} collective-permute-done((bf16[4,8,4096]{2,1,0:T(8,128)(2,1)S(1)}, bf16[4,8,4096]{2,1,0:T(8,128)(2,1)S(1)}, u32[]{:S(2)}, u32[]{:S(2)}) %collective-permute-start.14) | collective-permute-done | bytes 262176 | tf_op jit(solution)/shard_map/ppermute | solution.py:555
  55.3 1.1 %steps_mix.1 = (f32[32,4096]{1,0:T(8,128)S(1)}, f32[32,128]{1,0:T(8,128)S(1)}) custom-call(s32[16]{0:T(128)S(1)} %copy-done.7, bf16[8,4096]{1,0:T(8,128)(2,1)S(1)} %get-tuple-element.55.refs_0_, bf16[8,4096]{1,0:T(8,128)(2,1)S(1)} %collective-permute-done.7.refs_1_, bf16[8,4096]{1,0:T(8,128)(2,1)S(1)} %collective-permute-done.8.refs_2_, ...), custom_call_target="tpu_custom_call" | custom-call | tf_op jit(solution)/shard_map/steps_mix/pallas_call | solution.py:514
  56.4 1.5 %collective-permute-start.15 = (f32[32,128]{1,0:T(8,128)S(1)}, f32[32,128]{1,0:T(8,128)S(1)}, u32[]{:S(2)}, u32[]{:S(2)}) collective-permute-start(f32[32,128]{1,0:T(8,128)S(1)} %get-tuple-element.65.refs_2_.refs_0_), channel_id=1, source_target_pairs={{0,16},{16,0},{1,17},{17,1},{2,18},{18,2},{3,19},{19,3},{4,20},{20... | collective-permute-start | bytes 49160 | tf_op jit(solution)/shard_map/ppermute | solution.py:555
  57.9 1.8 %prompt_norm.5 = bf16[1024,4096]{1,0:T(8,128)(2,1)} custom-call(s32[1]{0:T(128)} %copy.18.length_ref, f32[1,4096]{1,0:T(1,128)S(1)} %bitcast.10, bf16[1024,4096]{1,0:T(8,128)(2,1)S(1)} %get-tuple-element.35.mixed_ref, f32[8,1024]{1,0:T(8,128)S(1)} %get-tuple-element.37.refs_0_, ...), custom_call_target="tpu_custom_call", output_to_operand_aliasing={{}: (6, {})} | custom-call | flops 3145728 | bytes 4194304 | tf_op jit(solution)/shard_map/prompt_norm/pallas_call | solution.py:174
  59.6 0.5 collective-permute-done.15.refs_1_
  60.1 0.8 %finish.1 = bf16[2,4,4,4096]{3,2,1,0:T(4,128)(2,1)} custom-call(f32[1,4096]{1,0:T(1,128)S(1)} %bitcast.11, f32[32,4096]{1,0:T(8,128)S(1)} %get-tuple-element.67.mixed_ref, f32[32,128]{1,0:T(8,128)S(1)} %get-tuple-element.65.refs_2_.refs_0_, f32[32,128]{1,0:T(8,128)S(1)} %collective-permute-done.15.refs_1_), custom_call_target="tpu_custom_call" | custom-call | tf_op jit(solution)/shard_map/finish/pallas_call | solution.py:544
  (26 shorter events, 0.7 us)
Async XLA Ops:
  0.6 3.8 %collective-permute-start = (bf16[2,4,4,4096]{3,2,1,0:T(4,128)(2,1)}, bf16[2,4,4,4096]{3,2,1,0:T(4,128)(2,1)S(1)}, u32[]{:S(2)}, u32[]{:S(2)}) collective-permute-start(bf16[2,4,4,4096]{3,2,1,0:T(4,128)(2,1)} %queries_ref.1), channel_id=1, source_target_pairs={{0,4},{4,0},{8,12},{12,8},{1,5},{5,1},{9,13},{13,9},{2,6},{6,2},{1... | collective-permute-start | bytes 786440 | tf_op jit(solution)/shard_map/ppermute | solution.py:555
  1.2 19.6 %collective-permute-start.1 = (bf16[2,4,4,4096]{3,2,1,0:T(4,128)(2,1)}, bf16[2,4,4,4096]{3,2,1,0:T(4,128)(2,1)S(1)}, u32[]{:S(2)}, u32[]{:S(2)}) collective-permute-start(bf16[2,4,4,4096]{3,2,1,0:T(4,128)(2,1)} %queries_ref.1), channel_id=1, source_target_pairs={{0,8},{4,12},{8,0},{12,4},{1,9},{5,13},{9,1},{13,5},{2,10},{6,14},... | collective-permute-start | bytes 786440 | tf_op jit(solution)/shard_map/ppermute | solution.py:555
  4.4 0.9 %copy-start.4 = (f32[1,32,1024]{2,1,0:T(8,128)S(1)}, f32[1,32,1024]{2,1,0:T(8,128)}, u32[]{:S(2)}) copy-start(f32[1,32,1024]{2,1,0:T(8,128)} %param.15) | copy-start | bytes 393220
  5.3 17.0 %copy-start = (bf16[2,4,4,4096]{3,2,1,0:T(4,128)(2,1)S(1)}, bf16[2,4,4,4096]{3,2,1,0:T(4,128)(2,1)}, u32[]{:S(2)}) copy-start(bf16[2,4,4,4096]{3,2,1,0:T(4,128)(2,1)} %queries_ref.1) | copy-start | bytes 786436
  5.3 17.0 %copy-start.1 = (bf16[2,4,4,4096]{3,2,1,0:T(4,128)(2,1)S(1)}, bf16[2,4,4,4096]{3,2,1,0:T(4,128)(2,1)}, u32[]{:S(2)}) copy-start(bf16[2,4,4,4096]{3,2,1,0:T(4,128)(2,1)} %keys_ref.1) | copy-start | bytes 786436
  5.3 17.0 %copy-start.2 = (bf16[2,4,4,4096]{3,2,1,0:T(4,128)(2,1)S(1)}, bf16[2,4,4,4096]{3,2,1,0:T(4,128)(2,1)}, u32[]{:S(2)}) copy-start(bf16[2,4,4,4096]{3,2,1,0:T(4,128)(2,1)} %values_ref.1) | copy-start | bytes 786436
  5.3 17.0 %copy-start.6 = (s32[4,16]{1,0:T(4,128)S(1)}, s32[4,16]{1,0:T(4,128)}, u32[]{:S(2)}) copy-start(s32[4,16]{1,0:T(4,128)} %parent_ref.3) | copy-start | bytes 772
  5.3 17.0 %copy-start.7 = (s32[16]{0:T(128)S(1)}, s32[16]{0:T(128)}, u32[]{:S(2)}) copy-start(s32[16]{0:T(128)} %owner_ref.5) | copy-start | bytes 196
  5.3 27.1 %copy-start.3 = (f32[4096]{0:T(1024)S(1)}, f32[4096]{0:T(1024)}, u32[]{:S(2)}) copy-start(f32[4096]{0:T(1024)} %param.17) | copy-start | bytes 49156
  20.8 1.6 %collective-permute-start.3 = (bf16[2,4,4,4096]{3,2,1,0:T(4,128)(2,1)S(1)}, bf16[2,4,4,4096]{3,2,1,0:T(4,128)(2,1)S(1)}, u32[]{:S(2)}, u32[]{:S(2)}) collective-permute-start(bf16[2,4,4,4096]{3,2,1,0:T(4,128)(2,1)S(1)} %collective-permute-done.1.refs_1_), channel_id=1, source_target_pairs={{0,4},{4,0},{8,12},{12,8},{1,5},{5,1},{9,13},{13,9},{2,6},{6,2},{1... | collective-permute-start | bytes 786440 | tf_op jit(solution)/shard_map/ppermute | solution.py:555
  24.0 10.1 %collective-permute-start.4 = (bf16[8,6144]{1,0:T(8,128)(2,1)S(1)}, bf16[8,6144]{1,0:T(8,128)(2,1)S(1)}, u32[]{:S(2)}, u32[]{:S(2)}) collective-permute-start(bf16[8,6144]{1,0:T(8,128)(2,1)S(1)} %get-tuple-element.40), channel_id=1, source_target_pairs={{0,1},{1,0},{2,3},{3,2},{4,5},{5,4},{6,7},{7,6},{8,9},{9,8},{10,11... | collective-permute-start | bytes 294920 | tf_op jit(solution)/shard_map/ppermute | solution.py:555
  25.7 10.6 %collective-permute-start.5 = (bf16[8,6144]{1,0:T(8,128)(2,1)S(1)}, bf16[8,6144]{1,0:T(8,128)(2,1)S(1)}, u32[]{:S(2)}, u32[]{:S(2)}) collective-permute-start(bf16[8,6144]{1,0:T(8,128)(2,1)S(1)} %get-tuple-element.41), channel_id=1, source_target_pairs={{0,2},{1,3},{2,0},{3,1},{4,6},{5,7},{6,4},{7,5},{8,10},{9,11},{10,... | collective-permute-start | bytes 294920 | tf_op jit(solution)/shard_map/ppermute | solution.py:555
  28.3 8.0 %collective-permute-start.6 = (bf16[8,6144]{1,0:T(8,128)(2,1)S(1)}, bf16[8,6144]{1,0:T(8,128)(2,1)S(1)}, u32[]{:S(2)}, u32[]{:S(2)}) collective-permute-start(bf16[8,6144]{1,0:T(8,128)(2,1)S(1)} %get-tuple-element.42.refs_2_), channel_id=1, source_target_pairs={{0,3},{1,2},{2,1},{3,0},{4,7},{5,6},{6,5},{7,4},{8,11},{9,10},{10,... | collective-permute-start | bytes 294920 | tf_op jit(solution)/shard_map/ppermute | solution.py:555
  28.5 3.9 %collective-permute-start.2 = (f32[8,1024]{1,0:T(8,128)S(1)}, f32[8,1024]{1,0:T(8,128)S(1)}, u32[]{:S(2)}, u32[]{:S(2)}) collective-permute-start(f32[8,1024]{1,0:T(8,128)S(1)} %get-tuple-element.37.refs_0_), channel_id=1, source_target_pairs={{0,16},{16,0},{1,17},{17,1},{2,18},{18,2},{3,19},{19,3},{4,20},{20... | collective-permute-start | bytes 98312 | tf_op jit(solution)/shard_map/ppermute | solution.py:555
  37.2 8.2 %collective-permute-start.7 = (bf16[8,4096]{1,0:T(8,128)(2,1)S(1)}, bf16[8,4096]{1,0:T(8,128)(2,1)S(1)}, u32[]{:S(2)}, u32[]{:S(2)}) collective-permute-start(bf16[8,4096]{1,0:T(8,128)(2,1)S(1)} %get-tuple-element.46), channel_id=1, source_target_pairs={{0,1},{1,0},{2,3},{3,2},{4,5},{5,4},{6,7},{7,6},{8,9},{9,8},{10,11... | collective-permute-start | bytes 196616 | tf_op jit(solution)/shard_map/ppermute | solution.py:555
  39.0 6.6 %collective-permute-start.8 = (bf16[8,4096]{1,0:T(8,128)(2,1)S(1)}, bf16[8,4096]{1,0:T(8,128)(2,1)S(1)}, u32[]{:S(2)}, u32[]{:S(2)}) collective-permute-start(bf16[8,4096]{1,0:T(8,128)(2,1)S(1)} %get-tuple-element.47), channel_id=1, source_target_pairs={{0,2},{1,3},{2,0},{3,1},{4,6},{5,7},{6,4},{7,5},{8,10},{9,11},{10,... | collective-permute-start | bytes 196616 | tf_op jit(solution)/shard_map/ppermute | solution.py:555
  40.4 6.2 %collective-permute-start.9 = (bf16[8,4096]{1,0:T(8,128)(2,1)S(1)}, bf16[8,4096]{1,0:T(8,128)(2,1)S(1)}, u32[]{:S(2)}, u32[]{:S(2)}) collective-permute-start(bf16[8,4096]{1,0:T(8,128)(2,1)S(1)} %get-tuple-element.48.refs_2_), channel_id=1, source_target_pairs={{0,3},{1,2},{2,1},{3,0},{4,7},{5,6},{6,5},{7,4},{8,11},{9,10},{10,... | collective-permute-start | bytes 196616 | tf_op jit(solution)/shard_map/ppermute | solution.py:555
  41.6 8.0 %copy-start.5 = (f32[2,4,16,32]{3,2,1,0:T(8,128)S(1)}, f32[2,4,16,32]{3,2,1,0:T(8,128)}, u32[]{:S(2)}) copy-start(f32[2,4,16,32]{3,2,1,0:T(8,128)} %decay_ref.1) | copy-start | bytes 49156
  41.6 10.0 %collective-permute-start.10 = (bf16[8,4096]{1,0:T(8,128)(2,1)S(1)}, bf16[8,4096]{1,0:T(8,128)(2,1)S(1)}, u32[]{:S(2)}, u32[]{:S(2)}) collective-permute-start(bf16[8,4096]{1,0:T(8,128)(2,1)S(1)} %get-tuple-element.55.refs_0_), channel_id=1, source_target_pairs={{0,8},{4,12},{8,0},{12,4},{1,9},{5,13},{9,1},{13,5},{2,10},{6,14},... | collective-permute-start | bytes 196616 | tf_op jit(solution)/shard_map/ppermute | solution.py:555
  46.6 5.1 %collective-permute-start.11 = (bf16[8,4096]{1,0:T(8,128)(2,1)S(1)}, bf16[8,4096]{1,0:T(8,128)(2,1)S(1)}, u32[]{:S(2)}, u32[]{:S(2)}) collective-permute-start(bf16[8,4096]{1,0:T(8,128)(2,1)S(1)} %collective-permute-done.7.refs_1_), channel_id=1, source_target_pairs={{0,8},{4,12},{8,0},{12,4},{1,9},{5,13},{9,1},{13,5},{2,10},{6,14},... | collective-permute-start | bytes 196616 | tf_op jit(solution)/shard_map/ppermute | solution.py:555
  47.6 4.3 %collective-permute-start.12 = (bf16[8,4096]{1,0:T(8,128)(2,1)S(1)}, bf16[8,4096]{1,0:T(8,128)(2,1)S(1)}, u32[]{:S(2)}, u32[]{:S(2)}) collective-permute-start(bf16[8,4096]{1,0:T(8,128)(2,1)S(1)} %collective-permute-done.8.refs_2_), channel_id=1, source_target_pairs={{0,8},{4,12},{8,0},{12,4},{1,9},{5,13},{9,1},{13,5},{2,10},{6,14},... | collective-permute-start | bytes 196616 | tf_op jit(solution)/shard_map/ppermute | solution.py:555
  48.6 4.3 %collective-permute-start.13 = (bf16[8,4096]{1,0:T(8,128)(2,1)S(1)}, bf16[8,4096]{1,0:T(8,128)(2,1)S(1)}, u32[]{:S(2)}, u32[]{:S(2)}) collective-permute-start(bf16[8,4096]{1,0:T(8,128)(2,1)S(1)} %collective-permute-done.9.refs_3_), channel_id=1, source_target_pairs={{0,8},{4,12},{8,0},{12,4},{1,9},{5,13},{9,1},{13,5},{2,10},{6,14},... | collective-permute-start | bytes 196616 | tf_op jit(solution)/shard_map/ppermute | solution.py:555
  53.7 1.6 %collective-permute-start.14 = (bf16[4,8,4096]{2,1,0:T(8,128)(2,1)S(1)}, bf16[4,8,4096]{2,1,0:T(8,128)(2,1)S(1)}, u32[]{:S(2)}, u32[]{:S(2)}) collective-permute-start(bf16[4,8,4096]{2,1,0:T(8,128)(2,1)S(1)} %reply.1), channel_id=1, source_target_pairs={{0,4},{4,0},{8,12},{12,8},{1,5},{5,1},{9,13},{13,9},{2,6},{6,2},{1... | collective-permute-start | bytes 786440 | tf_op jit(solution)/shard_map/ppermute | solution.py:555
  56.4 3.7 %collective-permute-start.15 = (f32[32,128]{1,0:T(8,128)S(1)}, f32[32,128]{1,0:T(8,128)S(1)}, u32[]{:S(2)}, u32[]{:S(2)}) collective-permute-start(f32[32,128]{1,0:T(8,128)S(1)} %get-tuple-element.65.refs_2_.refs_0_), channel_id=1, source_target_pairs={{0,16},{16,0},{1,17},{17,1},{2,18},{18,2},{3,19},{19,3},{4,20},{20... | collective-permute-start | bytes 49160 | tf_op jit(solution)/shard_map/ppermute | solution.py:555
